TPU v7x, 512 devices: a whole 4x8x8 slice. The times are simulated.
512 devices in a mesh: orient: 16 (over y_hi, z), slab: 32 (over x, y_lo, core).
Axes of the slice: x: 4, y: 8 (y_hi: 2, y_lo: 4; y = y_hi * 4 + y_lo), z: 8, core: 2. Of those that a mesh axis runs over, the one named last changes fastest.
Arguments:
- images: bfloat16 [1024, 65536], P('orient', 'slab'), may hold values from -8 to 8
- projections: bfloat16 [8, 768, 65536], P(None, 'orient', 'slab'), may hold values from -0.0234375 to 0.0234375
- noise_weight: float32 [65536], P('slab'), may hold values from 0.5 to 4
- prior_score: float32 [8, 768], P(None, 'orient'), may hold values from -4 to 4
- routing: int32 [32, 768, 16, 2], P('slab', 'orient'), may hold values from 0 to 63, as said below
- insert_kernel: bfloat16 [32, 64, 128, 128], P('slab', 'orient'), may hold values from -1.5 to 1.5
Outputs:
- volume: float32 [32, 64, 8, 128], P('slab', 'orient')
Inputs may be any that keep to these rules, and one draw needn't show every extreme that they name: routing[s, o, p, 0] names the slab owner that receives slice block s * 16 + p of orientation o, and routing[s, o, p, 1] a volume block of that owner's slab, below 64. Among the 768 entries with one s and one aligned block of 48 orientations, no owner is named more than 48 times, and for each aligned block of orientations there is one owner (the same for every s) that is named exactly 48 times for each s.
All inputs are finite; a program needn't handle non-finite values.
Results may differ from a plain program's by a relative error of at most 0.008.
Values may be sent and summed in bfloat16 or wider, within the bound.
No kernel may reach another device: no remote copies, remote signals or barrier semaphores. Data moves between devices by JAX's collectives and lax.ppermute only.
A program may use at most 64 MiB of HBM per device.

v0:
```python
import jax
import jax.numpy as jnp
from jax import lax
from jax.sharding import PartitionSpec as P

PIECE = 128


def joined(value, axis, join):
    pieces = jax.tree.map(lambda part: lax.all_gather(part, axis), value)
    head = jax.tree.map(lambda part: part[0], pieces)
    tail = jax.tree.map(lambda part: part[1:], pieces)
    subtotal, _ = lax.scan(lambda subtotal, slab: (join(subtotal, slab), None), head, tail)
    return subtotal


def combine_totals(earlier, later):
    ceiling = jnp.maximum(earlier[0], later[0])
    return (
        ceiling,
        earlier[1] * jnp.exp(earlier[0] - ceiling) + later[1] * jnp.exp(later[0] - ceiling),
    )


def normalize(scores):
    row_ceiling = jnp.max(scores, axis=1)
    summed = jnp.sum(jnp.exp(scores - row_ceiling[:, None]), axis=1)
    ceiling_all, summed_all = joined((row_ceiling, summed), "orient", combine_totals)
    log_total = ceiling_all + jnp.log(summed_all)
    return jnp.exp(scores - log_total[:, None]).astype(jnp.bfloat16)


def local(images, projections, noise_weight, prior_score, routing, insert_kernel):
    classes, orient_local, pixels_local = projections.shape
    columns = classes * orient_local
    image_rows = images.shape[0]
    orient_count = lax.axis_size("orient")
    slab_count = lax.axis_size("slab")
    all_images = image_rows * orient_count
    widened = projections.astype(jnp.float32)
    weighted = (
        (widened * noise_weight[None, None, :]).astype(jnp.bfloat16).reshape(columns, pixels_local)
    )
    penalty = (-0.5 * jnp.sum(widened * widened * noise_weight[None, None, :], axis=2)).reshape(
        columns
    )
    block_rows = lax.all_gather(images, "orient", axis=0, tiled=True)
    block_scores = (
        lax.dot_general(
            block_rows, weighted, (((1,), (1,)), ((), ())), preferred_element_type=jnp.float32
        )
        + penalty[None, :]
    )
    partial_scores = block_scores
    stored = block_rows
    partial_scores, stored = (partial_scores, stored)
    prior_row = prior_score.reshape(columns)
    scores = lax.psum(partial_scores, "slab") + prior_row[None, :]
    weights = normalize(scores)
    block_count = pixels_local // PIECE
    weight_cube = weights.reshape(all_images, classes, orient_local)
    stored_blocks = stored.reshape(all_images, block_count, PIECE)
    slices = jnp.einsum(
        "iko,ipc->opkc", weight_cube, stored_blocks, preferred_element_type=jnp.float32
    ).astype(jnp.bfloat16)
    piece_count = orient_local * block_count
    slices = slices.reshape(piece_count, classes * PIECE)
    target = routing[0, :, :, 0].reshape(piece_count)
    voxel_index = routing[0, :, :, 1].reshape(piece_count)
    capacity = 2 * piece_count // slab_count
    owner_onehot = (target[:, None] == jnp.arange(slab_count, dtype=jnp.int32)[None, :]).astype(
        jnp.int32
    )
    before = jnp.cumsum(owner_onehot, axis=0) - owner_onehot
    slot_rank = jnp.sum(before * owner_onehot, axis=1)
    slot_index = target * capacity + slot_rank
    placing = (
        jnp.arange(slab_count * capacity, dtype=jnp.int32)[:, None] == slot_index[None, :]
    ).astype(jnp.int32)
    outgoing = jnp.dot(
        placing.astype(jnp.bfloat16), slices, preferred_element_type=jnp.float32
    ).astype(jnp.bfloat16)
    voxel_blocks = insert_kernel.shape[1] * orient_count
    filled = jnp.sum(placing, axis=1)
    slot_voxel = jnp.sum(placing * voxel_index[None, :], axis=1) + (1 - filled) * voxel_blocks
    arriving, arriving_voxel = (
        lax.all_to_all(
            outgoing.reshape(slab_count, capacity, classes * PIECE),
            "slab",
            split_axis=0,
            concat_axis=0,
            tiled=True,
        ),
        lax.all_to_all(
            slot_voxel.reshape(slab_count, capacity),
            "slab",
            split_axis=0,
            concat_axis=0,
            tiled=True,
        ),
    )
    received = arriving.reshape(slab_count * capacity, classes * PIECE)
    gathering = (
        jnp.arange(voxel_blocks, dtype=jnp.int32)[:, None]
        == arriving_voxel.reshape(slab_count * capacity)[None, :]
    ).astype(jnp.bfloat16)
    accumulated = jnp.dot(gathering, received, preferred_element_type=jnp.float32)
    own_blocks = lax.psum_scatter(accumulated, "orient", scatter_dimension=0, tiled=True)
    rounded = own_blocks.astype(jnp.bfloat16).reshape(own_blocks.shape[0], classes, PIECE)
    volume = jnp.einsum(
        "vkc,vce->vke", rounded, insert_kernel[0], preferred_element_type=jnp.float32
    )
    return volume[None]


def solution(mesh):
    placed = (
        P("orient", "slab"),
        P(None, "orient", "slab"),
        P("slab"),
        P(None, "orient"),
        P("slab", "orient", None, None),
        P("slab", "orient", None, None),
    )
    return jax.shard_map(
        local,
        mesh=mesh,
        in_specs=placed,
        out_specs=P("slab", "orient", None, None),
        check_vma=False,
    )
```

profile of v0, /device:TPU:6, one launch (start us, length us, event | category | flops | bytes accessed | tf_op | source)
XLA Modules:
  0.0 723.8 jit_solution(9435200211898309589)
XLA Ops:
  6.5 0.7 all-gather.4.cloned.1.call-update
  7.3 2.0 fusion.2
  9.4 138.5 %all-gather.4.cloned.1.call-done = bf16[1024,2048]{1,0:T(8,128)(2,1)} async-done(((bf16[64,2048]{1,0:T(8,128)(2,1)}), bf16[1024,2048]{1,0:T(8,128)(2,1)}) %all-gather.4.cloned.1.call-update) | async-done | bytes 4194320 | tf_op jit(solution)/shard_map/all_gather | solution.py:47
  148.0 5.2 add_bitcast_fusion
  153.1 0.7 copy-done.2
  154.1 1.7 reduce-window.6
  156.4 1.4 convert_reduce_fusion
  157.8 0.7 add.57
  158.5 5.7 all-to-all-start
  164.3 6.4 copy.25
  170.7 248.4 %all-reduce.4.cloned.1.call-done = f32[1024,384]{0,1:T(8,128)} async-done(((f32[1024,384]{0,1:T(8,128)}), f32[1024,384]{0,1:T(8,128)}) %all-reduce.4.cloned.1.call-update) | async-done | bytes 1572880 | tf_op jit(solution)/shard_map/psum | solution.py:58
  419.2 1.7 add_reduce_fusion
  421.4 51.7 %all-gather.1 = f32[16384]{0:T(1024)S(1)} all-gather(f32[1024]{0:T(1024)S(1)} %exponential_reduce_fusion), channel_id=3, replica_groups=mesh['orient'=16,'slab'=32] {'orient'}, dimensions={0}, use_global_device_ids=true | all-gather | bytes 69632 | tf_op jit(solution)/shard_map/all_gather | solution.py:10
  473.1 45.5 %all-gather = f32[16384]{0:T(1024)S(1)} all-gather(f32[1024]{0:T(1024)S(1)} %add_reduce_fusion), channel_id=2, replica_groups=mesh['orient'=16,'slab'=32] {'orient'}, dimensions={0}, use_global_device_ids=true | all-gather | bytes 69632 | tf_op jit(solution)/shard_map/all_gather | solution.py:10
  518.6 0.8 while.12
  519.8 4.0 fusion.6
  523.8 1.0 copy.27
  524.8 3.9 convolution_convert_fusion
  528.7 20.4 %all-to-all-start.1 = ((bf16[32,48,1024]{2,1,0:T(8,128)(2,1)}), bf16[32,48,1024]{2,1,0:T(8,128)(2,1)S(1)}, u32[]{:S(2)}, u32[]{:S(2)}) async-start(bf16[32,48,1024]{2,1,0:T(8,128)(2,1)} %bitcast.76), calls=%async_computation.1 | async-start | bytes 6291456 | tf_op jit(solution)/shard_map/all_to_all | solution.py:87
  549.2 1.3 dynamic-slice
  551.6 0.7 reduce.5
  552.4 67.7 %all-to-all-done.1 = bf16[32,48,1024]{2,1,0:T(8,128)(2,1)S(1)} async-done(((bf16[32,48,1024]{2,1,0:T(8,128)(2,1)}), bf16[32,48,1024]{2,1,0:T(8,128)(2,1)S(1)}, u32[]{:S(2)}, u32[]{:S(2)}) %all-to-all-start.1) | async-done | bytes 3145760 | tf_op jit(solution)/shard_map/all_to_all | solution.py:87
  620.7 95.4 %all-reduce.5 = bf16[64,1024]{1,0:T(8,128)(2,1)S(1)} all-reduce(f32[64,1024]{1,0:T(8,128)S(1)} %fusion.7), channel_id=4, replica_groups=mesh['orient'=16,'slab'=32] {'orient'}, use_global_device_ids=true, to_apply=%region_11.12.clone | all-reduce | flops 65536 | bytes 393216
  716.2 0.8 convolution_bitcast_fusion
  (69 shorter events, 3.6 us)
Async XLA Ops:
  6.5 709.7 %copy-start = (bf16[1,4,128,128]{3,2,1,0:T(8,128)(2,1)S(1)}, bf16[1,4,128,128]{3,2,1,0:T(8,128)(2,1)}, u32[]{:S(2)}) copy-start(bf16[1,4,128,128]{3,2,1,0:T(8,128)(2,1)} %param.13) | copy-start | bytes 393220
  6.5 141.4 %all-gather.4.cloned.1.call-start = ((), (), s32[]{:S(2)}) async-start(), calls=%async_computation.2 | async-start | bytes 4456448 | tf_op jit(solution)/shard_map/all_gather | solution.py:47
  7.3 411.9 %all-reduce.4.cloned.1.call-start = ((), (), s32[]{:S(2)}) async-start(), calls=%async_computation.3 | async-start | bytes 3145728 | tf_op jit(solution)/shard_map/psum | solution.py:58
  153.1 0.7 copy-start.2
  153.1 11.1 %copy-start.3 = (f32[8,48]{1,0:T(8,128)S(1)}, f32[8,48]{1,0:T(8,128)}, u32[]{:S(2)}) copy-start(f32[8,48]{1,0:T(8,128)} %param.11) | copy-start | bytes 4612
  158.5 370.2 %all-to-all-start = ((s32[32,1,48]{2,1,0:T(1,128)}), s32[32,1,48]{2,1,0:T(1,128)S(1)}, u32[]{:S(2)}, u32[]{:S(2)}) async-start(s32[32,1,48]{2,1,0:T(1,128)} %add.57), calls=%async_computation | async-start | bytes 32768 | tf_op jit(solution)/shard_map/all_to_all | solution.py:94
  419.2 1.9 copy-start.1
  528.7 91.3 %all-to-all-start.1 = ((bf16[32,48,1024]{2,1,0:T(8,128)(2,1)}), bf16[32,48,1024]{2,1,0:T(8,128)(2,1)S(1)}, u32[]{:S(2)}, u32[]{:S(2)}) async-start(bf16[32,48,1024]{2,1,0:T(8,128)(2,1)} %bitcast.76), calls=%async_computation.1 | async-start | bytes 6291456 | tf_op jit(solution)/shard_map/all_to_all | solution.py:87
Sparse Core Ops, SparseCore 0:
  10.5 137.3 all-gather.3
  153.3 265.8 all-reduce.3
where the time goes:
time: 724 us
  waiting for transfers between devices  455 us (63%)
  blocking collectives  193 us (27%)
  starting transfers between devices  26.2 us (4%)
  matrix products  14.5 us (2%)
  between operations  14.2 us (2%)
  local copies, waits for them, and re-layouts  11.9 us (2%)
  other arithmetic  8.54 us (1%)
    psum x1, waiting for transfers between devices, local(): scores = lax.psum(partial_scores, 'slab') + prior_row[None, :]  248 us
    all_gather x1, waiting for transfers between devices, local(): block_rows = lax.all_gather(images, 'orient', axis=0, tiled=True)  139 us
    all_gather x2, blocking collectives, joined(): pieces = jax.tree.map(lambda part: lax.all_gather(part, axis), value)  97.2 us
    unnamed x1, blocking collectives  95.4 us
    all_to_all x1, waiting for transfers between devices, local(): lax.all_to_all(outgoing.reshape(slab_count, capacity, classes * PIECE), '...  67.7 us
    all_to_all x1, starting transfers between devices, local(): lax.all_to_all(outgoing.reshape(slab_count, capacity, classes * PIECE), '...  20.4 us
  transfers between devices with their start and end apart: 4, of which 3 were waited for; matrix products, arithmetic and copies ran while one was open for 4% of the time, Pallas kernels for 0%

commit v1 on v0

v1 whole, which is shorter than its diff:
```python
import jax
import jax.numpy as jnp
from jax import lax
from jax.sharding import Mesh, PartitionSpec as P

PIECE = 128
NAMES = ("yh", "z", "x", "yl", "core")
SIZES = (2, 8, 4, 4, 2)
ORIENT = ("yh", "z")
SLAB = ("x", "yl", "core")
bf16 = jnp.bfloat16
f32 = jnp.float32


def swapped(value, axis):
    return lax.ppermute(value, axis, [(0, 1), (1, 0)])


def exchanged(value, axis):
    return lax.all_to_all(value, axis, 0, 0, tiled=True)


def shared(value, axis, count):
    return exchanged(jnp.broadcast_to(value[None], (count,) + value.shape), axis)


def local(images, projections, noise_weight, prior_score, routing, insert_kernel):
    classes, orient_local, pixels = projections.shape
    columns = classes * orient_local
    rows = images.shape[0]
    orients = lax.axis_size(ORIENT)
    slabs = lax.axis_size(SLAB)
    total_rows = rows * orients
    share = total_rows // slabs
    blocks = pixels // PIECE
    pieces = orient_local * blocks
    voxels = insert_kernel.shape[1] * orients
    half = slabs // 2

    other = swapped(images, "yh")
    upper = lax.axis_index("yh") == 1
    pair = jnp.stack([jnp.where(upper, other, images), jnp.where(upper, images, other)])
    stored = lax.all_gather(pair, "z", axis=0).reshape(total_rows, pixels)

    widened = projections.astype(f32)
    product = widened * noise_weight[None, None, :]
    weighted = product.astype(bf16).reshape(columns, pixels)
    penalty = (-0.5 * jnp.sum(widened * product, axis=2)).reshape(columns)
    partial = (
        lax.dot_general(stored, weighted, (((1,), (1,)), ((), ())), preferred_element_type=f32)
        + penalty[None, :]
    )
    arrived = exchanged(partial.reshape(slabs, share, columns), SLAB)
    scores = jnp.sum(arrived, axis=0) + prior_score.reshape(columns)[None, :]
    peak = jnp.max(scores, axis=1)
    mass = jnp.sum(jnp.exp(scores - peak[:, None]), axis=1)
    stats = shared(jnp.stack([peak, mass]), ORIENT, orients)
    top = jnp.max(stats[:, 0], axis=0)
    total = top + jnp.log(jnp.sum(stats[:, 1] * jnp.exp(stats[:, 0] - top[None]), axis=0))
    own_weights = jnp.exp(scores - total[:, None]).astype(bf16)
    weights = shared(own_weights, SLAB, slabs).reshape(total_rows, classes, orient_local)
    slices = jnp.einsum(
        "iko,ipc->opkc",
        weights,
        stored.reshape(total_rows, blocks, PIECE),
        preferred_element_type=f32,
    ).astype(bf16)
    slices = slices.reshape(pieces, classes * PIECE)

    owner = routing[0, :, :, 0].reshape(pieces)
    voxel = routing[0, :, :, 1].reshape(pieces)
    far = (owner % 2) ^ lax.axis_index("core")
    slot = (far * half + owner // 2) * voxels + voxel
    placing = (
        jnp.arange(slabs * voxels, dtype=jnp.int32)[:, None] == slot[None, :]
    ).astype(bf16)
    placed = jnp.dot(placing, slices, preferred_element_type=f32)
    width = classes * PIECE
    near, away = placed[: half * voxels], placed[half * voxels :].astype(bf16)
    summed = (near + swapped(away, "core").astype(f32)).astype(bf16)
    summed = exchanged(summed.reshape(4, 4 * voxels, width), "x")
    summed = jnp.sum(summed.astype(f32), axis=0).astype(bf16)
    summed = exchanged(summed.reshape(4, voxels, width), "yl")
    summed = jnp.sum(summed.astype(f32), axis=0)
    summed = exchanged(summed.reshape(orients, voxels // orients, width), ORIENT)
    own_blocks = jnp.sum(summed, axis=0)
    rounded = own_blocks.astype(bf16).reshape(own_blocks.shape[0], classes, PIECE)
    volume = jnp.einsum("vkc,vce->vke", rounded, insert_kernel[0], preferred_element_type=f32)
    return volume[None]


def solution(mesh):
    fine = Mesh(mesh.devices.reshape(SIZES), NAMES)
    return jax.shard_map(
        local,
        mesh=fine,
        in_specs=(
            P(ORIENT, SLAB),
            P(None, ORIENT, SLAB),
            P(SLAB),
            P(None, ORIENT),
            P(SLAB, ORIENT, None, None),
            P(SLAB, ORIENT, None, None),
        ),
        out_specs=P(SLAB, ORIENT, None, None),
        check_vma=False,
    )
```

time: 724 us -> 279 us (0.39)
  waiting for transfers between devices: 455 us -> 129 us
  blocking collectives: 193 us -> 80.6 us
    psum x1 -> x0, waiting for transfers between devices: 248 us -> none  [local(): scores = lax.psum(partial_scores, 'slab') + prior_row[None, :]]
    all_gather x2 -> x0, blocking collectives: 97.2 us -> none  [joined(): pieces = jax.tree.map(lambda part: lax.all_gather(part, axis), value)]
    unnamed x1 -> x0, blocking collectives: 95.4 us -> none
    all_to_all x0 -> x4, blocking collectives: none -> 80.6 us  [exchanged(): return lax.all_to_all(value, axis, 0, 0, tiled=True)]
    all_gather x1, waiting for transfers between devices: 139 us -> 66 us  [local(): stored = lax.all_gather(pair, 'z', axis=0).reshape(total_rows, pixels)]
    all_to_all x2, waiting for transfers between devices: 67.7 us -> 51 us  [exchanged(): return lax.all_to_all(value, axis, 0, 0, tiled=True)]
    all_to_all x2, starting transfers between devices: 26.1 us -> 14 us  [exchanged(): return lax.all_to_all(value, axis, 0, 0, tiled=True)]
    ppermute x0 -> x2, waiting for transfers between devices: none -> 12.1 us  [swapped(): return lax.ppermute(value, axis, [(0, 1), (1, 0)])]
  transfers between devices with their start and end apart: 4 -> 5, of which waited for: 3 -> 5; matrix products, arithmetic and copies ran while one was open for 4% -> 2% of each run, Pallas kernels for 0% -> 0%
where the time goes in v1:
time: 279 us; the launch traced here: 277 us
  waiting for transfers between devices  129 us (46%)
  blocking collectives  80.6 us (29%)
  starting transfers between devices  24.4 us (9%)
  matrix products  14.1 us (5%)
  between operations  13.6 us (5%)
  local copies, waits for them, and re-layouts  11.1 us (4%)
  other arithmetic  4.32 us (2%)
    all_to_all x4, blocking collectives, exchanged(): return lax.all_to_all(value, axis, 0, 0, tiled=True)  80.6 us
    all_gather x1, waiting for transfers between devices, local(): stored = lax.all_gather(pair, 'z', axis=0).reshape(total_rows, pixels)  66 us
    all_to_all x2, waiting for transfers between devices, exchanged(): return lax.all_to_all(value, axis, 0, 0, tiled=True)  51 us
    all_to_all x2, starting transfers between devices, exchanged(): return lax.all_to_all(value, axis, 0, 0, tiled=True)  14 us
    ppermute x2, waiting for transfers between devices, swapped(): return lax.ppermute(value, axis, [(0, 1), (1, 0)])  12.1 us
    ppermute x2, starting transfers between devices, swapped(): return lax.ppermute(value, axis, [(0, 1), (1, 0)])  10.4 us
    dot_general x1, matrix products, local(): lax.dot_general(stored, weighted, (((1,), (1,)), ((), ())), preferred_ele...  5.73 us
    unnamed x11, local copies, waits for them, and re-layouts  5.6 us
  transfers between devices with their start and end apart: 5, of which 5 were waited for; matrix products, arithmetic and copies ran while one was open for 2% of the time, Pallas kernels for 0%

profile of v1, /device:TPU:6, one launch (start us, length us, event | category | flops | bytes accessed | tf_op | source)
XLA Modules:
  0.0 277.2 jit_solution(7272904982756691127)
XLA Ops:
  6.5 7.9 %collective-permute-start = (bf16[64,2048]{1,0:T(8,128)(2,1)}, bf16[64,2048]{1,0:T(8,128)(2,1)S(1)}, u32[]{:S(2)}, u32[]{:S(2)}) collective-permute-start(bf16[64,2048]{1,0:T(8,128)(2,1)} %param.6), channel_id=1, source_target_pairs={{0,256},{256,0},{1,257},{257,1},{2,258},{258,2},{3,259},{259,3},{4... | collective-permute-start | bytes 786440 | tf_op jit(solution)/shard_map/ppermute | solution.py:16
  14.4 8.3 %collective-permute-done = bf16[64,2048]{1,0:T(8,128)(2,1)S(1)} collective-permute-done((bf16[64,2048]{1,0:T(8,128)(2,1)}, bf16[64,2048]{1,0:T(8,128)(2,1)S(1)}, u32[]{:S(2)}, u32[]{:S(2)}) %collective-permute-start) | collective-permute-done | bytes 262176 | tf_op jit(solution)/shard_map/ppermute | solution.py:16
  22.7 1.0 select_bitcast_fusion.1
  23.7 0.8 pad_maximum_fusion
  25.2 66.0 %all-gather.3.cloned.1.call-done = bf16[16,64,2048]{2,1,0:T(8,128)(2,1)} async-done(((bf16[2,64,2048]{2,1,0:T(8,128)(2,1)}), bf16[16,64,2048]{2,1,0:T(8,128)(2,1)}) %all-gather.3.cloned.1.call-update) | async-done | bytes 4194320 | tf_op jit(solution)/shard_map/all_gather | solution.py:43
  91.2 5.7 %convolution_add_fusion = f32[1024,384]{1,0:T(8,128)} fusion(bf16[1024,2048]{1,0:T(8,128)(2,1)} %bitcast.52, bf16[384,2048]{1,0:T(8,128)(2,1)S(1)} %bitcast.56, f32[384]{0:T(512)S(1)} %mul.56), kind=kOutput, calls=%fused_computation.15 | convolution fusion | flops 1611005952 | bytes 7341568 | tf_op jit(solution)/shard_map/dot_general | solution.py:50
  97.0 7.9 %all-to-all-start = ((f32[32,32,384]{2,1,0:T(8,128)}), f32[32,32,384]{2,1,0:T(8,128)S(1)}, u32[]{:S(2)}, u32[]{:S(2)}) async-start(f32[32,32,384]{2,1,0:T(8,128)} %bitcast.57), calls=%async_computation | async-start | bytes 3145728 | tf_op jit(solution)/shard_map/all_to_all | solution.py:20
  105.0 36.9 %all-to-all-done = f32[32,32,384]{2,1,0:T(8,128)S(1)} async-done(((f32[32,32,384]{2,1,0:T(8,128)}), f32[32,32,384]{2,1,0:T(8,128)S(1)}, u32[]{:S(2)}, u32[]{:S(2)}) %all-to-all-start) | async-done | bytes 1572896 | tf_op jit(solution)/shard_map/all_to_all | solution.py:20
  142.3 18.7 %all_to_all.30 = f32[16,2,32]{2,1,0:T(2,128)S(1)} all-to-all(f32[16,2,32]{2,1,0:T(2,128)S(1)} %broadcast_in_dim.6), channel_id=1, replica_groups=mesh['yh'=2,'z'=8,'x'=4,'yl'=4,'core'=2] {'yh','z'}, dimensions={0} | all-to-all | bytes 8192 | tf_op jit(solution)/shard_map/all_to_all | solution.py:20
  161.1 1.0 broadcast_in_dim.7
  162.1 6.1 %all-to-all-start.2 = ((bf16[32,32,384]{2,1,0:T(8,128)(2,1)}), bf16[32,32,384]{2,1,0:T(8,128)(2,1)S(1)}, u32[]{:S(2)}, u32[]{:S(2)}) async-start(bf16[32,32,384]{2,1,0:T(8,128)(2,1)} %broadcast_in_dim.7), calls=%async_computation.2 | async-start | bytes 1572864 | tf_op jit(solution)/shard_map/all_to_all | solution.py:20
  168.6 5.6 %copy.38 = bf16[128,8,16,128]{3,2,1,0:T(8,128)(2,1)} copy(bf16[128,8,16,128]{3,1,2,0:T(8,128)(2,1)} %bitcast.53) | data formatting | bytes 8388608
  174.2 14.1 %all-to-all-done.2 = bf16[32,32,384]{2,1,0:T(8,128)(2,1)S(1)} async-done(((bf16[32,32,384]{2,1,0:T(8,128)(2,1)}), bf16[32,32,384]{2,1,0:T(8,128)(2,1)S(1)}, u32[]{:S(2)}, u32[]{:S(2)}) %all-to-all-start.2) | async-done | bytes 786464 | tf_op jit(solution)/shard_map/all_to_all | solution.py:20
  188.3 1.8 reshape.140
  190.1 1.4 copy.30
  191.6 4.0 %fusion.11 = bf16[48,16,8,128]{3,0,2,1:T(8,128)(2,1)S(1)} fusion(bf16[1024,16,128,1]{2,1,0,3:T(8,128)(2,1)} %bitcast.54, bf16[1024,8,48]{0,2,1:T(8,128)(2,1)S(1)} %copy.30), kind=kOutput, calls=%fused_computation.14 | convolution fusion | flops 1611399168 | bytes 6553600 | tf_op jit(solution)/shard_map/iko,ipc->opkc/dot_general | solution.py:62
  196.0 3.6 %fusion = f32[2048,1024]{1,0:T(8,128)S(1)} fusion(s32[768]{0:T(1024)S(1)} %fusion.22, bf16[96,8,8,128]{3,2,1,0:T(8,128)(2,1)S(1)} %bitcast.58), kind=kOutput, calls=%fused_computation.1 | convolution fusion | flops 3222798336 | bytes 9964544 | tf_op jit(solution)/shard_map/dot_general | solution.py:77
  199.9 2.5 collective-permute-start.1
  202.4 3.8 %collective-permute-done.1 = bf16[1024,1024]{1,0:T(8,128)(2,1)S(1)} collective-permute-done((bf16[1024,1024]{1,0:T(8,128)(2,1)S(1)}, bf16[1024,1024]{1,0:T(8,128)(2,1)S(1)}, u32[]{:S(2)}, u32[]{:S(2)}) %collective-permute-start.1) | collective-permute-done | bytes 2097184 | tf_op jit(solution)/shard_map/ppermute | solution.py:16
  206.2 0.8 fusion.1
  207.0 29.7 %all_to_all.31 = bf16[4,256,1024]{2,1,0:T(8,128)(2,1)S(1)} all-to-all(bf16[4,256,1024]{2,1,0:T(8,128)(2,1)S(1)} %bitcast.51), channel_id=1, replica_groups=mesh['yh'=2,'z'=8,'x'=4,'yl'=4,'core'=2] {'x'}, dimensions={0} | all-to-all | bytes 4194304 | tf_op jit(solution)/shard_map/all_to_all | solution.py:20
  237.1 16.7 %all_to_all.32 = bf16[4,64,1024]{2,1,0:T(8,128)(2,1)S(1)} all-to-all(bf16[4,64,1024]{2,1,0:T(8,128)(2,1)S(1)} %bitcast.55), channel_id=1, replica_groups=mesh['yh'=2,'z'=8,'x'=4,'yl'=4,'core'=2] {'yl'}, dimensions={0} | all-to-all | bytes 1048576 | tf_op jit(solution)/shard_map/all_to_all | solution.py:20
  254.0 15.6 %all_to_all.33 = f32[16,4,1024]{2,1,0:T(4,128)S(1)} all-to-all(f32[16,4,1024]{2,1,0:T(4,128)S(1)} %reshape.144), channel_id=1, replica_groups=mesh['yh'=2,'z'=8,'x'=4,'yl'=4,'core'=2] {'yh','z'}, dimensions={0} | all-to-all | bytes 524288 | tf_op jit(solution)/shard_map/all_to_all | solution.py:20
  269.6 0.8 convolution_bitcast_fusion
  (38 shorter events, 3.0 us)
Async XLA Ops:
  6.5 263.1 %copy-start = (bf16[1,4,128,128]{3,2,1,0:T(8,128)(2,1)S(1)}, bf16[1,4,128,128]{3,2,1,0:T(8,128)(2,1)}, u32[]{:S(2)}) copy-start(bf16[1,4,128,128]{3,2,1,0:T(8,128)(2,1)} %param.11) | copy-start | bytes 393220
  6.5 18.1 %copy-start.3 = (f32[2048]{0:T(1024)S(1)}, f32[2048]{0:T(1024)}, u32[]{:S(2)}) copy-start(f32[2048]{0:T(1024)} %param.8) | copy-start | bytes 24580
  6.5 18.1 %copy-start.1 = (bf16[8,48,2048]{2,1,0:T(8,128)(2,1)S(1)}, bf16[8,48,2048]{2,1,0:T(8,128)(2,1)}, u32[]{:S(2)}) copy-start(bf16[8,48,2048]{2,1,0:T(8,128)(2,1)} %param.7) | copy-start | bytes 4718596
  6.5 84.7 %all-gather.3.cloned.1.call-start = ((), (), s32[]{:S(2)}) async-start(), calls=%async_computation.6 | async-start | bytes 4718592 | tf_op jit(solution)/shard_map/all_gather | solution.py:43
  6.5 16.2 %collective-permute-start = (bf16[64,2048]{1,0:T(8,128)(2,1)}, bf16[64,2048]{1,0:T(8,128)(2,1)S(1)}, u32[]{:S(2)}, u32[]{:S(2)}) collective-permute-start(bf16[64,2048]{1,0:T(8,128)(2,1)} %param.6), channel_id=1, source_target_pairs={{0,256},{256,0},{1,257},{257,1},{2,258},{258,2},{3,259},{259,3},{4... | collective-permute-start | bytes 786440 | tf_op jit(solution)/shard_map/ppermute | solution.py:16
  97.0 7.9 %copy-start.4 = (f32[8,48]{1,0:T(8,128)S(1)}, f32[8,48]{1,0:T(8,128)}, u32[]{:S(2)}) copy-start(f32[8,48]{1,0:T(8,128)} %param.9) | copy-start | bytes 4612
  97.0 44.9 %all-to-all-start = ((f32[32,32,384]{2,1,0:T(8,128)}), f32[32,32,384]{2,1,0:T(8,128)S(1)}, u32[]{:S(2)}, u32[]{:S(2)}) async-start(f32[32,32,384]{2,1,0:T(8,128)} %bitcast.57), calls=%async_computation | async-start | bytes 3145728 | tf_op jit(solution)/shard_map/all_to_all | solution.py:20
  105.0 63.3 %copy-start.2 = (s32[1,48,16,2]{1,3,2,0:T(2,128)S(1)}, s32[1,48,16,2]{1,3,2,0:T(2,128)}, u32[]{:S(2)}) copy-start(s32[1,48,16,2]{1,3,2,0:T(2,128)} %param.10) | copy-start | bytes 18436
  162.1 26.2 %all-to-all-start.2 = ((bf16[32,32,384]{2,1,0:T(8,128)(2,1)}), bf16[32,32,384]{2,1,0:T(8,128)(2,1)S(1)}, u32[]{:S(2)}, u32[]{:S(2)}) async-start(bf16[32,32,384]{2,1,0:T(8,128)(2,1)} %broadcast_in_dim.7), calls=%async_computation.2 | async-start | bytes 1572864 | tf_op jit(solution)/shard_map/all_to_all | solution.py:20
  199.9 6.3 %collective-permute-start.1 = (bf16[1024,1024]{1,0:T(8,128)(2,1)S(1)}, bf16[1024,1024]{1,0:T(8,128)(2,1)S(1)}, u32[]{:S(2)}, u32[]{:S(2)}) collective-permute-start(bf16[1024,1024]{1,0:T(8,128)(2,1)S(1)} %slice.34), channel_id=1, source_target_pairs={{0,1},{1,0},{2,3},{3,2},{4,5},{5,4},{6,7},{7,6},{8,9},{9,8},{10,11... | collective-permute-start | bytes 6291464 | tf_op jit(solution)/shard_map/ppermute | solution.py:16
Sparse Core Ops, SparseCore 0:
  24.7 66.4 all-gather.2

commit v2 on v1

v2 whole, which is shorter than its diff:
```python
import jax
import jax.numpy as jnp
from jax import lax
from jax.sharding import Mesh, PartitionSpec as P

PIECE = 128
NAMES = ("yh", "z", "x", "yl", "core")
SIZES = (2, 8, 4, 4, 2)
ORIENT = ("yh", "z")
SLAB = ("x", "yl", "core")
bf16 = jnp.bfloat16
f32 = jnp.float32


def swapped(value, axis):
    return lax.ppermute(value, axis, [(0, 1), (1, 0)])


def exchanged(value, axis):
    return lax.all_to_all(value, axis, 0, 0, tiled=True)


def shared(value, axis, count):
    return exchanged(jnp.broadcast_to(value[None], (count,) + value.shape), axis)


def turned(block, step):
    count = 8
    return lax.ppermute(block, "z", [(i, (i + step) % count) for i in range(count)])


def ring_gathered(block):
    count = 8
    z = lax.axis_index("z")
    held = jnp.zeros((count,) + block.shape, block.dtype)
    held = lax.dynamic_update_index_in_dim(held, block, z, 0)
    up = down = block
    for step in range(1, count // 2 + 1):
        up = turned(up, 1)
        held = lax.dynamic_update_index_in_dim(held, up, (z - step) % count, 0)
        if step < count // 2:
            down = turned(down, -1)
            held = lax.dynamic_update_index_in_dim(held, down, (z + step) % count, 0)
    return held


def local(images, projections, noise_weight, prior_score, routing, insert_kernel):
    classes, orient_local, pixels = projections.shape
    columns = classes * orient_local
    rows = images.shape[0]
    orients, slabs, half = 32 // 2, 32, 16
    plane_rows = rows * orients // 2
    share = plane_rows // slabs
    blocks = pixels // PIECE
    pieces = orient_local * blocks
    voxels = insert_kernel.shape[1] * orients
    core = lax.axis_index("core")
    upper = lax.axis_index("yh") == 1

    other = swapped(images, "yh")
    own_plane = ring_gathered(images).reshape(plane_rows, pixels)
    other_plane = lax.all_gather(other, "z", axis=0).reshape(plane_rows, pixels)

    widened = projections.astype(f32)
    product = widened * noise_weight[None, None, :]
    weighted = product.astype(bf16).reshape(columns, pixels)
    penalty = (-0.5 * jnp.sum(widened * product, axis=2)).reshape(columns)
    prior = prior_score.reshape(columns)

    def plane_scores(stored):
        partial = (
            lax.dot_general(stored, weighted, (((1,), (1,)), ((), ())), preferred_element_type=f32)
            + penalty[None, :]
        )
        side = plane_rows // 2
        far = lax.dynamic_slice_in_dim(partial, (1 - core) * side, side, 0)
        near = lax.dynamic_slice_in_dim(partial, core * side, side, 0)
        summed = near + swapped(far, "core")
        arrived = exchanged(summed.reshape(half, share, columns), ("x", "yl"))
        return jnp.sum(arrived, axis=0) + prior[None, :]

    scores = jnp.stack([plane_scores(own_plane), plane_scores(other_plane)])
    peak = jnp.max(scores, axis=2)
    mass = jnp.sum(jnp.exp(scores - peak[:, :, None]), axis=2)
    stats = jnp.stack([peak, mass])
    stats = jnp.where(upper, stats[:, ::-1], stats)
    stats = shared(stats.reshape(2, 2 * share), ORIENT, orients)
    top = jnp.max(stats[:, 0], axis=0)
    total = top + jnp.log(jnp.sum(stats[:, 1] * jnp.exp(stats[:, 0] - top[None]), axis=0))
    total = total.reshape(2, share)
    total = jnp.where(upper, total[::-1], total)
    own_weights = jnp.exp(scores - total[:, :, None]).astype(bf16)
    weights = shared(own_weights, ("x", "yl"), half)
    both = jnp.stack([weights, swapped(weights, "core")])
    both = jnp.where(core == 1, both[::-1], both)
    both = both.transpose(2, 0, 1, 3, 4).reshape(2, plane_rows, classes, orient_local)

    def plane_slices(plane_weights, stored):
        return jnp.einsum(
            "iko,ipc->opkc",
            plane_weights,
            stored.reshape(plane_rows, blocks, PIECE),
            preferred_element_type=f32,
        )

    slices = plane_slices(both[0], own_plane) + plane_slices(both[1], other_plane)
    slices = slices.astype(bf16).reshape(pieces, classes * PIECE)

    owner = routing[0, :, :, 0].reshape(pieces)
    voxel = routing[0, :, :, 1].reshape(pieces)
    far = (owner % 2) ^ core
    slot = (far * half + owner // 2) * voxels + voxel
    placing = (
        jnp.arange(slabs * voxels, dtype=jnp.int32)[:, None] == slot[None, :]
    ).astype(bf16)
    width = classes * PIECE
    middle = half * voxels
    away = jnp.dot(placing[middle:], slices, preferred_element_type=f32).astype(bf16)
    near = jnp.dot(placing[:middle], slices, preferred_element_type=f32)
    summed = (near + swapped(away, "core").astype(f32)).astype(bf16)
    summed = exchanged(summed.reshape(4, 4 * voxels, width), "x")
    summed = jnp.sum(summed.astype(f32), axis=0).astype(bf16)
    summed = exchanged(summed.reshape(4 * orients, voxels // orients, width), ("yl", "yh", "z"))
    own_blocks = jnp.sum(summed.astype(f32), axis=0)
    rounded = own_blocks.astype(bf16).reshape(own_blocks.shape[0], classes, PIECE)
    volume = jnp.einsum("vkc,vce->vke", rounded, insert_kernel[0], preferred_element_type=f32)
    return volume[None]


def solution(mesh):
    fine = Mesh(mesh.devices.reshape(SIZES), NAMES)
    return jax.shard_map(
        local,
        mesh=fine,
        in_specs=(
            P(ORIENT, SLAB),
            P(None, ORIENT, SLAB),
            P(SLAB),
            P(None, ORIENT),
            P(SLAB, ORIENT, None, None),
            P(SLAB, ORIENT, None, None),
        ),
        out_specs=P(SLAB, ORIENT, None, None),
        check_vma=False,
    )
```

time: 279 us -> 243 us (0.87)
  waiting for transfers between devices: 129 us -> 49.9 us
  starting transfers between devices: 24.4 us -> 66.8 us
  blocking collectives: 80.6 us -> 70 us
  local copies, waits for them, and re-layouts: 11.1 us -> 18.6 us
  other arithmetic: 4.32 us -> 7.83 us
    all_gather x1, waiting for transfers between devices: 66 us -> 2.64 us  [local(): other_plane = lax.all_gather(other, 'z', axis=0).reshape(plane_rows, pixels)]
    all_to_all x2 -> x3, waiting for transfers between devices: 51 us -> 21.8 us  [exchanged(): return lax.all_to_all(value, axis, 0, 0, tiled=True)]
    ppermute x0 -> x7, starting transfers between devices: none -> 29 us  [turned(): lax.ppermute(block, 'z', [(i, (i + step) % count) for i in range(count)])]
    ppermute x0 -> x7, waiting for transfers between devices: none -> 18.1 us  [turned(): lax.ppermute(block, 'z', [(i, (i + step) % count) for i in range(count)])]
    all_to_all x4 -> x3, blocking collectives: 80.6 us -> 70 us  [exchanged(): return lax.all_to_all(value, axis, 0, 0, tiled=True)]
    all_to_all x2 -> x3, starting transfers between devices: 14 us -> 21.7 us  [exchanged(): return lax.all_to_all(value, axis, 0, 0, tiled=True)]
    squeeze x0 -> x4, local copies, waits for them, and re-layouts: none -> 6.85 us  [the longest x2 3.43 us: local(): both[1]]
    ppermute x2 -> x5, starting transfers between devices: 10.4 us -> 16.1 us  [swapped(): return lax.ppermute(value, axis, [(0, 1), (1, 0)])]
  transfers between devices with their start and end apart: 5 -> 16, of which waited for: 5 -> 10; matrix products, arithmetic and copies ran while one was open for 2% -> 8% of each run, Pallas kernels for 0% -> 0%
where the time goes in v2:
time: 243 us; the launch traced here: 240 us
  blocking collectives  70 us (29%)
  starting transfers between devices  66.8 us (27%)
  waiting for transfers between devices  49.9 us (21%)
  local copies, waits for them, and re-layouts  18.6 us (8%)
  between operations  14 us (6%)
  matrix products  12.6 us (5%)
  other arithmetic  7.83 us (3%)
    all_to_all x3, blocking collectives, exchanged(): return lax.all_to_all(value, axis, 0, 0, tiled=True)  70 us
    ppermute x7, starting transfers between devices, turned(): lax.ppermute(block, 'z', [(i, (i + step) % count) for i in range(count)])  29 us
    all_to_all x3, waiting for transfers between devices, exchanged(): return lax.all_to_all(value, axis, 0, 0, tiled=True)  21.8 us
    all_to_all x3, starting transfers between devices, exchanged(): return lax.all_to_all(value, axis, 0, 0, tiled=True)  21.7 us
    ppermute x7, waiting for transfers between devices, turned(): lax.ppermute(block, 'z', [(i, (i + step) % count) for i in range(count)])  18.1 us
    ppermute x5, starting transfers between devices, swapped(): return lax.ppermute(value, axis, [(0, 1), (1, 0)])  16.1 us
    ppermute x5, waiting for transfers between devices, swapped(): return lax.ppermute(value, axis, [(0, 1), (1, 0)])  7.36 us
  transfers between devices with their start and end apart: 16, of which 10 were waited for; matrix products, arithmetic and copies ran while one was open for 8% of the time, Pallas kernels for 0%

profile of v2, /device:TPU:6, one launch (start us, length us, event | category | flops | bytes accessed | tf_op | source)
XLA Modules:
  0.0 239.7 jit_solution(7274561646098538192)
XLA Ops:
  6.5 4.4 %collective-permute-start = (bf16[64,2048]{1,0:T(8,128)(2,1)}, bf16[64,2048]{1,0:T(8,128)(2,1)S(1)}, u32[]{:S(2)}, u32[]{:S(2)}) collective-permute-start(bf16[64,2048]{1,0:T(8,128)(2,1)} %param.6), channel_id=1, source_target_pairs={{0,32},{32,64},{64,96},{96,128},{128,160},{160,192},{192,224},{224... | collective-permute-start | bytes 786440 | tf_op jit(solution)/shard_map/ppermute | solution.py:29
  10.9 8.6 %collective-permute-start.1 = (bf16[64,2048]{1,0:T(8,128)(2,1)}, bf16[64,2048]{1,0:T(8,128)(2,1)S(1)}, u32[]{:S(2)}, u32[]{:S(2)}) collective-permute-start(bf16[64,2048]{1,0:T(8,128)(2,1)} %param.6), channel_id=1, source_target_pairs={{0,224},{32,0},{64,32},{96,64},{128,96},{160,128},{192,160},{224,1... | collective-permute-start | bytes 786440 | tf_op jit(solution)/shard_map/ppermute | solution.py:29
  19.5 7.7 %collective-permute-start.8 = (bf16[64,2048]{1,0:T(8,128)(2,1)}, bf16[64,2048]{1,0:T(8,128)(2,1)S(1)}, u32[]{:S(2)}, u32[]{:S(2)}) collective-permute-start(bf16[64,2048]{1,0:T(8,128)(2,1)} %param.6), channel_id=1, source_target_pairs={{0,256},{256,0},{1,257},{257,1},{2,258},{258,2},{3,259},{259,3},{4... | collective-permute-start | bytes 786440 | tf_op jit(solution)/shard_map/ppermute | solution.py:16
  27.4 3.1 %fusion = (f32[8,48]{1,0:T(8,128)S(1)}, bf16[8,48,2048]{2,1,0:T(8,128)(2,1)}) fusion(bf16[8,48,2048]{2,1,0:T(8,128)(2,1)} %param.7, f32[2048]{0:T(1024)} %param.8), kind=kLoop, calls=%fused_computation.4 | loop fusion | flops 3931776 | bytes 3155456 | tf_op jit(solution)/shard_map/reduce_sum | solution.py:67
  32.8 5.1 %collective-permute-start.3 = (bf16[64,2048]{1,0:T(8,128)(2,1)S(1)}, bf16[64,2048]{1,0:T(8,128)(2,1)S(1)}, u32[]{:S(2)}, u32[]{:S(2)}) collective-permute-start(bf16[64,2048]{1,0:T(8,128)(2,1)S(1)} %collective-permute-done.1), channel_id=1, source_target_pairs={{0,224},{32,0},{64,32},{96,64},{128,96},{160,128},{192,160},{224,1... | collective-permute-start | bytes 786440 | tf_op jit(solution)/shard_map/ppermute | solution.py:29
  38.7 2.7 %collective-permute-done.2 = bf16[64,2048]{1,0:T(8,128)(2,1)S(1)} collective-permute-done((bf16[64,2048]{1,0:T(8,128)(2,1)S(1)}, bf16[64,2048]{1,0:T(8,128)(2,1)S(1)}, u32[]{:S(2)}, u32[]{:S(2)}) %collective-permute-start.2) | collective-permute-done | bytes 262176 | tf_op jit(solution)/shard_map/ppermute | solution.py:29
  43.4 5.1 %collective-permute-start.5 = (bf16[64,2048]{1,0:T(8,128)(2,1)S(1)}, bf16[64,2048]{1,0:T(8,128)(2,1)S(1)}, u32[]{:S(2)}, u32[]{:S(2)}) collective-permute-start(bf16[64,2048]{1,0:T(8,128)(2,1)S(1)} %collective-permute-done.3), channel_id=1, source_target_pairs={{0,224},{32,0},{64,32},{96,64},{128,96},{160,128},{192,160},{224,1... | collective-permute-start | bytes 786440 | tf_op jit(solution)/shard_map/ppermute | solution.py:29
  48.6 2.5 %collective-permute-done.4 = bf16[64,2048]{1,0:T(8,128)(2,1)S(1)} collective-permute-done((bf16[64,2048]{1,0:T(8,128)(2,1)S(1)}, bf16[64,2048]{1,0:T(8,128)(2,1)S(1)}, u32[]{:S(2)}, u32[]{:S(2)}) %collective-permute-start.4) | collective-permute-done | bytes 262176 | tf_op jit(solution)/shard_map/ppermute | solution.py:29
  53.1 12.8 %collective-permute-done.6 = bf16[64,2048]{1,0:T(8,128)(2,1)S(1)} collective-permute-done((bf16[64,2048]{1,0:T(8,128)(2,1)S(1)}, bf16[64,2048]{1,0:T(8,128)(2,1)S(1)}, u32[]{:S(2)}, u32[]{:S(2)}) %collective-permute-start.6) | collective-permute-done | bytes 262176 | tf_op jit(solution)/shard_map/ppermute | solution.py:29
  72.7 8.7 %all-to-all-start = ((f32[16,16,384]{2,1,0:T(8,128)}), f32[16,16,384]{2,1,0:T(8,128)S(1)}, u32[]{:S(2)}, u32[]{:S(2)}) async-start(f32[16,16,384]{2,1,0:T(8,128)} %bitcast.11), calls=%async_computation | async-start | bytes 786432 | tf_op jit(solution)/shard_map/all_to_all | solution.py:20
  81.4 2.6 %all-gather.3.cloned.1.call-done = bf16[512,2048]{1,0:T(8,128)(2,1)} async-done(((bf16[64,2048]{1,0:T(8,128)(2,1)}), bf16[512,2048]{1,0:T(8,128)(2,1)}) %all-gather.3.cloned.1.call-update) | async-done | bytes 2097168 | tf_op jit(solution)/shard_map/all_gather | solution.py:62
  84.1 3.1 %convolution_add_fusion = f32[384,512]{1,0:T(8,128)S(1)} fusion(bf16[384,2048]{1,0:T(8,128)(2,1)} %bitcast.103, bf16[512,2048]{1,0:T(8,128)(2,1)} %all-gather.3.cloned.1.call-done, f32[384]{0:T(512)S(1)} %mul.64), kind=kOutput, calls=%fused_computation.18 | convolution fusion | flops 805502976 | bytes 4457984 | tf_op jit(solution)/shard_map/dot_general | solution.py:72
  93.1 7.2 %all-to-all-start.1 = ((f32[16,16,384]{2,1,0:T(8,128)}), f32[16,16,384]{2,1,0:T(8,128)S(1)}, u32[]{:S(2)}, u32[]{:S(2)}) async-start(f32[16,16,384]{2,1,0:T(8,128)} %bitcast.15), calls=%async_computation.1 | async-start | bytes 786432 | tf_op jit(solution)/shard_map/all_to_all | solution.py:20
  100.5 11.6 %all-to-all-done.1 = f32[16,16,384]{2,1,0:T(8,128)S(1)} async-done(((f32[16,16,384]{2,1,0:T(8,128)}), f32[16,16,384]{2,1,0:T(8,128)S(1)}, u32[]{:S(2)}, u32[]{:S(2)}) %all-to-all-start.1) | async-done | bytes 393248 | tf_op jit(solution)/shard_map/all_to_all | solution.py:20
  112.5 17.8 %all_to_all.30 = f32[16,2,32]{2,1,0:T(2,128)S(1)} all-to-all(f32[16,2,32]{2,1,0:T(2,128)S(1)} %broadcast_in_dim.60), channel_id=1, replica_groups=mesh['yh'=2,'z'=8,'x'=4,'yl'=4,'core'=2] {'yh','z'}, dimensions={0} | all-to-all | bytes 8192 | tf_op jit(solution)/shard_map/all_to_all | solution.py:20
  131.4 5.8 %all-to-all-start.3 = ((bf16[16,2,16,384]{3,2,1,0:T(8,128)(2,1)}), bf16[16,2,16,384]{3,2,1,0:T(8,128)(2,1)S(1)}, u32[]{:S(2)}, u32[]{:S(2)}) async-start(bf16[16,2,16,384]{3,2,1,0:T(8,128)(2,1)} %broadcast_in_dim.61), calls=%async_computation.3 | async-start | bytes 786432 | tf_op jit(solution)/shard_map/all_to_all | solution.py:20
  137.5 9.0 %all-to-all-done.3 = bf16[16,2,16,384]{3,2,1,0:T(8,128)(2,1)S(1)} async-done(((bf16[16,2,16,384]{3,2,1,0:T(8,128)(2,1)}), bf16[16,2,16,384]{3,2,1,0:T(8,128)(2,1)S(1)}, u32[]{:S(2)}, u32[]{:S(2)}) %all-to-all-start.3) | async-done | bytes 393248 | tf_op jit(solution)/shard_map/all_to_all | solution.py:20
  148.6 2.5 %iota_compare_fusion = pred[2048,768]{1,0:T(32,128)(4,1)} fusion(s32[768]{0:T(1024)S(1)} %fusion.28), kind=kLoop, calls=%fused_computation | loop fusion | flops 1572864 | bytes 1575936 | tf_op jit(solution)/shard_map/eq | solution.py:114
  153.0 2.9 %copy.57 = bf16[512,2048]{0,1:T(8,128)(2,1)S(1)} copy(bf16[512,2048]{1,0:T(8,128)(2,1)} %all-gather.3.cloned.1.call-done) | data formatting | bytes 4194304 | tf_op jit(solution)/shard_map/all_gather | solution.py:62
  163.9 2.7 %fusion.6 = f32[16,128,8,48]{1,3,2,0:T(8,128)S(1)} fusion(bf16[512,16,128,1]{2,1,0,3:T(8,128)(2,1)} %bitcast.101, bf16[512,8,48]{0,2,1:T(8,128)(2,1)} %copy.56), kind=kOutput, calls=%fused_computation.11 | convolution fusion | flops 805306368 | bytes 5636096 | tf_op jit(solution)/shard_map/iko,ipc->opkc/dot_general | solution.py:99
  171.0 2.4 %collective-permute-start.11 = (bf16[1024,1024]{1,0:T(8,128)(2,1)S(1)}, bf16[1024,1024]{1,0:T(8,128)(2,1)S(1)}, u32[]{:S(2)}, u32[]{:S(2)}) collective-permute-start(bf16[1024,1024]{1,0:T(8,128)(2,1)S(1)} %fusion.8), channel_id=1, source_target_pairs={{0,1},{1,0},{2,3},{3,2},{4,5},{5,4},{6,7},{7,6},{8,9},{9,8},{10,11... | collective-permute-start | bytes 6291464 | tf_op jit(solution)/shard_map/ppermute | solution.py:16
  173.4 3.8 %collective-permute-done.11 = bf16[1024,1024]{1,0:T(8,128)(2,1)S(1)} collective-permute-done((bf16[1024,1024]{1,0:T(8,128)(2,1)S(1)}, bf16[1024,1024]{1,0:T(8,128)(2,1)S(1)}, u32[]{:S(2)}, u32[]{:S(2)}) %collective-permute-start.11) | collective-permute-done | bytes 2097184 | tf_op jit(solution)/shard_map/ppermute | solution.py:16
  179.0 29.9 %all_to_all.31 = bf16[4,256,1024]{2,1,0:T(8,128)(2,1)S(1)} all-to-all(bf16[4,256,1024]{2,1,0:T(8,128)(2,1)S(1)} %bitcast.102), channel_id=1, replica_groups=mesh['yh'=2,'z'=8,'x'=4,'yl'=4,'core'=2] {'x'}, dimensions={0} | all-to-all | bytes 4194304 | tf_op jit(solution)/shard_map/all_to_all | solution.py:20
  209.5 22.3 %all_to_all.32 = bf16[64,4,1024]{2,1,0:T(4,128)(2,1)S(1)} all-to-all(bf16[64,4,1024]{2,1,0:T(4,128)(2,1)S(1)} %reshape.209), channel_id=1, replica_groups=mesh['yh'=2,'z'=8,'x'=4,'yl'=4,'core'=2] {'yl','yh','z'}, dimensions={0} | all-to-all | bytes 1048576 | tf_op jit(solution)/shard_map/all_to_all | solution.py:20
  (92 shorter events, 41.5 us)
Async XLA Ops:
  6.5 225.5 %copy-start = (bf16[1,4,128,128]{3,2,1,0:T(8,128)(2,1)S(1)}, bf16[1,4,128,128]{3,2,1,0:T(8,128)(2,1)}, u32[]{:S(2)}) copy-start(bf16[1,4,128,128]{3,2,1,0:T(8,128)(2,1)} %param.11) | copy-start | bytes 393220
  6.5 77.5 %all-gather.3.cloned.1.call-start = ((), (), s32[]{:S(2)}) async-start(), calls=%async_computation.6 | async-start | bytes 2359296 | tf_op jit(solution)/shard_map/all_gather | solution.py:62
  6.5 24.3 %collective-permute-start = (bf16[64,2048]{1,0:T(8,128)(2,1)}, bf16[64,2048]{1,0:T(8,128)(2,1)S(1)}, u32[]{:S(2)}, u32[]{:S(2)}) collective-permute-start(bf16[64,2048]{1,0:T(8,128)(2,1)} %param.6), channel_id=1, source_target_pairs={{0,32},{32,64},{64,96},{96,128},{128,160},{160,192},{192,224},{224... | collective-permute-start | bytes 786440 | tf_op jit(solution)/shard_map/ppermute | solution.py:29
  10.9 21.8 %collective-permute-start.1 = (bf16[64,2048]{1,0:T(8,128)(2,1)}, bf16[64,2048]{1,0:T(8,128)(2,1)S(1)}, u32[]{:S(2)}, u32[]{:S(2)}) collective-permute-start(bf16[64,2048]{1,0:T(8,128)(2,1)} %param.6), channel_id=1, source_target_pairs={{0,224},{32,0},{64,32},{96,64},{128,96},{160,128},{192,160},{224,1... | collective-permute-start | bytes 786440 | tf_op jit(solution)/shard_map/ppermute | solution.py:29
  19.5 18.4 %collective-permute-start.8 = (bf16[64,2048]{1,0:T(8,128)(2,1)}, bf16[64,2048]{1,0:T(8,128)(2,1)S(1)}, u32[]{:S(2)}, u32[]{:S(2)}) collective-permute-start(bf16[64,2048]{1,0:T(8,128)(2,1)} %param.6), channel_id=1, source_target_pairs={{0,256},{256,0},{1,257},{257,1},{2,258},{258,2},{3,259},{259,3},{4... | collective-permute-start | bytes 786440 | tf_op jit(solution)/shard_map/ppermute | solution.py:16
  27.4 3.4 %copy-start.4 = (bf16[64,2048]{1,0:T(8,128)(2,1)S(1)}, bf16[64,2048]{1,0:T(8,128)(2,1)}, u32[]{:S(2)}) copy-start(bf16[64,2048]{1,0:T(8,128)(2,1)} %param.6) | copy-start | bytes 786436
  30.9 10.6 %collective-permute-start.2 = (bf16[64,2048]{1,0:T(8,128)(2,1)S(1)}, bf16[64,2048]{1,0:T(8,128)(2,1)S(1)}, u32[]{:S(2)}, u32[]{:S(2)}) collective-permute-start(bf16[64,2048]{1,0:T(8,128)(2,1)S(1)} %collective-permute-done), channel_id=1, source_target_pairs={{0,32},{32,64},{64,96},{96,128},{128,160},{160,192},{192,224},{224... | collective-permute-start | bytes 786440 | tf_op jit(solution)/shard_map/ppermute | solution.py:29
  32.8 10.6 %collective-permute-start.3 = (bf16[64,2048]{1,0:T(8,128)(2,1)S(1)}, bf16[64,2048]{1,0:T(8,128)(2,1)S(1)}, u32[]{:S(2)}, u32[]{:S(2)}) collective-permute-start(bf16[64,2048]{1,0:T(8,128)(2,1)S(1)} %collective-permute-done.1), channel_id=1, source_target_pairs={{0,224},{32,0},{64,32},{96,64},{128,96},{160,128},{192,160},{224,1... | collective-permute-start | bytes 786440 | tf_op jit(solution)/shard_map/ppermute | solution.py:29
  37.9 0.7 copy-start.5
  38.7 27.3 %copy-start.2 = (bf16[8,48,2048]{2,1,0:T(8,128)(2,1)S(1)}, bf16[8,48,2048]{2,1,0:T(8,128)(2,1)}, u32[]{:S(2)}) copy-start(bf16[8,48,2048]{2,1,0:T(8,128)(2,1)} %get-tuple-element.6) | copy-start | bytes 4718596
  41.4 9.7 %collective-permute-start.4 = (bf16[64,2048]{1,0:T(8,128)(2,1)S(1)}, bf16[64,2048]{1,0:T(8,128)(2,1)S(1)}, u32[]{:S(2)}, u32[]{:S(2)}) collective-permute-start(bf16[64,2048]{1,0:T(8,128)(2,1)S(1)} %collective-permute-done.2), channel_id=1, source_target_pairs={{0,32},{32,64},{64,96},{96,128},{128,160},{160,192},{192,224},{224... | collective-permute-start | bytes 786440 | tf_op jit(solution)/shard_map/ppermute | solution.py:29
  43.4 9.7 %collective-permute-start.5 = (bf16[64,2048]{1,0:T(8,128)(2,1)S(1)}, bf16[64,2048]{1,0:T(8,128)(2,1)S(1)}, u32[]{:S(2)}, u32[]{:S(2)}) collective-permute-start(bf16[64,2048]{1,0:T(8,128)(2,1)S(1)} %collective-permute-done.3), channel_id=1, source_target_pairs={{0,224},{32,0},{64,32},{96,64},{128,96},{160,128},{192,160},{224,1... | collective-permute-start | bytes 786440 | tf_op jit(solution)/shard_map/ppermute | solution.py:29
  51.1 14.8 %collective-permute-start.6 = (bf16[64,2048]{1,0:T(8,128)(2,1)S(1)}, bf16[64,2048]{1,0:T(8,128)(2,1)S(1)}, u32[]{:S(2)}, u32[]{:S(2)}) collective-permute-start(bf16[64,2048]{1,0:T(8,128)(2,1)S(1)} %collective-permute-done.4), channel_id=1, source_target_pairs={{0,32},{32,64},{64,96},{96,128},{128,160},{160,192},{192,224},{224... | collective-permute-start | bytes 786440 | tf_op jit(solution)/shard_map/ppermute | solution.py:29
  68.1 3.8 %collective-permute-start.7 = (f32[256,384]{1,0:T(8,128)}, f32[256,384]{1,0:T(8,128)S(1)}, u32[]{:S(2)}, u32[]{:S(2)}) collective-permute-start(f32[256,384]{1,0:T(8,128)} %constant_dynamic-slice_fusion), channel_id=1, source_target_pairs={{0,1},{1,0},{2,3},{3,2},{4,5},{5,4},{6,7},{7,6},{8,9},{9,8},{10,11... | collective-permute-start | bytes 1179656 | tf_op jit(solution)/shard_map/ppermute | solution.py:16
  72.7 20.4 %all-to-all-start = ((f32[16,16,384]{2,1,0:T(8,128)}), f32[16,16,384]{2,1,0:T(8,128)S(1)}, u32[]{:S(2)}, u32[]{:S(2)}) async-start(f32[16,16,384]{2,1,0:T(8,128)} %bitcast.11), calls=%async_computation | async-start | bytes 786432 | tf_op jit(solution)/shard_map/all_to_all | solution.py:20
  87.2 13.2 %copy-start.7 = (f32[8,48]{1,0:T(8,128)S(1)}, f32[8,48]{1,0:T(8,128)}, u32[]{:S(2)}) copy-start(f32[8,48]{1,0:T(8,128)} %param.9) | copy-start | bytes 4612
  87.2 3.6 %collective-permute-start.9 = (f32[256,384]{0,1:T(8,128)S(1)}, f32[256,384]{0,1:T(8,128)S(1)}, u32[]{:S(2)}, u32[]{:S(2)}) collective-permute-start(f32[256,384]{0,1:T(8,128)S(1)} %dynamic-slice_bitcast_fusion), channel_id=1, source_target_pairs={{0,1},{1,0},{2,3},{3,2},{4,5},{5,4},{6,7},{7,6},{8,9},{9,8},{10,11... | collective-permute-start | bytes 1179656 | tf_op jit(solution)/shard_map/ppermute | solution.py:16
  90.9 46.2 %copy-start.6 = (s32[1,48,16,2]{1,3,2,0:T(2,128)S(1)}, s32[1,48,16,2]{1,3,2,0:T(2,128)}, u32[]{:S(2)}) copy-start(s32[1,48,16,2]{1,3,2,0:T(2,128)} %param.10) | copy-start | bytes 18436
  93.1 18.9 %all-to-all-start.1 = ((f32[16,16,384]{2,1,0:T(8,128)}), f32[16,16,384]{2,1,0:T(8,128)S(1)}, u32[]{:S(2)}, u32[]{:S(2)}) async-start(f32[16,16,384]{2,1,0:T(8,128)} %bitcast.15), calls=%async_computation.1 | async-start | bytes 786432 | tf_op jit(solution)/shard_map/all_to_all | solution.py:20
  131.4 15.1 %all-to-all-start.3 = ((bf16[16,2,16,384]{3,2,1,0:T(8,128)(2,1)}), bf16[16,2,16,384]{3,2,1,0:T(8,128)(2,1)S(1)}, u32[]{:S(2)}, u32[]{:S(2)}) async-start(bf16[16,2,16,384]{3,2,1,0:T(8,128)(2,1)} %broadcast_in_dim.61), calls=%async_computation.3 | async-start | bytes 786432 | tf_op jit(solution)/shard_map/all_to_all | solution.py:20
  146.5 9.4 %collective-permute-start.10 = (bf16[16,2,16,384]{3,2,1,0:T(8,128)(2,1)S(1)}, bf16[16,2,16,384]{3,2,1,0:T(8,128)(2,1)S(1)}, u32[]{:S(2)}, u32[]{:S(2)}) collective-permute-start(bf16[16,2,16,384]{3,2,1,0:T(8,128)(2,1)S(1)} %all-to-all-done.3), channel_id=1, source_target_pairs={{0,1},{1,0},{2,3},{3,2},{4,5},{5,4},{6,7},{7,6},{8,9},{9,8},{10,11... | collective-permute-start | bytes 1179656 | tf_op jit(solution)/shard_map/ppermute | solution.py:16
  163.9 2.7 %copy-start.1 = (bf16[512,8,48]{0,2,1:T(8,128)(2,1)S(1)}, bf16[512,8,48]{0,2,1:T(8,128)(2,1)}, u32[]{:S(2)}) copy-start(bf16[512,8,48]{0,2,1:T(8,128)(2,1)} %copy.58) | copy-start | bytes 1179652
  167.7 1.4 copy-start.3
  171.0 6.2 %collective-permute-start.11 = (bf16[1024,1024]{1,0:T(8,128)(2,1)S(1)}, bf16[1024,1024]{1,0:T(8,128)(2,1)S(1)}, u32[]{:S(2)}, u32[]{:S(2)}) collective-permute-start(bf16[1024,1024]{1,0:T(8,128)(2,1)S(1)} %fusion.8), channel_id=1, source_target_pairs={{0,1},{1,0},{2,3},{3,2},{4,5},{5,4},{6,7},{7,6},{8,9},{9,8},{10,11... | collective-permute-start | bytes 6291464 | tf_op jit(solution)/shard_map/ppermute | solution.py:16
Sparse Core Ops, SparseCore 0:
  38.8 45.2 all-gather.2

commit v3 on v2

v3 whole, which is shorter than its diff:
```python
import jax
import jax.numpy as jnp
from jax import lax
from jax.experimental import pallas as pl
from jax.experimental.pallas import tpu as pltpu
from jax.sharding import Mesh, PartitionSpec as P

PIECE = 128
NAMES = ("yh", "z", "x", "yl", "core")
SIZES = (2, 8, 4, 4, 2)
ORIENT = ("yh", "z")
SLAB = ("x", "yl", "core")
bf16 = jnp.bfloat16
f32 = jnp.float32


def swapped(value, axis):
    return lax.ppermute(value, axis, [(0, 1), (1, 0)])


def exchanged(value, axis):
    return lax.all_to_all(value, axis, 0, 0, tiled=True)


def shared(value, axis, count):
    return exchanged(jnp.broadcast_to(value[None], (count,) + value.shape), axis)


def turned(block, step):
    count = 8
    return lax.ppermute(block, "z", [(i, (i + step) % count) for i in range(count)])


def ring_gathered(block):
    count = 8
    z = lax.axis_index("z")
    held = jnp.zeros((count,) + block.shape, block.dtype)
    held = lax.dynamic_update_index_in_dim(held, block, z, 0)
    up = down = block
    for step in range(1, count // 2 + 1):
        up = turned(up, 1)
        held = lax.dynamic_update_index_in_dim(held, up, (z - step) % count, 0)
        if step < count // 2:
            down = turned(down, -1)
            held = lax.dynamic_update_index_in_dim(held, down, (z + step) % count, 0)
    return held


def kernel_params():
    return pltpu.CompilerParams(vmem_limit_bytes=40 * 2**20)


def score_kernel(core_ref, image_ref, weighted_ref, penalty_ref, far_ref, near_ref):
    side = far_ref.shape[0]
    core = core_ref[0]
    for out_ref, at in ((far_ref, 1 - core), (near_ref, core)):
        rows = image_ref[pl.ds(pl.multiple_of(at * side, side), side), :]
        out_ref[...] = (
            lax.dot_general(
                rows, weighted_ref[...], (((1,), (1,)), ((), ())), preferred_element_type=f32
            )
            + penalty_ref[...]
        )


def scored(core, stored, weighted, penalty):
    rows, pixels = stored.shape
    columns = weighted.shape[0]
    side = jax.ShapeDtypeStruct((rows // 2, columns), f32)
    whole = pl.BlockSpec(memory_space=pltpu.VMEM)
    return pl.pallas_call(
        score_kernel,
        out_shape=(side, side),
        in_specs=[pl.BlockSpec(memory_space=pltpu.SMEM), whole, whole, whole],
        out_specs=(whole, whole),
        compiler_params=kernel_params(),
        cost_estimate=pl.CostEstimate(
            flops=2 * rows * pixels * columns,
            bytes_accessed=2 * pixels * (rows + columns) + 4 * rows * columns,
            transcendentals=0,
        ),
    )(core, stored, weighted, penalty)


def spots(slot_ref, start, count):
    at = start + lax.broadcasted_iota(jnp.int32, (count, slot_ref.shape[1]), 0)
    return jnp.where(at == slot_ref[...], 1.0, 0.0).astype(bf16)


def slice_kernel(
    core_ref, mine_ref, twin_ref, own_ref, other_ref, slot_ref, pieces_ref, away_ref, turned_ref
):
    step = pl.program_id(0)
    columns, rows = turned_ref.shape
    part = rows // 4
    per_class = pieces_ref.shape[0] // 16
    classes = columns // per_class

    @pl.when(step == 0)
    def _():
        for plane in range(2):
            for core in range(2):
                mine = mine_ref[:, plane].reshape(part, columns)
                twin = twin_ref[:, plane].reshape(part, columns)
                block = jnp.where(core_ref[0] == core, mine.astype(f32), twin.astype(f32))
                at = (2 * plane + core) * part
                turned_ref[:, at : at + part] = block.T.astype(bf16)

    slices = jnp.dot(
        turned_ref[:, : 2 * part], own_ref[...], preferred_element_type=f32
    ) + jnp.dot(turned_ref[:, 2 * part :], other_ref[...], preferred_element_type=f32)
    slices = slices.astype(bf16)
    many = slices.shape[1] // PIECE
    for p in range(many):
        to = pl.ds(pl.multiple_of((step * many + p) * per_class, 16), per_class)
        for k in range(classes):
            pieces_ref[to, k * PIECE : (k + 1) * PIECE] = slices[
                k * per_class : (k + 1) * per_class, p * PIECE : (p + 1) * PIECE
            ]

    @pl.when(step == pl.num_programs(0) - 1)
    def _():
        slots = away_ref.shape[0]
        for r in range(0, slots, 256):
            away_ref[r : r + 256, :] = jnp.dot(
                spots(slot_ref, slots + r, 256), pieces_ref[...], preferred_element_type=f32
            ).astype(bf16)


def sliced(core, mine, twin, own_plane, other_plane, slot, slots):
    columns = mine.shape[3]
    rows, pixels = own_plane.shape
    pieces = slot.shape[1]
    width = columns * pixels // pieces
    steps = 4
    wide = pixels // steps
    fixed = lambda rank: lambda i: (0,) * rank
    shard = pl.BlockSpec(mine.shape, fixed(4))
    band = pl.BlockSpec((rows, wide), lambda i: (0, i))
    return pl.pallas_call(
        slice_kernel,
        grid=(steps,),
        out_shape=(
            jax.ShapeDtypeStruct((pieces, width), bf16),
            jax.ShapeDtypeStruct((slots, width), bf16),
        ),
        in_specs=[
            pl.BlockSpec(memory_space=pltpu.SMEM),
            shard,
            shard,
            band,
            band,
            pl.BlockSpec(slot.shape, fixed(2)),
        ],
        out_specs=(
            pl.BlockSpec((pieces, width), fixed(2)),
            pl.BlockSpec((slots, width), fixed(2)),
        ),
        scratch_shapes=[pltpu.VMEM((columns, 2 * rows), bf16)],
        compiler_params=kernel_params(),
        cost_estimate=pl.CostEstimate(
            flops=4 * rows * pixels * columns + 2 * slots * pieces * width,
            bytes_accessed=4 * rows * pixels + 2 * width * (pieces + slots),
            transcendentals=0,
        ),
    )(core, mine, twin, own_plane, other_plane, slot)


def near_kernel(slot_ref, pieces_ref, got_ref, sum_ref):
    count = sum_ref.shape[0]
    near = jnp.dot(
        spots(slot_ref, pl.program_id(0) * count, count),
        pieces_ref[...],
        preferred_element_type=f32,
    )
    sum_ref[...] = (near + got_ref[...].astype(f32)).astype(bf16)


def near_summed(slot, pieces, got):
    slots, width = got.shape
    steps = 4
    band = pl.BlockSpec((slots // steps, width), lambda i: (i, 0))
    return pl.pallas_call(
        near_kernel,
        grid=(steps,),
        out_shape=jax.ShapeDtypeStruct(got.shape, bf16),
        in_specs=[
            pl.BlockSpec(slot.shape, lambda i: (0, 0)),
            pl.BlockSpec(pieces.shape, lambda i: (0, 0)),
            band,
        ],
        out_specs=band,
        compiler_params=kernel_params(),
        cost_estimate=pl.CostEstimate(
            flops=2 * slots * pieces.shape[0] * width,
            bytes_accessed=2 * width * (pieces.shape[0] + 2 * slots),
            transcendentals=0,
        ),
    )(slot, pieces, got)


def local(images, projections, noise_weight, prior_score, routing, insert_kernel):
    classes, orient_local, pixels = projections.shape
    columns = classes * orient_local
    rows = images.shape[0]
    orients, slabs, half = 16, 32, 16
    plane_rows = rows * orients // 2
    share = plane_rows // slabs
    blocks = pixels // PIECE
    pieces = orient_local * blocks
    voxels = insert_kernel.shape[1] * orients
    core = lax.axis_index("core")
    upper = lax.axis_index("yh") == 1
    core_one = core.reshape(1)

    where = routing[0].transpose(1, 0, 2)
    owner = where[:, :, 0].reshape(1, pieces)
    voxel = where[:, :, 1].reshape(1, pieces)
    slot = (((owner % 2) ^ core) * half + owner // 2) * voxels + voxel

    other = swapped(images, "yh")
    own_plane = lax.all_gather(images, "z", axis=0).reshape(plane_rows, pixels)
    other_plane = ring_gathered(other).reshape(plane_rows, pixels)

    widened = projections.astype(f32)
    product = widened * noise_weight[None, None, :]
    weighted = product.astype(bf16).reshape(columns, pixels)
    penalty = (-0.5 * jnp.sum(widened * product, axis=2)).reshape(1, columns)
    prior = prior_score.reshape(columns)

    def plane_scores(stored):
        far, near = scored(core_one, stored, weighted, penalty)
        return (near + swapped(far, "core")).reshape(half, share, columns)

    summed = jnp.concatenate([plane_scores(own_plane), plane_scores(other_plane)], axis=1)
    scores = jnp.sum(exchanged(summed, ("x", "yl")), axis=0) + prior[None, :]
    scores = scores.reshape(2, share, columns)
    peak = jnp.max(scores, axis=2)
    mass = jnp.sum(jnp.exp(scores - peak[:, :, None]), axis=2)
    stats = jnp.stack([peak, mass])
    stats = jnp.where(upper, stats[:, ::-1], stats)
    stats = shared(stats.reshape(2, 2 * share), ORIENT, orients)
    top = jnp.max(stats[:, 0], axis=0)
    total = top + jnp.log(jnp.sum(stats[:, 1] * jnp.exp(stats[:, 0] - top[None]), axis=0))
    total = total.reshape(2, share)
    total = jnp.where(upper, total[::-1], total)
    own_weights = jnp.exp(scores - total[:, :, None]).astype(bf16)
    mine = shared(own_weights, ("x", "yl"), half)
    twin = swapped(mine, "core")

    cut, away = sliced(core_one, mine, twin, own_plane, other_plane, slot, half * voxels)
    summed = near_summed(slot, cut, swapped(away, "core"))
    width = classes * PIECE
    summed = exchanged(summed.reshape(4, 4 * voxels, width), "x")
    summed = jnp.sum(summed.astype(f32), axis=0).astype(bf16)
    summed = exchanged(summed.reshape(4 * orients, voxels // orients, width), ("yl", "yh", "z"))
    own_blocks = jnp.sum(summed.astype(f32), axis=0)
    rounded = own_blocks.astype(bf16).reshape(own_blocks.shape[0], classes, PIECE)
    volume = jnp.einsum("vkc,vce->vke", rounded, insert_kernel[0], preferred_element_type=f32)
    return volume[None]


def solution(mesh):
    fine = Mesh(mesh.devices.reshape(SIZES), NAMES)
    return jax.shard_map(
        local,
        mesh=fine,
        in_specs=(
            P(ORIENT, SLAB),
            P(None, ORIENT, SLAB),
            P(SLAB),
            P(None, ORIENT),
            P(SLAB, ORIENT, None, None),
            P(SLAB, ORIENT, None, None),
        ),
        out_specs=P(SLAB, ORIENT, None, None),
        check_vma=False,
    )
```

time: 243 us -> 241 us (level)
  blocking collectives: 70 us -> 86.2 us
  local copies, waits for them, and re-layouts: 18.6 us -> 5.94 us
  waiting for transfers between devices: 49.9 us -> 62.3 us
  matrix products: 12.6 us -> 0.75 us
  starting transfers between devices: 66.8 us -> 55.6 us
  Pallas kernels: 0 us -> 9.84 us
  other arithmetic: 7.83 us -> 4.25 us
    all_to_all x3 -> x4, blocking collectives: 70 us -> 86.2 us  [exchanged(): return lax.all_to_all(value, axis, 0, 0, tiled=True)]
    dot_general x6 -> x0, matrix products: 11.8 us -> none  [the longest x2 4.43 us: plane_scores(): lax.dot_general(stored, weighted, (((1,), (1,)), ((), ())), preferred_ele...]
    all_to_all x3 -> x1, starting transfers between devices: 21.7 us -> 10.7 us  [exchanged(): return lax.all_to_all(value, axis, 0, 0, tiled=True)]
    ppermute x7, waiting for transfers between devices: 18.1 us -> 29.1 us  [turned(): lax.ppermute(block, 'z', [(i, (i + step) % count) for i in range(count)])]
    pallas_call x0 -> x4, Pallas kernels: none -> 9.84 us  [the longest x1 4.96 us: sliced(): pl.pallas_call(slice_kernel, grid=(steps,), out_shape=(jax.ShapeDtypeStru...]
    squeeze x4 -> x0, local copies, waits for them, and re-layouts: 6.85 us -> none  [the longest x2 3.43 us: local(): both[1]]
    ppermute x5, waiting for transfers between devices: 7.36 us -> 12.8 us  [swapped(): return lax.ppermute(value, axis, [(0, 1), (1, 0)])]
    all_gather x1 -> x0, local copies, waits for them, and re-layouts: 2.86 us -> none  [local(): other_plane = lax.all_gather(other, 'z', axis=0).reshape(plane_rows, pixels)]
  transfers between devices with their start and end apart: 16 -> 14, of which waited for: 10 -> 9; matrix products, arithmetic and copies ran while one was open for 8% -> 1% of each run, Pallas kernels for 0% -> 1%
where the time goes in v3:
time: 241 us; the launch traced here: 239 us
  blocking collectives  86.2 us (36%)
  waiting for transfers between devices  62.3 us (26%)
  starting transfers between devices  55.6 us (23%)
  between operations  13.8 us (6%)
  Pallas kernels  9.84 us (4%)
  local copies, waits for them, and re-layouts  5.94 us (2%)
  other arithmetic  4.25 us (2%)
    all_to_all x4, blocking collectives, exchanged(): return lax.all_to_all(value, axis, 0, 0, tiled=True)  86.2 us
    ppermute x7, waiting for transfers between devices, turned(): lax.ppermute(block, 'z', [(i, (i + step) % count) for i in range(count)])  29.1 us
    ppermute x7, starting transfers between devices, turned(): lax.ppermute(block, 'z', [(i, (i + step) % count) for i in range(count)])  28.8 us
    all_to_all x1, waiting for transfers between devices, exchanged(): return lax.all_to_all(value, axis, 0, 0, tiled=True)  20.3 us
    ppermute x5, starting transfers between devices, swapped(): return lax.ppermute(value, axis, [(0, 1), (1, 0)])  16.1 us
    ppermute x5, waiting for transfers between devices, swapped(): return lax.ppermute(value, axis, [(0, 1), (1, 0)])  12.8 us
    all_to_all x1, starting transfers between devices, exchanged(): return lax.all_to_all(value, axis, 0, 0, tiled=True)  10.7 us
    pallas_call x1, Pallas kernels, sliced(): pl.pallas_call(slice_kernel, grid=(steps,), out_shape=(jax.ShapeDtypeStru...  4.96 us
  transfers between devices with their start and end apart: 14, of which 9 were waited for; matrix products, arithmetic and copies ran while one was open for 1% of the time, Pallas kernels for 1%

profile of v3, /device:TPU:6, one launch (start us, length us, event | category | flops | bytes accessed | tf_op | source)
XLA Modules:
  0.0 238.8 jit_solution(12145705053313402303)
XLA Ops:
  6.5 7.9 %collective-permute-start.1 = (bf16[64,2048]{1,0:T(8,128)(2,1)}, bf16[64,2048]{1,0:T(8,128)(2,1)S(1)}, u32[]{:S(2)}, u32[]{:S(2)}) collective-permute-start(bf16[64,2048]{1,0:T(8,128)(2,1)} %param.6), channel_id=1, source_target_pairs={{0,256},{256,0},{1,257},{257,1},{2,258},{258,2},{3,259},{259,3},{4... | collective-permute-start | bytes 786440 | tf_op jit(solution)/shard_map/ppermute | solution.py:18
  14.4 1.9 fusion
  16.6 6.1 %collective-permute-done.1 = bf16[64,2048]{1,0:T(8,128)(2,1)S(1)} collective-permute-done((bf16[64,2048]{1,0:T(8,128)(2,1)}, bf16[64,2048]{1,0:T(8,128)(2,1)S(1)}, u32[]{:S(2)}, u32[]{:S(2)}) %collective-permute-start.1) | collective-permute-done | bytes 262176 | tf_op jit(solution)/shard_map/ppermute | solution.py:18
  22.7 4.3 %collective-permute-start.2 = (bf16[64,2048]{1,0:T(8,128)(2,1)S(1)}, bf16[64,2048]{1,0:T(8,128)(2,1)S(1)}, u32[]{:S(2)}, u32[]{:S(2)}) collective-permute-start(bf16[64,2048]{1,0:T(8,128)(2,1)S(1)} %collective-permute-done.1), channel_id=1, source_target_pairs={{0,32},{32,64},{64,96},{96,128},{128,160},{160,192},{192,224},{224... | collective-permute-start | bytes 786440 | tf_op jit(solution)/shard_map/ppermute | solution.py:31
  27.0 8.6 %collective-permute-start.3 = (bf16[64,2048]{1,0:T(8,128)(2,1)S(1)}, bf16[64,2048]{1,0:T(8,128)(2,1)S(1)}, u32[]{:S(2)}, u32[]{:S(2)}) collective-permute-start(bf16[64,2048]{1,0:T(8,128)(2,1)S(1)} %collective-permute-done.1), channel_id=1, source_target_pairs={{0,224},{32,0},{64,32},{96,64},{128,96},{160,128},{192,160},{224,1... | collective-permute-start | bytes 786440 | tf_op jit(solution)/shard_map/ppermute | solution.py:31
  35.9 9.9 %collective-permute-done.2 = bf16[64,2048]{1,0:T(8,128)(2,1)S(1)} collective-permute-done((bf16[64,2048]{1,0:T(8,128)(2,1)S(1)}, bf16[64,2048]{1,0:T(8,128)(2,1)S(1)}, u32[]{:S(2)}, u32[]{:S(2)}) %collective-permute-start.2) | collective-permute-done | bytes 262176 | tf_op jit(solution)/shard_map/ppermute | solution.py:31
  45.7 1.9 collective-permute-start.4
  47.7 5.1 %collective-permute-start.5 = (bf16[64,2048]{1,0:T(8,128)(2,1)S(1)}, bf16[64,2048]{1,0:T(8,128)(2,1)S(1)}, u32[]{:S(2)}, u32[]{:S(2)}) collective-permute-start(bf16[64,2048]{1,0:T(8,128)(2,1)S(1)} %collective-permute-done.3), channel_id=1, source_target_pairs={{0,224},{32,0},{64,32},{96,64},{128,96},{160,128},{192,160},{224,1... | collective-permute-start | bytes 786440 | tf_op jit(solution)/shard_map/ppermute | solution.py:31
  52.9 9.4 %collective-permute-done.4 = bf16[64,2048]{1,0:T(8,128)(2,1)S(1)} collective-permute-done((bf16[64,2048]{1,0:T(8,128)(2,1)S(1)}, bf16[64,2048]{1,0:T(8,128)(2,1)S(1)}, u32[]{:S(2)}, u32[]{:S(2)}) %collective-permute-start.4) | collective-permute-done | bytes 262176 | tf_op jit(solution)/shard_map/ppermute | solution.py:31
  64.2 5.1 %collective-permute-start.7 = (bf16[64,2048]{1,0:T(8,128)(2,1)S(1)}, bf16[64,2048]{1,0:T(8,128)(2,1)S(1)}, u32[]{:S(2)}, u32[]{:S(2)}) collective-permute-start(bf16[64,2048]{1,0:T(8,128)(2,1)S(1)} %collective-permute-done.5), channel_id=1, source_target_pairs={{0,224},{32,0},{64,32},{96,64},{128,96},{160,128},{192,160},{224,1... | collective-permute-start | bytes 786440 | tf_op jit(solution)/shard_map/ppermute | solution.py:31
  69.4 2.3 collective-permute-done.6
  71.7 1.9 collective-permute-start.8
  73.7 7.5 %collective-permute-done.8 = bf16[64,2048]{1,0:T(8,128)(2,1)S(1)} collective-permute-done((bf16[64,2048]{1,0:T(8,128)(2,1)S(1)}, bf16[64,2048]{1,0:T(8,128)(2,1)S(1)}, u32[]{:S(2)}, u32[]{:S(2)}) %collective-permute-start.8) | collective-permute-done | bytes 262176 | tf_op jit(solution)/shard_map/ppermute | solution.py:31
  88.6 2.4 %collective-permute-start = (f32[256,384]{1,0:T(8,128)S(1)}, f32[256,384]{1,0:T(8,128)S(1)}, u32[]{:S(2)}, u32[]{:S(2)}) collective-permute-start(f32[256,384]{1,0:T(8,128)S(1)} %get-tuple-element.12), channel_id=1, source_target_pairs={{0,1},{1,0},{2,3},{3,2},{4,5},{5,4},{6,7},{7,6},{8,9},{9,8},{10,11... | collective-permute-start | bytes 1179656 | tf_op jit(solution)/shard_map/ppermute | solution.py:18
  93.4 10.7 %all-to-all-start = ((f32[16,32,384]{2,1,0:T(8,128)}), f32[16,32,384]{2,1,0:T(8,128)S(1)}, u32[]{:S(2)}, u32[]{:S(2)}) async-start(f32[16,32,384]{2,1,0:T(8,128)} %pad_maximum_fusion), calls=%async_computation | async-start | bytes 1572864 | tf_op jit(solution)/shard_map/all_to_all | solution.py:22
  104.1 20.3 %all-to-all-done = f32[16,32,384]{2,1,0:T(8,128)S(1)} async-done(((f32[16,32,384]{2,1,0:T(8,128)}), f32[16,32,384]{2,1,0:T(8,128)S(1)}, u32[]{:S(2)}, u32[]{:S(2)}) %all-to-all-start) | async-done | bytes 786464 | tf_op jit(solution)/shard_map/all_to_all | solution.py:22
  125.1 18.8 %all_to_all.25 = f32[16,2,32]{2,1,0:T(2,128)S(1)} all-to-all(f32[16,2,32]{2,1,0:T(2,128)S(1)} %broadcast_in_dim.58), channel_id=1, replica_groups=mesh['yh'=2,'z'=8,'x'=4,'yl'=4,'core'=2] {'yh','z'}, dimensions={0} | all-to-all | bytes 8192 | tf_op jit(solution)/shard_map/all_to_all | solution.py:22
  144.3 15.4 %all_to_all.26.mine_ref = bf16[16,2,16,384]{3,2,1,0:T(8,128)(2,1)S(1)} all-to-all(bf16[16,2,16,384]{3,2,1,0:T(8,128)(2,1)S(1)} %broadcast_in_dim.59), channel_id=1, replica_groups=mesh['yh'=2,'z'=8,'x'=4,'yl'=4,'core'=2] {'x','yl'}, dimensions={0} | all-to-all | bytes 786432 | tf_op jit(solution)/shard_map/all_to_all | solution.py:22
  164.9 5.0 %shard_map.66 = (bf16[768,1024]{1,0:T(8,128)(2,1)S(1)}, bf16[1024,1024]{1,0:T(8,128)(2,1)S(1)}) custom-call(s32[1]{0:T(128)} %bitcast.3.core_ref, bf16[16,2,16,384]{3,2,1,0:T(8,128)(2,1)S(1)} %all_to_all.26.mine_ref, bf16[16,2,16,384]{3,2,1,0:T(8,128)(2,1)S(1)} %collective-permute-done.10.twin_ref, bf16[512,2048]{1,0:T(8,128)(2,1)S(1)} %copy-done.4, ...), custom_call_target="tpu_custom_call" | custom-call | flops 3221225472 | bytes 7864320 | tf_op jit(solution)/shard_map/pallas_call | solution.py:140
  169.8 2.0 collective-permute-start.11
  171.9 4.0 %collective-permute-done.11.got_ref = bf16[1024,1024]{1,0:T(8,128)(2,1)S(1)} collective-permute-done((bf16[1024,1024]{1,0:T(8,128)(2,1)S(1)}, bf16[1024,1024]{1,0:T(8,128)(2,1)S(1)}, u32[]{:S(2)}, u32[]{:S(2)}) %collective-permute-start.11) | collective-permute-done | bytes 2097184 | tf_op jit(solution)/shard_map/ppermute | solution.py:18
  175.9 2.4 shard_map.67
  178.3 29.7 %all_to_all.27 = bf16[4,256,1024]{2,1,0:T(8,128)(2,1)S(1)} all-to-all(bf16[4,256,1024]{2,1,0:T(8,128)(2,1)S(1)} %bitcast.43), channel_id=1, replica_groups=mesh['yh'=2,'z'=8,'x'=4,'yl'=4,'core'=2] {'x'}, dimensions={0} | all-to-all | bytes 4194304 | tf_op jit(solution)/shard_map/all_to_all | solution.py:22
  208.6 22.3 %all_to_all.28 = bf16[64,4,1024]{2,1,0:T(4,128)(2,1)S(1)} all-to-all(bf16[64,4,1024]{2,1,0:T(4,128)(2,1)S(1)} %reshape.244), channel_id=1, replica_groups=mesh['yh'=2,'z'=8,'x'=4,'yl'=4,'core'=2] {'yl','yh','z'}, dimensions={0} | all-to-all | bytes 1048576 | tf_op jit(solution)/shard_map/all_to_all | solution.py:22
  (71 shorter events, 20.0 us)
Async XLA Ops:
  6.5 224.6 %copy-start = (bf16[1,4,128,128]{3,2,1,0:T(8,128)(2,1)S(1)}, bf16[1,4,128,128]{3,2,1,0:T(8,128)(2,1)}, u32[]{:S(2)}) copy-start(bf16[1,4,128,128]{3,2,1,0:T(8,128)(2,1)} %param.11) | copy-start | bytes 393220
  6.5 79.2 %all-gather.3.cloned.1.call-start = ((), (), s32[]{:S(2)}) async-start(), calls=%async_computation.5 | async-start | bytes 2359296 | tf_op jit(solution)/shard_map/all_gather | solution.py:222
  6.5 16.2 %collective-permute-start.1 = (bf16[64,2048]{1,0:T(8,128)(2,1)}, bf16[64,2048]{1,0:T(8,128)(2,1)S(1)}, u32[]{:S(2)}, u32[]{:S(2)}) collective-permute-start(bf16[64,2048]{1,0:T(8,128)(2,1)} %param.6), channel_id=1, source_target_pairs={{0,256},{256,0},{1,257},{257,1},{2,258},{258,2},{3,259},{259,3},{4... | collective-permute-start | bytes 786440 | tf_op jit(solution)/shard_map/ppermute | solution.py:18
  22.7 23.0 %collective-permute-start.2 = (bf16[64,2048]{1,0:T(8,128)(2,1)S(1)}, bf16[64,2048]{1,0:T(8,128)(2,1)S(1)}, u32[]{:S(2)}, u32[]{:S(2)}) collective-permute-start(bf16[64,2048]{1,0:T(8,128)(2,1)S(1)} %collective-permute-done.1), channel_id=1, source_target_pairs={{0,32},{32,64},{64,96},{96,128},{128,160},{160,192},{192,224},{224... | collective-permute-start | bytes 786440 | tf_op jit(solution)/shard_map/ppermute | solution.py:31
  27.0 20.7 %collective-permute-start.3 = (bf16[64,2048]{1,0:T(8,128)(2,1)S(1)}, bf16[64,2048]{1,0:T(8,128)(2,1)S(1)}, u32[]{:S(2)}, u32[]{:S(2)}) collective-permute-start(bf16[64,2048]{1,0:T(8,128)(2,1)S(1)} %collective-permute-done.1), channel_id=1, source_target_pairs={{0,224},{32,0},{64,32},{96,64},{128,96},{160,128},{192,160},{224,1... | collective-permute-start | bytes 786440 | tf_op jit(solution)/shard_map/ppermute | solution.py:31
  45.7 16.6 %collective-permute-start.4 = (bf16[64,2048]{1,0:T(8,128)(2,1)S(1)}, bf16[64,2048]{1,0:T(8,128)(2,1)S(1)}, u32[]{:S(2)}, u32[]{:S(2)}) collective-permute-start(bf16[64,2048]{1,0:T(8,128)(2,1)S(1)} %collective-permute-done.2), channel_id=1, source_target_pairs={{0,32},{32,64},{64,96},{96,128},{128,160},{160,192},{192,224},{224... | collective-permute-start | bytes 786440 | tf_op jit(solution)/shard_map/ppermute | solution.py:31
  47.7 16.5 %collective-permute-start.5 = (bf16[64,2048]{1,0:T(8,128)(2,1)S(1)}, bf16[64,2048]{1,0:T(8,128)(2,1)S(1)}, u32[]{:S(2)}, u32[]{:S(2)}) collective-permute-start(bf16[64,2048]{1,0:T(8,128)(2,1)S(1)} %collective-permute-done.3), channel_id=1, source_target_pairs={{0,224},{32,0},{64,32},{96,64},{128,96},{160,128},{192,160},{224,1... | collective-permute-start | bytes 786440 | tf_op jit(solution)/shard_map/ppermute | solution.py:31
  62.3 9.5 %collective-permute-start.6 = (bf16[64,2048]{1,0:T(8,128)(2,1)S(1)}, bf16[64,2048]{1,0:T(8,128)(2,1)S(1)}, u32[]{:S(2)}, u32[]{:S(2)}) collective-permute-start(bf16[64,2048]{1,0:T(8,128)(2,1)S(1)} %collective-permute-done.4), channel_id=1, source_target_pairs={{0,32},{32,64},{64,96},{96,128},{128,160},{160,192},{192,224},{224... | collective-permute-start | bytes 786440 | tf_op jit(solution)/shard_map/ppermute | solution.py:31
  64.2 9.5 %collective-permute-start.7 = (bf16[64,2048]{1,0:T(8,128)(2,1)S(1)}, bf16[64,2048]{1,0:T(8,128)(2,1)S(1)}, u32[]{:S(2)}, u32[]{:S(2)}) collective-permute-start(bf16[64,2048]{1,0:T(8,128)(2,1)S(1)} %collective-permute-done.5), channel_id=1, source_target_pairs={{0,224},{32,0},{64,32},{96,64},{128,96},{160,128},{192,160},{224,1... | collective-permute-start | bytes 786440 | tf_op jit(solution)/shard_map/ppermute | solution.py:31
  71.7 9.5 %collective-permute-start.8 = (bf16[64,2048]{1,0:T(8,128)(2,1)S(1)}, bf16[64,2048]{1,0:T(8,128)(2,1)S(1)}, u32[]{:S(2)}, u32[]{:S(2)}) collective-permute-start(bf16[64,2048]{1,0:T(8,128)(2,1)S(1)} %collective-permute-done.6), channel_id=1, source_target_pairs={{0,32},{32,64},{64,96},{96,128},{128,160},{160,192},{192,224},{224... | collective-permute-start | bytes 786440 | tf_op jit(solution)/shard_map/ppermute | solution.py:31
  82.5 1.3 copy-start.1
  83.8 7.2 %collective-permute-start.9 = (f32[256,384]{1,0:T(8,128)S(1)}, f32[256,384]{1,0:T(8,128)S(1)}, u32[]{:S(2)}, u32[]{:S(2)}) collective-permute-start(f32[256,384]{1,0:T(8,128)S(1)} %get-tuple-element.14), channel_id=1, source_target_pairs={{0,1},{1,0},{2,3},{3,2},{4,5},{5,4},{6,7},{7,6},{8,9},{9,8},{10,11... | collective-permute-start | bytes 1179656 | tf_op jit(solution)/shard_map/ppermute | solution.py:18
  85.8 1.6 copy-start.3
  88.6 3.7 %collective-permute-start = (f32[256,384]{1,0:T(8,128)S(1)}, f32[256,384]{1,0:T(8,128)S(1)}, u32[]{:S(2)}, u32[]{:S(2)}) collective-permute-start(f32[256,384]{1,0:T(8,128)S(1)} %get-tuple-element.12), channel_id=1, source_target_pairs={{0,1},{1,0},{2,3},{3,2},{4,5},{5,4},{6,7},{7,6},{8,9},{9,8},{10,11... | collective-permute-start | bytes 1179656 | tf_op jit(solution)/shard_map/ppermute | solution.py:18
  92.3 11.7 %copy-start.6 = (f32[8,48]{1,0:T(8,128)S(1)}, f32[8,48]{1,0:T(8,128)}, u32[]{:S(2)}) copy-start(f32[8,48]{1,0:T(8,128)} %param.9) | copy-start | bytes 4612
  93.4 68.2 %copy-start.5 = (s32[1,48,16,2]{1,3,2,0:T(2,128)S(1)}, s32[1,48,16,2]{1,3,2,0:T(2,128)}, u32[]{:S(2)}) copy-start(s32[1,48,16,2]{1,3,2,0:T(2,128)} %param.10) | copy-start | bytes 18436
  93.4 69.9 %copy-start.2 = (bf16[8,64,2048]{2,1,0:T(8,128)(2,1)S(1)}, bf16[8,64,2048]{2,1,0:T(8,128)(2,1)}, u32[]{:S(2)}) copy-start(bf16[8,64,2048]{2,1,0:T(8,128)(2,1)} %copy-done.1) | copy-start | bytes 6291460
  93.4 31.1 %all-to-all-start = ((f32[16,32,384]{2,1,0:T(8,128)}), f32[16,32,384]{2,1,0:T(8,128)S(1)}, u32[]{:S(2)}, u32[]{:S(2)}) async-start(f32[16,32,384]{2,1,0:T(8,128)} %pad_maximum_fusion), calls=%async_computation | async-start | bytes 1572864 | tf_op jit(solution)/shard_map/all_to_all | solution.py:22
  159.7 3.6 %collective-permute-start.10 = (bf16[16,2,16,384]{3,2,1,0:T(8,128)(2,1)S(1)}, bf16[16,2,16,384]{3,2,1,0:T(8,128)(2,1)S(1)}, u32[]{:S(2)}, u32[]{:S(2)}) collective-permute-start(bf16[16,2,16,384]{3,2,1,0:T(8,128)(2,1)S(1)} %all_to_all.26.mine_ref), channel_id=1, source_target_pairs={{0,1},{1,0},{2,3},{3,2},{4,5},{5,4},{6,7},{7,6},{8,9},{9,8},{10,11... | collective-permute-start | bytes 1179656 | tf_op jit(solution)/shard_map/ppermute | solution.py:18
  163.3 1.6 copy-start.4
  169.8 6.1 %collective-permute-start.11 = (bf16[1024,1024]{1,0:T(8,128)(2,1)S(1)}, bf16[1024,1024]{1,0:T(8,128)(2,1)S(1)}, u32[]{:S(2)}, u32[]{:S(2)}) collective-permute-start(bf16[1024,1024]{1,0:T(8,128)(2,1)S(1)} %get-tuple-element.16), channel_id=1, source_target_pairs={{0,1},{1,0},{2,3},{3,2},{4,5},{5,4},{6,7},{7,6},{8,9},{9,8},{10,11... | collective-permute-start | bytes 6291464 | tf_op jit(solution)/shard_map/ppermute | solution.py:18
Sparse Core Ops, SparseCore 0:
  14.5 50.8 all-gather.2

commit v4 on v3

--- a/solution.py
+++ b/solution.py
@@ -1,3 +1,5 @@
+import functools
+
 import jax
 import jax.numpy as jnp
 from jax import lax
@@ -26,9 +28,8 @@
     return exchanged(jnp.broadcast_to(value[None], (count,) + value.shape), axis)
 
 
-def turned(block, step):
-    count = 8
-    return lax.ppermute(block, "z", [(i, (i + step) % count) for i in range(count)])
+def turned(block, step, axis="z", count=8):
+    return lax.ppermute(block, axis, [(i, (i + step) % count) for i in range(count)])
 
 
 def ring_gathered(block):
@@ -47,7 +48,7 @@
 
 
 def kernel_params():
-    return pltpu.CompilerParams(vmem_limit_bytes=40 * 2**20)
+    return pltpu.CompilerParams(vmem_limit_bytes=24 * 2**20)
 
 
 def score_kernel(core_ref, image_ref, weighted_ref, penalty_ref, far_ref, near_ref):
@@ -88,7 +89,7 @@
 
 
 def slice_kernel(
-    core_ref, mine_ref, twin_ref, own_ref, other_ref, slot_ref, pieces_ref, away_ref, turned_ref
+    core_ref, mine_ref, twin_ref, other_ref, own_ref, slot_ref, pieces_ref, away_ref, turned_ref
 ):
     step = pl.program_id(0)
     columns, rows = turned_ref.shape
@@ -107,8 +108,8 @@
                 turned_ref[:, at : at + part] = block.T.astype(bf16)
 
     slices = jnp.dot(
-        turned_ref[:, : 2 * part], own_ref[...], preferred_element_type=f32
-    ) + jnp.dot(turned_ref[:, 2 * part :], other_ref[...], preferred_element_type=f32)
+        turned_ref[:, : 2 * part], other_ref[...], preferred_element_type=f32
+    ) + jnp.dot(turned_ref[:, 2 * part :], own_ref[...], preferred_element_type=f32)
     slices = slices.astype(bf16)
     many = slices.shape[1] // PIECE
     for p in range(many):
@@ -127,9 +128,9 @@
             ).astype(bf16)
 
 
-def sliced(core, mine, twin, own_plane, other_plane, slot, slots):
+def sliced(core, mine, twin, other_plane, own_plane, slot, slots):
     columns = mine.shape[3]
-    rows, pixels = own_plane.shape
+    rows, pixels = other_plane.shape
     pieces = slot.shape[1]
     width = columns * pixels // pieces
     steps = 4
@@ -163,37 +164,30 @@
             bytes_accessed=4 * rows * pixels + 2 * width * (pieces + slots),
             transcendentals=0,
         ),
-    )(core, mine, twin, own_plane, other_plane, slot)
-
-
-def near_kernel(slot_ref, pieces_ref, got_ref, sum_ref):
+    )(core, mine, twin, other_plane, own_plane, slot)
+
+
+def near_kernel(start, slot_ref, pieces_ref, got_ref, sum_ref):
     count = sum_ref.shape[0]
     near = jnp.dot(
-        spots(slot_ref, pl.program_id(0) * count, count),
-        pieces_ref[...],
-        preferred_element_type=f32,
+        spots(slot_ref, start, count), pieces_ref[...], preferred_element_type=f32
     )
-    sum_ref[...] = (near + got_ref[...].astype(f32)).astype(bf16)
-
-
-def near_summed(slot, pieces, got):
+    sum_ref[...] = (near + got_ref[start : start + count, :].astype(f32)).astype(sum_ref.dtype)
+
+
+def near_summed(slot, pieces, got, part, dtype):
     slots, width = got.shape
-    steps = 4
-    band = pl.BlockSpec((slots // steps, width), lambda i: (i, 0))
+    count = slots // 4
+    whole = pl.BlockSpec(memory_space=pltpu.VMEM)
     return pl.pallas_call(
-        near_kernel,
-        grid=(steps,),
-        out_shape=jax.ShapeDtypeStruct(got.shape, bf16),
-        in_specs=[
-            pl.BlockSpec(slot.shape, lambda i: (0, 0)),
-            pl.BlockSpec(pieces.shape, lambda i: (0, 0)),
-            band,
-        ],
-        out_specs=band,
+        functools.partial(near_kernel, part * count),
+        out_shape=jax.ShapeDtypeStruct((count, width), dtype),
+        in_specs=[whole] * 3,
+        out_specs=whole,
         compiler_params=kernel_params(),
         cost_estimate=pl.CostEstimate(
-            flops=2 * slots * pieces.shape[0] * width,
-            bytes_accessed=2 * width * (pieces.shape[0] + 2 * slots),
+            flops=2 * count * pieces.shape[0] * width,
+            bytes_accessed=2 * width * (pieces.shape[0] + 2 * count),
             transcendentals=0,
         ),
     )(slot, pieces, got)
@@ -210,17 +204,18 @@
     pieces = orient_local * blocks
     voxels = insert_kernel.shape[1] * orients
     core = lax.axis_index("core")
-    upper = lax.axis_index("yh") == 1
+    upper = lax.axis_index("yh") == 0
     core_one = core.reshape(1)
 
     where = routing[0].transpose(1, 0, 2)
     owner = where[:, :, 0].reshape(1, pieces)
     voxel = where[:, :, 1].reshape(1, pieces)
-    slot = (((owner % 2) ^ core) * half + owner // 2) * voxels + voxel
+    ahead = (owner // 8 + 4 - lax.axis_index("x")) % 4
+    slot = ((((owner % 2) ^ core) * 4 + ahead) * 4 + owner // 2 % 4) * voxels + voxel
 
     other = swapped(images, "yh")
-    own_plane = lax.all_gather(images, "z", axis=0).reshape(plane_rows, pixels)
-    other_plane = ring_gathered(other).reshape(plane_rows, pixels)
+    other_plane = lax.all_gather(other, "z", axis=0).reshape(plane_rows, pixels)
+    own_plane = ring_gathered(images).reshape(plane_rows, pixels)
 
     widened = projections.astype(f32)
     product = widened * noise_weight[None, None, :]
@@ -230,11 +225,10 @@
 
     def plane_scores(stored):
         far, near = scored(core_one, stored, weighted, penalty)
-        return (near + swapped(far, "core")).reshape(half, share, columns)
-
-    summed = jnp.concatenate([plane_scores(own_plane), plane_scores(other_plane)], axis=1)
-    scores = jnp.sum(exchanged(summed, ("x", "yl")), axis=0) + prior[None, :]
-    scores = scores.reshape(2, share, columns)
+        summed = (near + swapped(far, "core")).reshape(half, share, columns)
+        return jnp.sum(exchanged(summed, ("x", "yl")), axis=0) + prior[None, :]
+
+    scores = jnp.stack([plane_scores(other_plane), plane_scores(own_plane)])
     peak = jnp.max(scores, axis=2)
     mass = jnp.sum(jnp.exp(scores - peak[:, :, None]), axis=2)
     stats = jnp.stack([peak, mass])
@@ -248,11 +242,14 @@
     mine = shared(own_weights, ("x", "yl"), half)
     twin = swapped(mine, "core")
 
-    cut, away = sliced(core_one, mine, twin, own_plane, other_plane, slot, half * voxels)
-    summed = near_summed(slot, cut, swapped(away, "core"))
+    cut, away = sliced(core_one, mine, twin, other_plane, own_plane, slot, half * voxels)
+    got = swapped(away, "core")
     width = classes * PIECE
-    summed = exchanged(summed.reshape(4, 4 * voxels, width), "x")
-    summed = jnp.sum(summed.astype(f32), axis=0).astype(bf16)
+    summed = near_summed(slot, cut, got, 0, f32)
+    for part in (2, 1, 3):
+        sent = near_summed(slot, cut, got, part, bf16)
+        summed = summed + turned(sent, part, "x", 4).astype(f32)
+    summed = summed.astype(bf16)
     summed = exchanged(summed.reshape(4 * orients, voxels // orients, width), ("yl", "yh", "z"))
     own_blocks = jnp.sum(summed.astype(f32), axis=0)
     rounded = own_blocks.astype(bf16).reshape(own_blocks.shape[0], classes, PIECE)

time: 241 us -> 225 us (0.934)
  blocking collectives: 86.2 us -> 55.3 us
  starting transfers between devices: 55.6 us -> 67.9 us
  waiting for transfers between devices: 62.3 us -> 56.4 us
  local copies, waits for them, and re-layouts: 5.94 us -> 10.5 us
  Pallas kernels: 9.84 us -> 12.7 us
    all_to_all x4 -> x3, blocking collectives: 86.2 us -> 55.3 us  [exchanged(): return lax.all_to_all(value, axis, 0, 0, tiled=True)]
    ppermute x7 -> x10, starting transfers between devices: 28.8 us -> 38 us  [turned(): lax.ppermute(block, axis, [(i, (i + step) % count) for i in range(count)])]
    all_to_all x1 -> x2, waiting for transfers between devices: 20.3 us -> 14.3 us  [exchanged(): return lax.all_to_all(value, axis, 0, 0, tiled=True)]
    ppermute x5, waiting for transfers between devices: 12.8 us -> 8.75 us  [swapped(): return lax.ppermute(value, axis, [(0, 1), (1, 0)])]
    all_to_all x1 -> x2, starting transfers between devices: 10.7 us -> 14.4 us  [exchanged(): return lax.all_to_all(value, axis, 0, 0, tiled=True)]
    ppermute x7 -> x10, waiting for transfers between devices: 29.1 us -> 32.6 us  [turned(): lax.ppermute(block, axis, [(i, (i + step) % count) for i in range(count)])]
    dynamic_update_slice x4, local copies, waits for them, and re-layouts: 0.09 us -> 2.87 us  [ring_gathered(): held = lax.dynamic_update_index_in_dim(held, up, (z - step) % count, 0)]
  transfers between devices with their start and end apart: 14 -> 18, of which waited for: 9 -> 14; matrix products, arithmetic and copies ran while one was open for 1% -> 5% of each run, Pallas kernels for 1% -> 3%
where the time goes in v4:
time: 225 us; the launch traced here: 222 us
  starting transfers between devices  67.9 us (30%)
  waiting for transfers between devices  56.4 us (25%)
  blocking collectives  55.3 us (25%)
  between operations  13.8 us (6%)
  Pallas kernels  12.7 us (6%)
  local copies, waits for them, and re-layouts  10.5 us (5%)
  other arithmetic  4.76 us (2%)
    all_to_all x3, blocking collectives, exchanged(): return lax.all_to_all(value, axis, 0, 0, tiled=True)  55.3 us
    ppermute x10, starting transfers between devices, turned(): lax.ppermute(block, axis, [(i, (i + step) % count) for i in range(count)])  38 us
    ppermute x10, waiting for transfers between devices, turned(): lax.ppermute(block, axis, [(i, (i + step) % count) for i in range(count)])  32.6 us
    ppermute x5, starting transfers between devices, swapped(): return lax.ppermute(value, axis, [(0, 1), (1, 0)])  15.5 us
    all_to_all x2, starting transfers between devices, exchanged(): return lax.all_to_all(value, axis, 0, 0, tiled=True)  14.4 us
    all_to_all x2, waiting for transfers between devices, exchanged(): return lax.all_to_all(value, axis, 0, 0, tiled=True)  14.3 us
    ppermute x5, waiting for transfers between devices, swapped(): return lax.ppermute(value, axis, [(0, 1), (1, 0)])  8.75 us
    pallas_call x1, Pallas kernels, sliced(): pl.pallas_call(slice_kernel, grid=(steps,), out_shape=(jax.ShapeDtypeStru...  6.25 us
  transfers between devices with their start and end apart: 18, of which 14 were waited for; matrix products, arithmetic and copies ran while one was open for 5% of the time, Pallas kernels for 3%

profile of v4, /device:TPU:6, one launch (start us, length us, event | category | flops | bytes accessed | tf_op | source)
XLA Modules:
  0.0 222.2 jit_solution(8460425517953421348)
XLA Ops:
  6.5 4.4 %collective-permute-start.2 = (bf16[64,2048]{1,0:T(8,128)(2,1)}, bf16[64,2048]{1,0:T(8,128)(2,1)S(1)}, u32[]{:S(2)}, u32[]{:S(2)}) collective-permute-start(bf16[64,2048]{1,0:T(8,128)(2,1)} %param.6), channel_id=1, source_target_pairs={{0,32},{32,64},{64,96},{96,128},{128,160},{160,192},{192,224},{224... | collective-permute-start | bytes 786440 | tf_op jit(solution)/shard_map/ppermute | solution.py:32
  10.9 8.6 %collective-permute-start.3 = (bf16[64,2048]{1,0:T(8,128)(2,1)}, bf16[64,2048]{1,0:T(8,128)(2,1)S(1)}, u32[]{:S(2)}, u32[]{:S(2)}) collective-permute-start(bf16[64,2048]{1,0:T(8,128)(2,1)} %param.6), channel_id=1, source_target_pairs={{0,224},{32,0},{64,32},{96,64},{128,96},{160,128},{192,160},{224,1... | collective-permute-start | bytes 786440 | tf_op jit(solution)/shard_map/ppermute | solution.py:32
  19.5 7.7 %collective-permute-start = (bf16[64,2048]{1,0:T(8,128)(2,1)}, bf16[64,2048]{1,0:T(8,128)(2,1)S(1)}, u32[]{:S(2)}, u32[]{:S(2)}) collective-permute-start(bf16[64,2048]{1,0:T(8,128)(2,1)} %param.6), channel_id=1, source_target_pairs={{0,256},{256,0},{1,257},{257,1},{2,258},{258,2},{3,259},{259,3},{4... | collective-permute-start | bytes 786440 | tf_op jit(solution)/shard_map/ppermute | solution.py:20
  27.4 2.0 fusion
  33.7 5.1 %collective-permute-start.5 = (bf16[64,2048]{1,0:T(8,128)(2,1)S(1)}, bf16[64,2048]{1,0:T(8,128)(2,1)S(1)}, u32[]{:S(2)}, u32[]{:S(2)}) collective-permute-start(bf16[64,2048]{1,0:T(8,128)(2,1)S(1)} %collective-permute-done.3), channel_id=1, source_target_pairs={{0,224},{32,0},{64,32},{96,64},{128,96},{160,128},{192,160},{224,1... | collective-permute-start | bytes 786440 | tf_op jit(solution)/shard_map/ppermute | solution.py:32
  44.3 5.1 %collective-permute-start.7 = (bf16[64,2048]{1,0:T(8,128)(2,1)S(1)}, bf16[64,2048]{1,0:T(8,128)(2,1)S(1)}, u32[]{:S(2)}, u32[]{:S(2)}) collective-permute-start(bf16[64,2048]{1,0:T(8,128)(2,1)S(1)} %collective-permute-done.5), channel_id=1, source_target_pairs={{0,224},{32,0},{64,32},{96,64},{128,96},{160,128},{192,160},{224,1... | collective-permute-start | bytes 786440 | tf_op jit(solution)/shard_map/ppermute | solution.py:32
  56.1 11.6 %collective-permute-done.8 = bf16[64,2048]{1,0:T(8,128)(2,1)S(1)} collective-permute-done((bf16[64,2048]{1,0:T(8,128)(2,1)S(1)}, bf16[64,2048]{1,0:T(8,128)(2,1)S(1)}, u32[]{:S(2)}, u32[]{:S(2)}) %collective-permute-start.8) | collective-permute-done | bytes 262176 | tf_op jit(solution)/shard_map/ppermute | solution.py:32
  68.4 2.9 %shard_map.65 = (f32[256,384]{1,0:T(8,128)S(1)}, f32[256,384]{1,0:T(8,128)S(1)}) custom-call(s32[1]{0:T(128)} %bitcast.3.core_ref, bf16[512,2048]{1,0:T(8,128)(2,1)} %bitcast.15.image_ref.own_ref, bf16[384,2048]{1,0:T(8,128)(2,1)S(1)} %bitcast.43, f32[1,384]{1,0:T(1,128)S(1)} %mul.75.penalty_ref), custom_call_target="tpu_custom_call" | custom-call | flops 805306368 | bytes 4456448 | tf_op jit(solution)/shard_map/pallas_call | solution.py:72
  71.3 1.9 collective-permute-start.9
  75.7 8.6 %all-to-all-start.1 = ((f32[16,16,384]{2,1,0:T(8,128)}), f32[16,16,384]{2,1,0:T(8,128)S(1)}, u32[]{:S(2)}, u32[]{:S(2)}) async-start(f32[16,16,384]{2,1,0:T(8,128)} %bitcast.16), calls=%async_computation.1 | async-start | bytes 786432 | tf_op jit(solution)/shard_map/all_to_all | solution.py:24
  92.3 3.7 %all-to-all-done.1 = f32[16,16,384]{2,1,0:T(8,128)S(1)} async-done(((f32[16,16,384]{2,1,0:T(8,128)}), f32[16,16,384]{2,1,0:T(8,128)S(1)}, u32[]{:S(2)}, u32[]{:S(2)}) %all-to-all-start.1) | async-done | bytes 393248 | tf_op jit(solution)/shard_map/all_to_all | solution.py:24
  96.0 5.8 %all-to-all-start = ((f32[16,16,384]{2,1,0:T(8,128)}), f32[16,16,384]{2,1,0:T(8,128)S(1)}, u32[]{:S(2)}, u32[]{:S(2)}) async-start(f32[16,16,384]{2,1,0:T(8,128)} %bitcast.5), calls=%async_computation | async-start | bytes 786432 | tf_op jit(solution)/shard_map/all_to_all | solution.py:24
  101.9 10.6 %all-to-all-done = f32[16,16,384]{2,1,0:T(8,128)S(1)} async-done(((f32[16,16,384]{2,1,0:T(8,128)}), f32[16,16,384]{2,1,0:T(8,128)S(1)}, u32[]{:S(2)}, u32[]{:S(2)}) %all-to-all-start) | async-done | bytes 393248 | tf_op jit(solution)/shard_map/all_to_all | solution.py:24
  113.0 17.8 %all_to_all.25 = f32[16,2,32]{2,1,0:T(2,128)S(1)} all-to-all(f32[16,2,32]{2,1,0:T(2,128)S(1)} %broadcast_in_dim.58), channel_id=1, replica_groups=mesh['yh'=2,'z'=8,'x'=4,'yl'=4,'core'=2] {'yh','z'}, dimensions={0} | all-to-all | bytes 8192 | tf_op jit(solution)/shard_map/all_to_all | solution.py:24
  131.2 14.5 %all_to_all.26.mine_ref = bf16[16,2,16,384]{3,2,1,0:T(8,128)(2,1)S(1)} all-to-all(bf16[16,2,16,384]{3,2,1,0:T(8,128)(2,1)S(1)} %broadcast_in_dim.59), channel_id=1, replica_groups=mesh['yh'=2,'z'=8,'x'=4,'yl'=4,'core'=2] {'x','yl'}, dimensions={0} | all-to-all | bytes 786432 | tf_op jit(solution)/shard_map/all_to_all | solution.py:24
  149.3 6.2 %shard_map.66 = (bf16[768,1024]{1,0:T(8,128)(2,1)S(1)}, bf16[1024,1024]{1,0:T(8,128)(2,1)S(1)}) custom-call(s32[1]{0:T(128)} %bitcast.3.core_ref, bf16[16,2,16,384]{3,2,1,0:T(8,128)(2,1)S(1)} %all_to_all.26.mine_ref, bf16[16,2,16,384]{3,2,1,0:T(8,128)(2,1)S(1)} %collective-permute-done.10.twin_ref, bf16[512,2048]{1,0:T(8,128)(2,1)S(1)} %copy-done.2, ...), custom_call_target="tpu_custom_call" | custom-call | flops 3221225472 | bytes 7864320 | tf_op jit(solution)/shard_map/pallas_call | solution.py:141
  155.5 2.1 collective-permute-start.11
  157.6 4.0 %collective-permute-done.11.got_ref = bf16[1024,1024]{1,0:T(8,128)(2,1)S(1)} collective-permute-done((bf16[1024,1024]{1,0:T(8,128)(2,1)S(1)}, bf16[1024,1024]{1,0:T(8,128)(2,1)S(1)}, u32[]{:S(2)}, u32[]{:S(2)}) %collective-permute-start.11) | collective-permute-done | bytes 2097184 | tf_op jit(solution)/shard_map/ppermute | solution.py:20
  162.2 3.1 %collective-permute-start.12 = (bf16[256,1024]{1,0:T(8,128)(2,1)S(1)}, bf16[256,1024]{1,0:T(8,128)(2,1)S(1)}, u32[]{:S(2)}, u32[]{:S(2)}) collective-permute-start(bf16[256,1024]{1,0:T(8,128)(2,1)S(1)} %shard_map.68), channel_id=1, source_target_pairs={{0,16},{8,24},{16,0},{24,8},{1,17},{9,25},{17,1},{25,9},{2,18},{10... | collective-permute-start | bytes 1572872 | tf_op jit(solution)/shard_map/ppermute | solution.py:32
  165.8 4.0 %collective-permute-start.13 = (bf16[256,1024]{1,0:T(8,128)(2,1)S(1)}, bf16[256,1024]{1,0:T(8,128)(2,1)S(1)}, u32[]{:S(2)}, u32[]{:S(2)}) collective-permute-start(bf16[256,1024]{1,0:T(8,128)(2,1)S(1)} %shard_map.69), channel_id=1, source_target_pairs={{0,8},{8,16},{16,24},{24,0},{1,9},{9,17},{17,25},{25,1},{2,10},{10... | collective-permute-start | bytes 1572872 | tf_op jit(solution)/shard_map/ppermute | solution.py:32
  170.4 1.9 collective-permute-start.14
  172.9 7.4 %collective-permute-done.12 = bf16[256,1024]{1,0:T(8,128)(2,1)S(1)} collective-permute-done((bf16[256,1024]{1,0:T(8,128)(2,1)S(1)}, bf16[256,1024]{1,0:T(8,128)(2,1)S(1)}, u32[]{:S(2)}, u32[]{:S(2)}) %collective-permute-start.12) | collective-permute-done | bytes 524320 | tf_op jit(solution)/shard_map/ppermute | solution.py:32
  180.4 10.1 %collective-permute-done.13 = bf16[256,1024]{1,0:T(8,128)(2,1)S(1)} collective-permute-done((bf16[256,1024]{1,0:T(8,128)(2,1)S(1)}, bf16[256,1024]{1,0:T(8,128)(2,1)S(1)}, u32[]{:S(2)}, u32[]{:S(2)}) %collective-permute-start.13) | collective-permute-done | bytes 524320 | tf_op jit(solution)/shard_map/ppermute | solution.py:32
  191.3 23.0 %all_to_all.27 = bf16[64,4,1024]{2,1,0:T(4,128)(2,1)S(1)} all-to-all(bf16[64,4,1024]{2,1,0:T(4,128)(2,1)S(1)} %reshape.464), channel_id=1, replica_groups=mesh['yh'=2,'z'=8,'x'=4,'yl'=4,'core'=2] {'yl','yh','z'}, dimensions={0} | all-to-all | bytes 1048576 | tf_op jit(solution)/shard_map/all_to_all | solution.py:24
  (79 shorter events, 36.1 us)
Async XLA Ops:
  6.5 208.0 %copy-start = (bf16[1,4,128,128]{3,2,1,0:T(8,128)(2,1)S(1)}, bf16[1,4,128,128]{3,2,1,0:T(8,128)(2,1)}, u32[]{:S(2)}) copy-start(bf16[1,4,128,128]{3,2,1,0:T(8,128)(2,1)} %param.11) | copy-start | bytes 393220
  6.5 78.5 %all-gather.3.cloned.1.call-start = ((), (), s32[]{:S(2)}) async-start(), calls=%async_computation.5 | async-start | bytes 2359296 | tf_op jit(solution)/shard_map/all_gather | solution.py:217
  6.5 25.3 %collective-permute-start.2 = (bf16[64,2048]{1,0:T(8,128)(2,1)}, bf16[64,2048]{1,0:T(8,128)(2,1)S(1)}, u32[]{:S(2)}, u32[]{:S(2)}) collective-permute-start(bf16[64,2048]{1,0:T(8,128)(2,1)} %param.6), channel_id=1, source_target_pairs={{0,32},{32,64},{64,96},{96,128},{128,160},{160,192},{192,224},{224... | collective-permute-start | bytes 786440 | tf_op jit(solution)/shard_map/ppermute | solution.py:32
  10.9 22.8 %collective-permute-start.3 = (bf16[64,2048]{1,0:T(8,128)(2,1)}, bf16[64,2048]{1,0:T(8,128)(2,1)S(1)}, u32[]{:S(2)}, u32[]{:S(2)}) collective-permute-start(bf16[64,2048]{1,0:T(8,128)(2,1)} %param.6), channel_id=1, source_target_pairs={{0,224},{32,0},{64,32},{96,64},{128,96},{160,128},{192,160},{224,1... | collective-permute-start | bytes 786440 | tf_op jit(solution)/shard_map/ppermute | solution.py:32
  19.5 19.3 %collective-permute-start = (bf16[64,2048]{1,0:T(8,128)(2,1)}, bf16[64,2048]{1,0:T(8,128)(2,1)S(1)}, u32[]{:S(2)}, u32[]{:S(2)}) collective-permute-start(bf16[64,2048]{1,0:T(8,128)(2,1)} %param.6), channel_id=1, source_target_pairs={{0,256},{256,0},{1,257},{257,1},{2,258},{258,2},{3,259},{259,3},{4... | collective-permute-start | bytes 786440 | tf_op jit(solution)/shard_map/ppermute | solution.py:20
  27.4 3.7 %copy-start.3 = (bf16[64,2048]{1,0:T(8,128)(2,1)S(1)}, bf16[64,2048]{1,0:T(8,128)(2,1)}, u32[]{:S(2)}) copy-start(bf16[64,2048]{1,0:T(8,128)(2,1)} %param.6) | copy-start | bytes 786436
  31.8 10.6 %collective-permute-start.4 = (bf16[64,2048]{1,0:T(8,128)(2,1)S(1)}, bf16[64,2048]{1,0:T(8,128)(2,1)S(1)}, u32[]{:S(2)}, u32[]{:S(2)}) collective-permute-start(bf16[64,2048]{1,0:T(8,128)(2,1)S(1)} %collective-permute-done.2), channel_id=1, source_target_pairs={{0,32},{32,64},{64,96},{96,128},{128,160},{160,192},{192,224},{224... | collective-permute-start | bytes 786440 | tf_op jit(solution)/shard_map/ppermute | solution.py:32
  33.7 10.6 %collective-permute-start.5 = (bf16[64,2048]{1,0:T(8,128)(2,1)S(1)}, bf16[64,2048]{1,0:T(8,128)(2,1)S(1)}, u32[]{:S(2)}, u32[]{:S(2)}) collective-permute-start(bf16[64,2048]{1,0:T(8,128)(2,1)S(1)} %collective-permute-done.3), channel_id=1, source_target_pairs={{0,224},{32,0},{64,32},{96,64},{128,96},{160,128},{192,160},{224,1... | collective-permute-start | bytes 786440 | tf_op jit(solution)/shard_map/ppermute | solution.py:32
  42.4 9.7 %collective-permute-start.6 = (bf16[64,2048]{1,0:T(8,128)(2,1)S(1)}, bf16[64,2048]{1,0:T(8,128)(2,1)S(1)}, u32[]{:S(2)}, u32[]{:S(2)}) collective-permute-start(bf16[64,2048]{1,0:T(8,128)(2,1)S(1)} %collective-permute-done.4), channel_id=1, source_target_pairs={{0,32},{32,64},{64,96},{96,128},{128,160},{160,192},{192,224},{224... | collective-permute-start | bytes 786440 | tf_op jit(solution)/shard_map/ppermute | solution.py:32
  44.3 11.1 %collective-permute-start.7 = (bf16[64,2048]{1,0:T(8,128)(2,1)S(1)}, bf16[64,2048]{1,0:T(8,128)(2,1)S(1)}, u32[]{:S(2)}, u32[]{:S(2)}) collective-permute-start(bf16[64,2048]{1,0:T(8,128)(2,1)S(1)} %collective-permute-done.5), channel_id=1, source_target_pairs={{0,224},{32,0},{64,32},{96,64},{128,96},{160,128},{192,160},{224,1... | collective-permute-start | bytes 786440 | tf_op jit(solution)/shard_map/ppermute | solution.py:32
  52.0 15.6 %collective-permute-start.8 = (bf16[64,2048]{1,0:T(8,128)(2,1)S(1)}, bf16[64,2048]{1,0:T(8,128)(2,1)S(1)}, u32[]{:S(2)}, u32[]{:S(2)}) collective-permute-start(bf16[64,2048]{1,0:T(8,128)(2,1)S(1)} %collective-permute-done.6), channel_id=1, source_target_pairs={{0,32},{32,64},{64,96},{96,128},{128,160},{160,192},{192,224},{224... | collective-permute-start | bytes 786440 | tf_op jit(solution)/shard_map/ppermute | solution.py:32
  71.3 3.6 %collective-permute-start.9 = (f32[256,384]{1,0:T(8,128)S(1)}, f32[256,384]{1,0:T(8,128)S(1)}, u32[]{:S(2)}, u32[]{:S(2)}) collective-permute-start(f32[256,384]{1,0:T(8,128)S(1)} %get-tuple-element.14), channel_id=1, source_target_pairs={{0,1},{1,0},{2,3},{3,2},{4,5},{5,4},{6,7},{7,6},{8,9},{9,8},{10,11... | collective-permute-start | bytes 1179656 | tf_op jit(solution)/shard_map/ppermute | solution.py:20
  75.7 20.3 %all-to-all-start.1 = ((f32[16,16,384]{2,1,0:T(8,128)}), f32[16,16,384]{2,1,0:T(8,128)S(1)}, u32[]{:S(2)}, u32[]{:S(2)}) async-start(f32[16,16,384]{2,1,0:T(8,128)} %bitcast.16), calls=%async_computation.1 | async-start | bytes 786432 | tf_op jit(solution)/shard_map/all_to_all | solution.py:24
  85.0 1.6 copy-start.1
  86.6 15.2 %copy-start.6 = (f32[8,48]{1,0:T(8,128)S(1)}, f32[8,48]{1,0:T(8,128)}, u32[]{:S(2)}) copy-start(f32[8,48]{1,0:T(8,128)} %param.9) | copy-start | bytes 4612
  87.9 3.6 %collective-permute-start.1 = (f32[256,384]{1,0:T(8,128)S(1)}, f32[256,384]{1,0:T(8,128)S(1)}, u32[]{:S(2)}, u32[]{:S(2)}) collective-permute-start(f32[256,384]{1,0:T(8,128)S(1)} %get-tuple-element.12), channel_id=1, source_target_pairs={{0,1},{1,0},{2,3},{3,2},{4,5},{5,4},{6,7},{7,6},{8,9},{9,8},{10,11... | collective-permute-start | bytes 1179656 | tf_op jit(solution)/shard_map/ppermute | solution.py:20
  91.5 56.1 %copy-start.5 = (s32[1,48,16,2]{1,3,2,0:T(2,128)S(1)}, s32[1,48,16,2]{1,3,2,0:T(2,128)}, u32[]{:S(2)}) copy-start(s32[1,48,16,2]{1,3,2,0:T(2,128)} %param.10) | copy-start | bytes 18436
  91.5 57.8 %copy-start.2 = (bf16[512,2048]{1,0:T(8,128)(2,1)S(1)}, bf16[512,2048]{1,0:T(8,128)(2,1)}, u32[]{:S(2)}) copy-start(bf16[512,2048]{1,0:T(8,128)(2,1)} %all-gather.3.cloned.1.call-done.image_ref.other_ref) | copy-start | bytes 6291460
  96.0 16.6 %all-to-all-start = ((f32[16,16,384]{2,1,0:T(8,128)}), f32[16,16,384]{2,1,0:T(8,128)S(1)}, u32[]{:S(2)}, u32[]{:S(2)}) async-start(f32[16,16,384]{2,1,0:T(8,128)} %bitcast.5), calls=%async_computation | async-start | bytes 786432 | tf_op jit(solution)/shard_map/all_to_all | solution.py:24
  145.6 3.6 %collective-permute-start.10 = (bf16[16,2,16,384]{3,2,1,0:T(8,128)(2,1)S(1)}, bf16[16,2,16,384]{3,2,1,0:T(8,128)(2,1)S(1)}, u32[]{:S(2)}, u32[]{:S(2)}) collective-permute-start(bf16[16,2,16,384]{3,2,1,0:T(8,128)(2,1)S(1)} %all_to_all.26.mine_ref), channel_id=1, source_target_pairs={{0,1},{1,0},{2,3},{3,2},{4,5},{5,4},{6,7},{7,6},{8,9},{9,8},{10,11... | collective-permute-start | bytes 1179656 | tf_op jit(solution)/shard_map/ppermute | solution.py:20
  155.5 6.1 %collective-permute-start.11 = (bf16[1024,1024]{1,0:T(8,128)(2,1)S(1)}, bf16[1024,1024]{1,0:T(8,128)(2,1)S(1)}, u32[]{:S(2)}, u32[]{:S(2)}) collective-permute-start(bf16[1024,1024]{1,0:T(8,128)(2,1)S(1)} %get-tuple-element.16), channel_id=1, source_target_pairs={{0,1},{1,0},{2,3},{3,2},{4,5},{5,4},{6,7},{7,6},{8,9},{9,8},{10,11... | collective-permute-start | bytes 6291464 | tf_op jit(solution)/shard_map/ppermute | solution.py:20
  162.2 18.2 %collective-permute-start.12 = (bf16[256,1024]{1,0:T(8,128)(2,1)S(1)}, bf16[256,1024]{1,0:T(8,128)(2,1)S(1)}, u32[]{:S(2)}, u32[]{:S(2)}) collective-permute-start(bf16[256,1024]{1,0:T(8,128)(2,1)S(1)} %shard_map.68), channel_id=1, source_target_pairs={{0,16},{8,24},{16,0},{24,8},{1,17},{9,25},{17,1},{25,9},{2,18},{10... | collective-permute-start | bytes 1572872 | tf_op jit(solution)/shard_map/ppermute | solution.py:32
  165.8 24.7 %collective-permute-start.13 = (bf16[256,1024]{1,0:T(8,128)(2,1)S(1)}, bf16[256,1024]{1,0:T(8,128)(2,1)S(1)}, u32[]{:S(2)}, u32[]{:S(2)}) collective-permute-start(bf16[256,1024]{1,0:T(8,128)(2,1)S(1)} %shard_map.69), channel_id=1, source_target_pairs={{0,8},{8,16},{16,24},{24,0},{1,9},{9,17},{17,25},{25,1},{2,10},{10... | collective-permute-start | bytes 1572872 | tf_op jit(solution)/shard_map/ppermute | solution.py:32
  170.4 20.4 %collective-permute-start.14 = (bf16[256,1024]{1,0:T(8,128)(2,1)S(1)}, bf16[256,1024]{1,0:T(8,128)(2,1)S(1)}, u32[]{:S(2)}, u32[]{:S(2)}) collective-permute-start(bf16[256,1024]{1,0:T(8,128)(2,1)S(1)} %shard_map.70), channel_id=1, source_target_pairs={{0,24},{8,0},{16,8},{24,16},{1,25},{9,1},{17,9},{25,17},{2,26},{10... | collective-permute-start | bytes 1572872 | tf_op jit(solution)/shard_map/ppermute | solution.py:32
  (1 other events, 0.7 us)
Sparse Core Ops, SparseCore 0:
  39.7 45.2 all-gather.2

commit v5 on v4

--- a/solution.py
+++ b/solution.py
@@ -8,6 +8,8 @@
 from jax.sharding import Mesh, PartitionSpec as P
 
 PIECE = 128
+SCORE = 56
+SLICE = 24
 NAMES = ("yh", "z", "x", "yl", "core")
 SIZES = (2, 8, 4, 4, 2)
 ORIENT = ("yh", "z")
@@ -32,23 +34,25 @@
     return lax.ppermute(block, axis, [(i, (i + step) % count) for i in range(count)])
 
 
-def ring_gathered(block):
+def ring_gathered(block, later, other):
     count = 8
     z = lax.axis_index("z")
     held = jnp.zeros((count,) + block.shape, block.dtype)
     held = lax.dynamic_update_index_in_dim(held, block, z, 0)
-    up = down = block
+    up, down = block, later
     for step in range(1, count // 2 + 1):
         up = turned(up, 1)
         held = lax.dynamic_update_index_in_dim(held, up, (z - step) % count, 0)
         if step < count // 2:
+            if step == 2:
+                down, other = lax.optimization_barrier((down, other))
             down = turned(down, -1)
             held = lax.dynamic_update_index_in_dim(held, down, (z + step) % count, 0)
-    return held
-
-
-def kernel_params():
-    return pltpu.CompilerParams(vmem_limit_bytes=24 * 2**20)
+    return held, other
+
+
+def kernel_params(mebibytes=16):
+    return pltpu.CompilerParams(vmem_limit_bytes=mebibytes * 2**20)
 
 
 def score_kernel(core_ref, image_ref, weighted_ref, penalty_ref, far_ref, near_ref):
@@ -74,7 +78,7 @@
         out_shape=(side, side),
         in_specs=[pl.BlockSpec(memory_space=pltpu.SMEM), whole, whole, whole],
         out_specs=(whole, whole),
-        compiler_params=kernel_params(),
+        compiler_params=kernel_params(SCORE),
         cost_estimate=pl.CostEstimate(
             flops=2 * rows * pixels * columns,
             bytes_accessed=2 * pixels * (rows + columns) + 4 * rows * columns,
@@ -121,11 +125,10 @@
 
     @pl.when(step == pl.num_programs(0) - 1)
     def _():
-        slots = away_ref.shape[0]
-        for r in range(0, slots, 256):
-            away_ref[r : r + 256, :] = jnp.dot(
-                spots(slot_ref, slots + r, 256), pieces_ref[...], preferred_element_type=f32
-            ).astype(bf16)
+        count = away_ref.shape[0]
+        away_ref[...] = jnp.dot(
+            spots(slot_ref, 6 * count, count), pieces_ref[...], preferred_element_type=f32
+        ).astype(bf16)
 
 
 def sliced(core, mine, twin, other_plane, own_plane, slot, slots):
@@ -158,7 +161,7 @@
             pl.BlockSpec((slots, width), fixed(2)),
         ),
         scratch_shapes=[pltpu.VMEM((columns, 2 * rows), bf16)],
-        compiler_params=kernel_params(),
+        compiler_params=kernel_params(SLICE),
         cost_estimate=pl.CostEstimate(
             flops=4 * rows * pixels * columns + 2 * slots * pieces * width,
             bytes_accessed=4 * rows * pixels + 2 * width * (pieces + slots),
@@ -167,30 +170,68 @@
     )(core, mine, twin, other_plane, own_plane, slot)
 
 
-def near_kernel(start, slot_ref, pieces_ref, got_ref, sum_ref):
-    count = sum_ref.shape[0]
+def away_kernel(slot_ref, pieces_ref, away_ref):
+    count = away_ref.shape[0] // 3
+    for row, part in enumerate((1, 3, 0)):
+        away_ref[row * count : (row + 1) * count, :] = jnp.dot(
+            spots(slot_ref, (4 + part) * count, count),
+            pieces_ref[...],
+            preferred_element_type=f32,
+        ).astype(bf16)
+
+
+def near_kernel(part, row, lead, slot_ref, pieces_ref, got_ref, *refs):
+    count = refs[-1].shape[0]
     near = jnp.dot(
-        spots(slot_ref, start, count), pieces_ref[...], preferred_element_type=f32
-    )
-    sum_ref[...] = (near + got_ref[start : start + count, :].astype(f32)).astype(sum_ref.dtype)
-
-
-def near_summed(slot, pieces, got, part, dtype):
-    slots, width = got.shape
-    count = slots // 4
+        spots(slot_ref, part * count, count), pieces_ref[...], preferred_element_type=f32
+    ) + got_ref[row * count : (row + 1) * count, :].astype(f32)
+    if part == 2:
+        half = near.shape[1] // 2
+        refs[0][...] = near[:, :half].astype(bf16)
+        refs[1][...] = near[:, half:].astype(bf16)
+    elif part == 0:
+        refs[0][...] = near
+    else:
+        passed_ref, sum_ref = refs
+        half = passed_ref.shape[1]
+        added = slice(lead, lead + half)
+        other = slice(half - lead, 2 * half - lead)
+        sum_ref[:, added] = (near[:, added] + passed_ref[...].astype(f32)).astype(bf16)
+        sum_ref[:, other] = near[:, other].astype(bf16)
+
+
+def whole_call(kernel, outs, flops, *args):
     whole = pl.BlockSpec(memory_space=pltpu.VMEM)
+    moved = sum(x.size * x.dtype.itemsize for x in args)
     return pl.pallas_call(
-        functools.partial(near_kernel, part * count),
-        out_shape=jax.ShapeDtypeStruct((count, width), dtype),
-        in_specs=[whole] * 3,
-        out_specs=whole,
+        kernel,
+        out_shape=outs,
+        in_specs=[whole] * len(args),
+        out_specs=jax.tree.map(lambda _: whole, outs),
         compiler_params=kernel_params(),
-        cost_estimate=pl.CostEstimate(
-            flops=2 * count * pieces.shape[0] * width,
-            bytes_accessed=2 * width * (pieces.shape[0] + 2 * count),
-            transcendentals=0,
-        ),
-    )(slot, pieces, got)
+        cost_estimate=pl.CostEstimate(flops=flops, bytes_accessed=moved, transcendentals=0),
+    )(*args)
+
+
+def slots_summed(slot, cut, away, count):
+    pieces, width = cut.shape
+    flops = 2 * count * pieces * width
+    shape = lambda wide, dtype: jax.ShapeDtypeStruct((count, wide), dtype)
+    far = swapped(away, "core")
+    rest = jax.ShapeDtypeStruct((3 * count, width), bf16)
+    rest = swapped(whole_call(away_kernel, rest, 3 * flops, slot, cut), "core")
+
+    def near(part, row, lead, outs, *args):
+        kernel = functools.partial(near_kernel, part, row, lead)
+        return whole_call(kernel, outs, flops, slot, cut, *args)
+
+    halves = (shape(width // 2, bf16),) * 2
+    left, right = near(2, 0, 0, halves, far)
+    left, right = turned(left, 1, "x", 4), turned(right, -1, "x", 4)
+    summed = near(0, 2, 0, shape(width, f32), rest)
+    one = turned(near(1, 0, 0, shape(width, bf16), rest, left), 1, "x", 4)
+    three = turned(near(3, 1, width // 2, shape(width, bf16), rest, right), -1, "x", 4)
+    return (summed + one.astype(f32) + three.astype(f32)).astype(bf16)
 
 
 def local(images, projections, noise_weight, prior_score, routing, insert_kernel):
@@ -214,14 +255,16 @@
     slot = ((((owner % 2) ^ core) * 4 + ahead) * 4 + owner // 2 % 4) * voxels + voxel
 
     other = swapped(images, "yh")
-    other_plane = lax.all_gather(other, "z", axis=0).reshape(plane_rows, pixels)
-    own_plane = ring_gathered(images).reshape(plane_rows, pixels)
 
     widened = projections.astype(f32)
     product = widened * noise_weight[None, None, :]
     weighted = product.astype(bf16).reshape(columns, pixels)
     penalty = (-0.5 * jnp.sum(widened * product, axis=2)).reshape(1, columns)
     prior = prior_score.reshape(columns)
+    later, penalty = lax.optimization_barrier((images, penalty))
+    own_plane, other = ring_gathered(images, later, other)
+    own_plane = own_plane.reshape(plane_rows, pixels)
+    other_plane = lax.all_gather(other, "z", axis=0).reshape(plane_rows, pixels)
 
     def plane_scores(stored):
         far, near = scored(core_one, stored, weighted, penalty)
@@ -242,14 +285,9 @@
     mine = shared(own_weights, ("x", "yl"), half)
     twin = swapped(mine, "core")
 
-    cut, away = sliced(core_one, mine, twin, other_plane, own_plane, slot, half * voxels)
-    got = swapped(away, "core")
+    cut, away = sliced(core_one, mine, twin, other_plane, own_plane, slot, 4 * voxels)
     width = classes * PIECE
-    summed = near_summed(slot, cut, got, 0, f32)
-    for part in (2, 1, 3):
-        sent = near_summed(slot, cut, got, part, bf16)
-        summed = summed + turned(sent, part, "x", 4).astype(f32)
-    summed = summed.astype(bf16)
+    summed = slots_summed(slot, cut, away, 4 * voxels)
     summed = exchanged(summed.reshape(4 * orients, voxels // orients, width), ("yl", "yh", "z"))
     own_blocks = jnp.sum(summed.astype(f32), axis=0)
     rounded = own_blocks.astype(bf16).reshape(own_blocks.shape[0], classes, PIECE)

time: 225 us -> 243 us (1.080)
  waiting for transfers between devices: 56.4 us -> 72.5 us
  local copies, waits for them, and re-layouts: 10.5 us -> 4.78 us
  starting transfers between devices: 67.9 us -> 71.6 us
  other arithmetic: 4.76 us -> 7.82 us
  Pallas kernels: 12.7 us -> 15.7 us
    ppermute x10 -> x11, waiting for transfers between devices: 32.6 us -> 52.2 us  [turned(): lax.ppermute(block, axis, [(i, (i + step) % count) for i in range(count)])]
    ppermute x10 -> x11, starting transfers between devices: 38 us -> 43.1 us  [turned(): lax.ppermute(block, axis, [(i, (i + step) % count) for i in range(count)])]
    pallas_call x2, Pallas kernels: 4.12 us -> 8.15 us  [scored(): pl.pallas_call(score_kernel, out_shape=(side, side), in_specs=[pl.BlockSp...]
    all_to_all x2, starting transfers between devices: 14.4 us -> 10.8 us  [exchanged(): return lax.all_to_all(value, axis, 0, 0, tiled=True)]
    convert_element_type x1 -> x2, other arithmetic: 0.35 us -> 3.29 us  [the longest x1 3.04 us: local(): weighted = product.astype(bf16).reshape(columns, pixels)]
    dynamic_update_slice x4, local copies, waits for them, and re-layouts: 2.87 us -> 0.09 us  [ring_gathered(): held = lax.dynamic_update_index_in_dim(held, up, (z - step) % count, 0)]
    pallas_call x1, Pallas kernels: 6.25 us -> 3.74 us  [sliced(): pl.pallas_call(slice_kernel, grid=(steps,), out_shape=(jax.ShapeDtypeStru...]
    ppermute x5 -> x6, starting transfers between devices: 15.5 us -> 17.8 us  [swapped(): return lax.ppermute(value, axis, [(0, 1), (1, 0)])]
  transfers between devices with their start and end apart: 18 -> 20, of which waited for: 14 -> 13; matrix products, arithmetic and copies ran while one was open for 5% -> 3% of each run, Pallas kernels for 3% -> 4%
where the time goes in v5:
time: 243 us; the launch traced here: 242 us
  waiting for transfers between devices  72.5 us (30%)
  starting transfers between devices  71.6 us (29%)
  blocking collectives  54.9 us (23%)
  Pallas kernels  15.7 us (6%)
  between operations  13.9 us (6%)
  other arithmetic  7.82 us (3%)
  local copies, waits for them, and re-layouts  4.78 us (2%)
    all_to_all x3, blocking collectives, exchanged(): return lax.all_to_all(value, axis, 0, 0, tiled=True)  54.9 us
    ppermute x11, waiting for transfers between devices, turned(): lax.ppermute(block, axis, [(i, (i + step) % count) for i in range(count)])  52.2 us
    ppermute x11, starting transfers between devices, turned(): lax.ppermute(block, axis, [(i, (i + step) % count) for i in range(count)])  43.1 us
    ppermute x6, starting transfers between devices, swapped(): return lax.ppermute(value, axis, [(0, 1), (1, 0)])  17.8 us
    all_to_all x2, waiting for transfers between devices, exchanged(): return lax.all_to_all(value, axis, 0, 0, tiled=True)  13.3 us
    all_to_all x2, starting transfers between devices, exchanged(): return lax.all_to_all(value, axis, 0, 0, tiled=True)  10.8 us
    pallas_call x2, Pallas kernels, scored(): pl.pallas_call(score_kernel, out_shape=(side, side), in_specs=[pl.BlockSp...  8.15 us
    ppermute x6, waiting for transfers between devices, swapped(): return lax.ppermute(value, axis, [(0, 1), (1, 0)])  6.89 us
  transfers between devices with their start and end apart: 20, of which 13 were waited for; matrix products, arithmetic and copies ran while one was open for 3% of the time, Pallas kernels for 4%

profile of v5, /device:TPU:6, one launch (start us, length us, event | category | flops | bytes accessed | tf_op | source)
XLA Modules:
  0.0 242.0 jit_solution(6671661766229643144)
XLA Ops:
  6.5 4.4 %collective-permute-start.3 = (bf16[64,2048]{1,0:T(8,128)(2,1)}, bf16[64,2048]{1,0:T(8,128)(2,1)S(1)}, u32[]{:S(2)}, u32[]{:S(2)}) collective-permute-start(bf16[64,2048]{1,0:T(8,128)(2,1)} %param.6), channel_id=1, source_target_pairs={{0,32},{32,64},{64,96},{96,128},{128,160},{160,192},{192,224},{224... | collective-permute-start | bytes 786440 | tf_op jit(solution)/shard_map/ppermute | solution.py:34
  10.9 7.7 %collective-permute-start.1 = (bf16[64,2048]{1,0:T(8,128)(2,1)}, bf16[64,2048]{1,0:T(8,128)(2,1)S(1)}, u32[]{:S(2)}, u32[]{:S(2)}) collective-permute-start(bf16[64,2048]{1,0:T(8,128)(2,1)} %param.6), channel_id=1, source_target_pairs={{0,256},{256,0},{1,257},{257,1},{2,258},{258,2},{3,259},{259,3},{4... | collective-permute-start | bytes 786440 | tf_op jit(solution)/shard_map/ppermute | solution.py:22
  18.7 3.0 %multiply_convert_fusion = (bf16[8,48,2048]{2,1,0:T(8,128)(2,1)}, f32[8,48]{1,0:T(8,128)S(1)}) fusion(bf16[8,48,2048]{2,1,0:T(8,128)(2,1)} %param.7, f32[2048]{0:T(1024)} %param.8), kind=kLoop, calls=%fused_computation | loop fusion | flops 3931776 | bytes 3155456 | tf_op jit(solution)/shard_map/convert_element_type | solution.py:261
  22.4 8.6 %collective-permute-start = (bf16[64,2048]{1,0:T(8,128)(2,1)S(1)}, bf16[64,2048]{1,0:T(8,128)(2,1)S(1)}, u32[]{:S(2)}, u32[]{:S(2)}) collective-permute-start(bf16[64,2048]{1,0:T(8,128)(2,1)S(1)} %copy-done.4), channel_id=1, source_target_pairs={{0,224},{32,0},{64,32},{96,64},{128,96},{160,128},{192,160},{224,1... | collective-permute-start | bytes 786440 | tf_op jit(solution)/shard_map/ppermute | solution.py:34
  31.4 4.8 %collective-permute-done = bf16[64,2048]{1,0:T(8,128)(2,1)S(1)} collective-permute-done((bf16[64,2048]{1,0:T(8,128)(2,1)S(1)}, bf16[64,2048]{1,0:T(8,128)(2,1)S(1)}, u32[]{:S(2)}, u32[]{:S(2)}) %collective-permute-start) | collective-permute-done | bytes 262176 | tf_op jit(solution)/shard_map/ppermute | solution.py:34
  36.2 5.6 %collective-permute-start.5 = (bf16[64,2048]{1,0:T(8,128)(2,1)S(1)}, bf16[64,2048]{1,0:T(8,128)(2,1)S(1)}, u32[]{:S(2)}, u32[]{:S(2)}) collective-permute-start(bf16[64,2048]{1,0:T(8,128)(2,1)S(1)} %collective-permute-done), channel_id=1, source_target_pairs={{0,224},{32,0},{64,32},{96,64},{128,96},{160,128},{192,160},{224,1... | collective-permute-start | bytes 786440 | tf_op jit(solution)/shard_map/ppermute | solution.py:34
  43.9 7.7 %collective-permute-done.4 = bf16[64,2048]{1,0:T(8,128)(2,1)S(1)} collective-permute-done((bf16[64,2048]{1,0:T(8,128)(2,1)S(1)}, bf16[64,2048]{1,0:T(8,128)(2,1)S(1)}, u32[]{:S(2)}, u32[]{:S(2)}) %collective-permute-start.4) | collective-permute-done | bytes 262176 | tf_op jit(solution)/shard_map/ppermute | solution.py:34
  53.5 5.1 %collective-permute-start.7 = (bf16[64,2048]{1,0:T(8,128)(2,1)S(1)}, bf16[64,2048]{1,0:T(8,128)(2,1)S(1)}, u32[]{:S(2)}, u32[]{:S(2)}) collective-permute-start(bf16[64,2048]{1,0:T(8,128)(2,1)S(1)} %collective-permute-done.5), channel_id=1, source_target_pairs={{0,224},{32,0},{64,32},{96,64},{128,96},{160,128},{192,160},{224,1... | collective-permute-start | bytes 786440 | tf_op jit(solution)/shard_map/ppermute | solution.py:34
  58.7 8.8 %collective-permute-done.6 = bf16[64,2048]{1,0:T(8,128)(2,1)S(1)} collective-permute-done((bf16[64,2048]{1,0:T(8,128)(2,1)S(1)}, bf16[64,2048]{1,0:T(8,128)(2,1)S(1)}, u32[]{:S(2)}, u32[]{:S(2)}) %collective-permute-start.6) | collective-permute-done | bytes 262176 | tf_op jit(solution)/shard_map/ppermute | solution.py:34
  69.4 13.4 %collective-permute-done.8 = bf16[64,2048]{1,0:T(8,128)(2,1)S(1)} collective-permute-done((bf16[64,2048]{1,0:T(8,128)(2,1)S(1)}, bf16[64,2048]{1,0:T(8,128)(2,1)S(1)}, u32[]{:S(2)}, u32[]{:S(2)}) %collective-permute-start.8) | collective-permute-done | bytes 262176 | tf_op jit(solution)/shard_map/ppermute | solution.py:34
  84.2 4.1 %shard_map.65 = (f32[256,384]{1,0:T(8,128)}, f32[256,384]{1,0:T(8,128)}) custom-call(s32[1]{0:T(128)} %bitcast.3.core_ref, bf16[512,2048]{1,0:T(8,128)(2,1)} %bitcast.43, bf16[384,2048]{1,0:T(8,128)(2,1)} %bitcast.45, f32[1,384]{1,0:T(1,128)} %mul.75.penalty_ref), custom_call_target="tpu_custom_call" | custom-call | flops 805306368 | bytes 4456448 | tf_op jit(solution)/shard_map/pallas_call | solution.py:76
  93.9 5.0 %all-to-all-start.1 = ((f32[16,16,384]{2,1,0:T(8,128)}), f32[16,16,384]{2,1,0:T(8,128)S(1)}, u32[]{:S(2)}, u32[]{:S(2)}) async-start(f32[16,16,384]{2,1,0:T(8,128)} %bitcast.16), calls=%async_computation.1 | async-start | bytes 786432 | tf_op jit(solution)/shard_map/all_to_all | solution.py:26
  98.9 4.1 %shard_map.64 = (f32[256,384]{1,0:T(8,128)}, f32[256,384]{1,0:T(8,128)}) custom-call(s32[1]{0:T(128)} %bitcast.3.core_ref, bf16[512,2048]{1,0:T(8,128)(2,1)} %all-gather.3.cloned.1.call-done.image_ref.other_ref, bf16[384,2048]{1,0:T(8,128)(2,1)} %bitcast.46, f32[1,384]{1,0:T(1,128)} %mul.75.penalty_ref), custom_call_target="tpu_custom_call" | custom-call | flops 805306368 | bytes 4456448 | tf_op jit(solution)/shard_map/pallas_call | solution.py:76
  110.5 5.8 %all-to-all-start = ((f32[16,16,384]{2,1,0:T(8,128)}), f32[16,16,384]{2,1,0:T(8,128)S(1)}, u32[]{:S(2)}, u32[]{:S(2)}) async-start(f32[16,16,384]{2,1,0:T(8,128)} %bitcast.5), calls=%async_computation | async-start | bytes 786432 | tf_op jit(solution)/shard_map/all_to_all | solution.py:26
  116.5 11.5 %all-to-all-done = f32[16,16,384]{2,1,0:T(8,128)S(1)} async-done(((f32[16,16,384]{2,1,0:T(8,128)}), f32[16,16,384]{2,1,0:T(8,128)S(1)}, u32[]{:S(2)}, u32[]{:S(2)}) %all-to-all-start) | async-done | bytes 393248 | tf_op jit(solution)/shard_map/all_to_all | solution.py:26
  128.4 18.8 %all_to_all.25 = f32[16,2,32]{2,1,0:T(2,128)S(1)} all-to-all(f32[16,2,32]{2,1,0:T(2,128)S(1)} %broadcast_in_dim.58), channel_id=1, replica_groups=mesh['yh'=2,'z'=8,'x'=4,'yl'=4,'core'=2] {'yh','z'}, dimensions={0} | all-to-all | bytes 8192 | tf_op jit(solution)/shard_map/all_to_all | solution.py:26
  147.6 14.9 %all_to_all.26.mine_ref = bf16[16,2,16,384]{3,2,1,0:T(8,128)(2,1)S(1)} all-to-all(bf16[16,2,16,384]{3,2,1,0:T(8,128)(2,1)S(1)} %broadcast_in_dim.59), channel_id=1, replica_groups=mesh['yh'=2,'z'=8,'x'=4,'yl'=4,'core'=2] {'x','yl'}, dimensions={0} | all-to-all | bytes 786432 | tf_op jit(solution)/shard_map/all_to_all | solution.py:26
  167.7 3.7 %shard_map.66 = (bf16[768,1024]{1,0:T(8,128)(2,1)S(1)}, bf16[256,1024]{1,0:T(8,128)(2,1)S(1)}) custom-call(s32[1]{0:T(128)} %bitcast.3.core_ref, bf16[16,2,16,384]{3,2,1,0:T(8,128)(2,1)S(1)} %all_to_all.26.mine_ref, bf16[16,2,16,384]{3,2,1,0:T(8,128)(2,1)S(1)} %collective-permute-done.10.twin_ref, bf16[512,2048]{1,0:T(8,128)(2,1)S(1)} %copy-done.3, ...), custom_call_target="tpu_custom_call" | custom-call | flops 2013265920 | bytes 6291456 | tf_op jit(solution)/shard_map/pallas_call | solution.py:144
  179.5 4.3 %collective-permute-start.13 = (bf16[256,512]{1,0:T(8,128)(2,1)S(1)}, bf16[256,512]{1,0:T(8,128)(2,1)S(1)}, u32[]{:S(2)}, u32[]{:S(2)}) collective-permute-start(bf16[256,512]{1,0:T(8,128)(2,1)S(1)} %get-tuple-element.27), channel_id=1, source_target_pairs={{0,8},{8,16},{16,24},{24,0},{1,9},{9,17},{17,25},{25,1},{2,10},{10... | collective-permute-start | bytes 786440 | tf_op jit(solution)/shard_map/ppermute | solution.py:34
  185.7 4.1 %collective-permute-done.13.refs_0_ = bf16[256,512]{1,0:T(8,128)(2,1)S(1)} collective-permute-done((bf16[256,512]{1,0:T(8,128)(2,1)S(1)}, bf16[256,512]{1,0:T(8,128)(2,1)S(1)}, u32[]{:S(2)}, u32[]{:S(2)}) %collective-permute-start.13) | collective-permute-done | bytes 262176 | tf_op jit(solution)/shard_map/ppermute | solution.py:34
  190.4 5.5 %collective-permute-start.14 = (bf16[256,1024]{1,0:T(8,128)(2,1)S(1)}, bf16[256,1024]{1,0:T(8,128)(2,1)S(1)}, u32[]{:S(2)}, u32[]{:S(2)}) collective-permute-start(bf16[256,1024]{1,0:T(8,128)(2,1)S(1)} %shard_map.70), channel_id=1, source_target_pairs={{0,8},{8,16},{16,24},{24,0},{1,9},{9,17},{17,25},{25,1},{2,10},{10... | collective-permute-start | bytes 1572872 | tf_op jit(solution)/shard_map/ppermute | solution.py:34
  199.0 7.5 %collective-permute-done.14 = bf16[256,1024]{1,0:T(8,128)(2,1)S(1)} collective-permute-done((bf16[256,1024]{1,0:T(8,128)(2,1)S(1)}, bf16[256,1024]{1,0:T(8,128)(2,1)S(1)}, u32[]{:S(2)}, u32[]{:S(2)}) %collective-permute-start.14) | collective-permute-done | bytes 524320 | tf_op jit(solution)/shard_map/ppermute | solution.py:34
  206.6 6.0 %collective-permute-done.16 = bf16[256,1024]{1,0:T(8,128)(2,1)S(1)} collective-permute-done((bf16[256,1024]{1,0:T(8,128)(2,1)S(1)}, bf16[256,1024]{1,0:T(8,128)(2,1)S(1)}, u32[]{:S(2)}, u32[]{:S(2)}) %collective-permute-start.16) | collective-permute-done | bytes 524320 | tf_op jit(solution)/shard_map/ppermute | solution.py:34
  213.0 21.1 %all_to_all.27 = bf16[64,4,1024]{2,1,0:T(4,128)(2,1)S(1)} all-to-all(bf16[64,4,1024]{2,1,0:T(4,128)(2,1)S(1)} %reshape.464), channel_id=1, replica_groups=mesh['yh'=2,'z'=8,'x'=4,'yl'=4,'core'=2] {'yl','yh','z'}, dimensions={0} | all-to-all | bytes 1048576 | tf_op jit(solution)/shard_map/all_to_all | solution.py:26
  (86 shorter events, 42.5 us)
Async XLA Ops:
  6.5 227.8 %copy-start = (bf16[1,4,128,128]{3,2,1,0:T(8,128)(2,1)S(1)}, bf16[1,4,128,128]{3,2,1,0:T(8,128)(2,1)}, u32[]{:S(2)}) copy-start(bf16[1,4,128,128]{3,2,1,0:T(8,128)(2,1)} %param.11) | copy-start | bytes 393220
  6.5 92.3 %all-gather.3.cloned.1.call-start = ((), (), s32[]{:S(2)}) async-start(), calls=%async_computation.5 | async-start | bytes 2359296 | tf_op jit(solution)/shard_map/all_gather | solution.py:267
  6.5 35.3 %collective-permute-start.3 = (bf16[64,2048]{1,0:T(8,128)(2,1)}, bf16[64,2048]{1,0:T(8,128)(2,1)S(1)}, u32[]{:S(2)}, u32[]{:S(2)}) collective-permute-start(bf16[64,2048]{1,0:T(8,128)(2,1)} %param.6), channel_id=1, source_target_pairs={{0,32},{32,64},{64,96},{96,128},{128,160},{160,192},{192,224},{224... | collective-permute-start | bytes 786440 | tf_op jit(solution)/shard_map/ppermute | solution.py:34
  10.9 25.3 %collective-permute-start.1 = (bf16[64,2048]{1,0:T(8,128)(2,1)}, bf16[64,2048]{1,0:T(8,128)(2,1)S(1)}, u32[]{:S(2)}, u32[]{:S(2)}) collective-permute-start(bf16[64,2048]{1,0:T(8,128)(2,1)} %param.6), channel_id=1, source_target_pairs={{0,256},{256,0},{1,257},{257,1},{2,258},{258,2},{3,259},{259,3},{4... | collective-permute-start | bytes 786440 | tf_op jit(solution)/shard_map/ppermute | solution.py:22
  22.4 13.8 %collective-permute-start = (bf16[64,2048]{1,0:T(8,128)(2,1)S(1)}, bf16[64,2048]{1,0:T(8,128)(2,1)S(1)}, u32[]{:S(2)}, u32[]{:S(2)}) collective-permute-start(bf16[64,2048]{1,0:T(8,128)(2,1)S(1)} %copy-done.4), channel_id=1, source_target_pairs={{0,224},{32,0},{64,32},{96,64},{128,96},{160,128},{192,160},{224,1... | collective-permute-start | bytes 786440 | tf_op jit(solution)/shard_map/ppermute | solution.py:34
  36.2 17.2 %collective-permute-start.5 = (bf16[64,2048]{1,0:T(8,128)(2,1)S(1)}, bf16[64,2048]{1,0:T(8,128)(2,1)S(1)}, u32[]{:S(2)}, u32[]{:S(2)}) collective-permute-start(bf16[64,2048]{1,0:T(8,128)(2,1)S(1)} %collective-permute-done), channel_id=1, source_target_pairs={{0,224},{32,0},{64,32},{96,64},{128,96},{160,128},{192,160},{224,1... | collective-permute-start | bytes 786440 | tf_op jit(solution)/shard_map/ppermute | solution.py:34
  41.9 9.7 %collective-permute-start.4 = (bf16[64,2048]{1,0:T(8,128)(2,1)S(1)}, bf16[64,2048]{1,0:T(8,128)(2,1)S(1)}, u32[]{:S(2)}, u32[]{:S(2)}) collective-permute-start(bf16[64,2048]{1,0:T(8,128)(2,1)S(1)} %collective-permute-done.3), channel_id=1, source_target_pairs={{0,32},{32,64},{64,96},{96,128},{128,160},{160,192},{192,224},{224... | collective-permute-start | bytes 786440 | tf_op jit(solution)/shard_map/ppermute | solution.py:34
  51.6 15.9 %collective-permute-start.6 = (bf16[64,2048]{1,0:T(8,128)(2,1)S(1)}, bf16[64,2048]{1,0:T(8,128)(2,1)S(1)}, u32[]{:S(2)}, u32[]{:S(2)}) collective-permute-start(bf16[64,2048]{1,0:T(8,128)(2,1)S(1)} %collective-permute-done.4), channel_id=1, source_target_pairs={{0,32},{32,64},{64,96},{96,128},{128,160},{160,192},{192,224},{224... | collective-permute-start | bytes 786440 | tf_op jit(solution)/shard_map/ppermute | solution.py:34
  53.5 15.9 %collective-permute-start.7 = (bf16[64,2048]{1,0:T(8,128)(2,1)S(1)}, bf16[64,2048]{1,0:T(8,128)(2,1)S(1)}, u32[]{:S(2)}, u32[]{:S(2)}) collective-permute-start(bf16[64,2048]{1,0:T(8,128)(2,1)S(1)} %collective-permute-done.5), channel_id=1, source_target_pairs={{0,224},{32,0},{64,32},{96,64},{128,96},{160,128},{192,160},{224,1... | collective-permute-start | bytes 786440 | tf_op jit(solution)/shard_map/ppermute | solution.py:34
  67.4 15.4 %collective-permute-start.8 = (bf16[64,2048]{1,0:T(8,128)(2,1)S(1)}, bf16[64,2048]{1,0:T(8,128)(2,1)S(1)}, u32[]{:S(2)}, u32[]{:S(2)}) collective-permute-start(bf16[64,2048]{1,0:T(8,128)(2,1)S(1)} %collective-permute-done.6), channel_id=1, source_target_pairs={{0,32},{32,64},{64,96},{96,128},{128,160},{160,192},{192,224},{224... | collective-permute-start | bytes 786440 | tf_op jit(solution)/shard_map/ppermute | solution.py:34
  88.3 3.8 %collective-permute-start.9 = (f32[256,384]{1,0:T(8,128)}, f32[256,384]{1,0:T(8,128)S(1)}, u32[]{:S(2)}, u32[]{:S(2)}) collective-permute-start(f32[256,384]{1,0:T(8,128)} %get-tuple-element.24), channel_id=1, source_target_pairs={{0,1},{1,0},{2,3},{3,2},{4,5},{5,4},{6,7},{7,6},{8,9},{9,8},{10,11... | collective-permute-start | bytes 1179656 | tf_op jit(solution)/shard_map/ppermute | solution.py:22
  93.9 16.7 %all-to-all-start.1 = ((f32[16,16,384]{2,1,0:T(8,128)}), f32[16,16,384]{2,1,0:T(8,128)S(1)}, u32[]{:S(2)}, u32[]{:S(2)}) async-start(f32[16,16,384]{2,1,0:T(8,128)} %bitcast.16), calls=%async_computation.1 | async-start | bytes 786432 | tf_op jit(solution)/shard_map/all_to_all | solution.py:26
  98.8 17.5 %copy-start.7 = (f32[8,48]{1,0:T(8,128)S(1)}, f32[8,48]{1,0:T(8,128)}, u32[]{:S(2)}) copy-start(f32[8,48]{1,0:T(8,128)} %param.9) | copy-start | bytes 4612
  103.0 3.8 %collective-permute-start.2 = (f32[256,384]{1,0:T(8,128)}, f32[256,384]{1,0:T(8,128)S(1)}, u32[]{:S(2)}, u32[]{:S(2)}) collective-permute-start(f32[256,384]{1,0:T(8,128)} %get-tuple-element.21), channel_id=1, source_target_pairs={{0,1},{1,0},{2,3},{3,2},{4,5},{5,4},{6,7},{7,6},{8,9},{9,8},{10,11... | collective-permute-start | bytes 1179656 | tf_op jit(solution)/shard_map/ppermute | solution.py:22
  106.8 57.7 %copy-start.6 = (s32[1,48,16,2]{1,3,2,0:T(2,128)S(1)}, s32[1,48,16,2]{1,3,2,0:T(2,128)}, u32[]{:S(2)}) copy-start(s32[1,48,16,2]{1,3,2,0:T(2,128)} %param.10) | copy-start | bytes 18436
  106.8 59.3 %copy-start.2 = (bf16[8,64,2048]{2,1,0:T(8,128)(2,1)S(1)}, bf16[8,64,2048]{2,1,0:T(8,128)(2,1)}, u32[]{:S(2)}) copy-start(bf16[8,64,2048]{2,1,0:T(8,128)(2,1)} %copy-done.1) | copy-start | bytes 6291460
  110.5 17.4 %all-to-all-start = ((f32[16,16,384]{2,1,0:T(8,128)}), f32[16,16,384]{2,1,0:T(8,128)S(1)}, u32[]{:S(2)}, u32[]{:S(2)}) async-start(f32[16,16,384]{2,1,0:T(8,128)} %bitcast.5), calls=%async_computation | async-start | bytes 786432 | tf_op jit(solution)/shard_map/all_to_all | solution.py:26
  162.5 3.6 %collective-permute-start.10 = (bf16[16,2,16,384]{3,2,1,0:T(8,128)(2,1)S(1)}, bf16[16,2,16,384]{3,2,1,0:T(8,128)(2,1)S(1)}, u32[]{:S(2)}, u32[]{:S(2)}) collective-permute-start(bf16[16,2,16,384]{3,2,1,0:T(8,128)(2,1)S(1)} %all_to_all.26.mine_ref), channel_id=1, source_target_pairs={{0,1},{1,0},{2,3},{3,2},{4,5},{5,4},{6,7},{7,6},{8,9},{9,8},{10,11... | collective-permute-start | bytes 1179656 | tf_op jit(solution)/shard_map/ppermute | solution.py:22
  172.9 16.9 %collective-permute-start.11 = (bf16[768,1024]{1,0:T(8,128)(2,1)S(1)}, bf16[768,1024]{1,0:T(8,128)(2,1)S(1)}, u32[]{:S(2)}, u32[]{:S(2)}) collective-permute-start(bf16[768,1024]{1,0:T(8,128)(2,1)S(1)} %shard_map.67), channel_id=1, source_target_pairs={{0,1},{1,0},{2,3},{3,2},{4,5},{5,4},{6,7},{7,6},{8,9},{9,8},{10,11... | collective-permute-start | bytes 4718600 | tf_op jit(solution)/shard_map/ppermute | solution.py:22
  174.9 4.0 %collective-permute-start.12 = (bf16[256,1024]{1,0:T(8,128)(2,1)S(1)}, bf16[256,1024]{1,0:T(8,128)(2,1)S(1)}, u32[]{:S(2)}, u32[]{:S(2)}) collective-permute-start(bf16[256,1024]{1,0:T(8,128)(2,1)S(1)} %get-tuple-element.26), channel_id=1, source_target_pairs={{0,1},{1,0},{2,3},{3,2},{4,5},{5,4},{6,7},{7,6},{8,9},{9,8},{10,11... | collective-permute-start | bytes 1572872 | tf_op jit(solution)/shard_map/ppermute | solution.py:22
  179.5 10.3 %collective-permute-start.13 = (bf16[256,512]{1,0:T(8,128)(2,1)S(1)}, bf16[256,512]{1,0:T(8,128)(2,1)S(1)}, u32[]{:S(2)}, u32[]{:S(2)}) collective-permute-start(bf16[256,512]{1,0:T(8,128)(2,1)S(1)} %get-tuple-element.27), channel_id=1, source_target_pairs={{0,8},{8,16},{16,24},{24,0},{1,9},{9,17},{17,25},{25,1},{2,10},{10... | collective-permute-start | bytes 786440 | tf_op jit(solution)/shard_map/ppermute | solution.py:34
  183.8 12.1 %collective-permute-start.15 = (bf16[256,512]{1,0:T(8,128)(2,1)S(1)}, bf16[256,512]{1,0:T(8,128)(2,1)S(1)}, u32[]{:S(2)}, u32[]{:S(2)}) collective-permute-start(bf16[256,512]{1,0:T(8,128)(2,1)S(1)} %get-tuple-element.28), channel_id=1, source_target_pairs={{0,24},{8,0},{16,8},{24,16},{1,25},{9,1},{17,9},{25,17},{2,26},{10... | collective-permute-start | bytes 786440 | tf_op jit(solution)/shard_map/ppermute | solution.py:34
  190.4 16.2 %collective-permute-start.14 = (bf16[256,1024]{1,0:T(8,128)(2,1)S(1)}, bf16[256,1024]{1,0:T(8,128)(2,1)S(1)}, u32[]{:S(2)}, u32[]{:S(2)}) collective-permute-start(bf16[256,1024]{1,0:T(8,128)(2,1)S(1)} %shard_map.70), channel_id=1, source_target_pairs={{0,8},{8,16},{16,24},{24,0},{1,9},{9,17},{17,25},{25,1},{2,10},{10... | collective-permute-start | bytes 1572872 | tf_op jit(solution)/shard_map/ppermute | solution.py:34
  196.5 16.0 %collective-permute-start.16 = (bf16[256,1024]{1,0:T(8,128)(2,1)S(1)}, bf16[256,1024]{1,0:T(8,128)(2,1)S(1)}, u32[]{:S(2)}, u32[]{:S(2)}) collective-permute-start(bf16[256,1024]{1,0:T(8,128)(2,1)S(1)} %shard_map.71), channel_id=1, source_target_pairs={{0,24},{8,0},{16,8},{24,16},{1,25},{9,1},{17,9},{25,17},{2,26},{10... | collective-permute-start | bytes 1572872 | tf_op jit(solution)/shard_map/ppermute | solution.py:34
  (4 other events, 24.4 us)
Sparse Core Ops, SparseCore 0:
  42.0 44.1 all-gather.2

commit v6 on v4

--- a/solution.py
+++ b/solution.py
@@ -32,23 +32,55 @@
     return lax.ppermute(block, axis, [(i, (i + step) % count) for i in range(count)])
 
 
-def ring_gathered(block):
-    count = 8
-    z = lax.axis_index("z")
-    held = jnp.zeros((count,) + block.shape, block.dtype)
-    held = lax.dynamic_update_index_in_dim(held, block, z, 0)
+STEPS = (0, 1, -1, 2, -2, 3, -3, 4)
+
+
+def ring_gathered(block, held_back):
+    got = [block]
     up = down = block
-    for step in range(1, count // 2 + 1):
+    for step in range(1, 5):
+        if step == 2:
+            up, held_back = lax.optimization_barrier((up, held_back))
         up = turned(up, 1)
-        held = lax.dynamic_update_index_in_dim(held, up, (z - step) % count, 0)
-        if step < count // 2:
+        got.append(up)
+        if step < 4:
             down = turned(down, -1)
-            held = lax.dynamic_update_index_in_dim(held, down, (z + step) % count, 0)
-    return held
+            got.append(down)
+    return got, held_back
 
 
 def kernel_params():
     return pltpu.CompilerParams(vmem_limit_bytes=24 * 2**20)
+
+
+def ring_score_kernel(core_ref, z_ref, *refs):
+    blocks, (weighted_ref, penalty_ref, far_ref, near_ref, plane_ref) = refs[:-5], refs[-5:]
+    rows = blocks[0].shape[0]
+    for step, block_ref in zip(STEPS, blocks):
+        owner = lax.rem(z_ref[0] + 8 - step, 8)
+        plane_ref[pl.ds(pl.multiple_of(owner * rows, rows), rows), :] = block_ref[...]
+    score_kernel(core_ref, plane_ref, weighted_ref, penalty_ref, far_ref, near_ref)
+
+
+def ring_scored(core, z, blocks, weighted, penalty):
+    rows, pixels = blocks[0].shape
+    rows *= len(blocks)
+    columns = weighted.shape[0]
+    side = jax.ShapeDtypeStruct((rows // 2, columns), f32)
+    whole = pl.BlockSpec(memory_space=pltpu.VMEM)
+    one = pl.BlockSpec(memory_space=pltpu.SMEM)
+    return pl.pallas_call(
+        ring_score_kernel,
+        out_shape=(side, side, jax.ShapeDtypeStruct((rows, pixels), bf16)),
+        in_specs=[one, one] + [whole] * (len(blocks) + 2),
+        out_specs=(whole, whole, whole),
+        compiler_params=kernel_params(),
+        cost_estimate=pl.CostEstimate(
+            flops=2 * rows * pixels * columns,
+            bytes_accessed=2 * pixels * (2 * rows + columns) + 4 * rows * columns,
+            transcendentals=0,
+        ),
+    )(core, z, *blocks, weighted, penalty)
 
 
 def score_kernel(core_ref, image_ref, weighted_ref, penalty_ref, far_ref, near_ref):
@@ -214,8 +246,8 @@
     slot = ((((owner % 2) ^ core) * 4 + ahead) * 4 + owner // 2 % 4) * voxels + voxel
 
     other = swapped(images, "yh")
+    ring, other = ring_gathered(images, other)
     other_plane = lax.all_gather(other, "z", axis=0).reshape(plane_rows, pixels)
-    own_plane = ring_gathered(images).reshape(plane_rows, pixels)
 
     widened = projections.astype(f32)
     product = widened * noise_weight[None, None, :]
@@ -223,12 +255,15 @@
     penalty = (-0.5 * jnp.sum(widened * product, axis=2)).reshape(1, columns)
     prior = prior_score.reshape(columns)
 
-    def plane_scores(stored):
-        far, near = scored(core_one, stored, weighted, penalty)
+    def summed_scores(far, near):
         summed = (near + swapped(far, "core")).reshape(half, share, columns)
         return jnp.sum(exchanged(summed, ("x", "yl")), axis=0) + prior[None, :]
 
-    scores = jnp.stack([plane_scores(other_plane), plane_scores(own_plane)])
+    z_one = lax.axis_index("z").reshape(1)
+    far, near, own_plane = ring_scored(core_one, z_one, ring, weighted, penalty)
+    own_scores = summed_scores(far, near)
+    other_scores = summed_scores(*scored(core_one, other_plane, weighted, penalty))
+    scores = jnp.stack([other_scores, own_scores])
     peak = jnp.max(scores, axis=2)
     mass = jnp.sum(jnp.exp(scores - peak[:, :, None]), axis=2)
     stats = jnp.stack([peak, mass])

time: 225 us -> 241 us (1.071)
  waiting for transfers between devices: 56.4 us -> 72.2 us
  starting transfers between devices: 67.9 us -> 72.9 us
  local copies, waits for them, and re-layouts: 10.5 us -> 6.05 us
    ppermute x10, waiting for transfers between devices: 32.6 us -> 45.7 us  [turned(): lax.ppermute(block, axis, [(i, (i + step) % count) for i in range(count)])]
    dynamic_update_slice x8 -> x0, local copies, waits for them, and re-layouts: 5.77 us -> none  [the longest x4 2.87 us: ring_gathered(): held = lax.dynamic_update_index_in_dim(held, up, (z - step) % count, 0)]
    all_to_all x2, starting transfers between devices: 14.4 us -> 18.3 us  [exchanged(): return lax.all_to_all(value, axis, 0, 0, tiled=True)]
    unnamed x14 -> x18, local copies, waits for them, and re-layouts: 2.32 us -> 5.2 us
    pallas_call x2 -> x1, Pallas kernels: 4.12 us -> 1.25 us  [scored(): pl.pallas_call(score_kernel, out_shape=(side, side), in_specs=[pl.BlockSp...]
    ppermute x5, waiting for transfers between devices: 8.75 us -> 11.4 us  [swapped(): return lax.ppermute(value, axis, [(0, 1), (1, 0)])]
  transfers between devices with their start and end apart: 18 -> 18, of which waited for: 14 -> 15; matrix products, arithmetic and copies ran while one was open for 5% -> 2% of each run, Pallas kernels for 3% -> 2%
where the time goes in v6:
time: 241 us; the launch traced here: 238 us
  starting transfers between devices  72.9 us (30%)
  waiting for transfers between devices  72.2 us (30%)
  blocking collectives  57 us (24%)
  between operations  13.7 us (6%)
  Pallas kernels  10.8 us (4%)
  local copies, waits for them, and re-layouts  6.05 us (3%)
  other arithmetic  4.68 us (2%)
    all_to_all x3, blocking collectives, exchanged(): return lax.all_to_all(value, axis, 0, 0, tiled=True)  57 us
    ppermute x10, waiting for transfers between devices, turned(): lax.ppermute(block, axis, [(i, (i + step) % count) for i in range(count)])  45.7 us
    ppermute x10, starting transfers between devices, turned(): lax.ppermute(block, axis, [(i, (i + step) % count) for i in range(count)])  39.1 us
    all_to_all x2, starting transfers between devices, exchanged(): return lax.all_to_all(value, axis, 0, 0, tiled=True)  18.3 us
    ppermute x5, starting transfers between devices, swapped(): return lax.ppermute(value, axis, [(0, 1), (1, 0)])  15.5 us
    all_to_all x2, waiting for transfers between devices, exchanged(): return lax.all_to_all(value, axis, 0, 0, tiled=True)  15.1 us
    ppermute x5, waiting for transfers between devices, swapped(): return lax.ppermute(value, axis, [(0, 1), (1, 0)])  11.4 us
    unnamed x18, local copies, waits for them, and re-layouts  5.2 us
  transfers between devices with their start and end apart: 18, of which 15 were waited for; matrix products, arithmetic and copies ran while one was open for 2% of the time, Pallas kernels for 2%

profile of v6, /device:TPU:6, one launch (start us, length us, event | category | flops | bytes accessed | tf_op | source)
XLA Modules:
  0.0 238.0 jit_solution(6355820499242943554)
XLA Ops:
  6.5 4.4 %collective-permute-start = (bf16[64,2048]{1,0:T(8,128)(2,1)}, bf16[64,2048]{1,0:T(8,128)(2,1)S(1)}, u32[]{:S(2)}, u32[]{:S(2)}) collective-permute-start(bf16[64,2048]{1,0:T(8,128)(2,1)} %refs_0_.1), channel_id=1, source_target_pairs={{0,32},{32,64},{64,96},{96,128},{128,160},{160,192},{192,224},{224... | collective-permute-start | bytes 786440 | tf_op jit(solution)/shard_map/ppermute | solution.py:32
  10.9 7.7 %collective-permute-start.1 = (bf16[64,2048]{1,0:T(8,128)(2,1)}, bf16[64,2048]{1,0:T(8,128)(2,1)S(1)}, u32[]{:S(2)}, u32[]{:S(2)}) collective-permute-start(bf16[64,2048]{1,0:T(8,128)(2,1)} %refs_0_.1), channel_id=1, source_target_pairs={{0,256},{256,0},{1,257},{257,1},{2,258},{258,2},{3,259},{259,3},{4... | collective-permute-start | bytes 786440 | tf_op jit(solution)/shard_map/ppermute | solution.py:20
  18.7 5.4 %collective-permute-done.refs_1_ = bf16[64,2048]{1,0:T(8,128)(2,1)S(1)} collective-permute-done((bf16[64,2048]{1,0:T(8,128)(2,1)}, bf16[64,2048]{1,0:T(8,128)(2,1)S(1)}, u32[]{:S(2)}, u32[]{:S(2)}) %collective-permute-start) | collective-permute-done | bytes 262176 | tf_op jit(solution)/shard_map/ppermute | solution.py:32
  24.1 2.6 %collective-permute-done.1 = bf16[64,2048]{1,0:T(8,128)(2,1)S(1)} collective-permute-done((bf16[64,2048]{1,0:T(8,128)(2,1)}, bf16[64,2048]{1,0:T(8,128)(2,1)S(1)}, u32[]{:S(2)}, u32[]{:S(2)}) %collective-permute-start.1) | collective-permute-done | bytes 262176 | tf_op jit(solution)/shard_map/ppermute | solution.py:20
  27.5 8.9 %collective-permute-start.3 = (bf16[64,2048]{1,0:T(8,128)(2,1)}, bf16[64,2048]{1,0:T(8,128)(2,1)S(1)}, u32[]{:S(2)}, u32[]{:S(2)}) collective-permute-start(bf16[64,2048]{1,0:T(8,128)(2,1)} %refs_0_.1), channel_id=1, source_target_pairs={{0,224},{32,0},{64,32},{96,64},{128,96},{160,128},{192,160},{224,1... | collective-permute-start | bytes 786440 | tf_op jit(solution)/shard_map/ppermute | solution.py:32
  38.3 3.1 %collective-permute-done.3.refs_2_ = bf16[64,2048]{1,0:T(8,128)(2,1)S(1)} collective-permute-done((bf16[64,2048]{1,0:T(8,128)(2,1)}, bf16[64,2048]{1,0:T(8,128)(2,1)S(1)}, u32[]{:S(2)}, u32[]{:S(2)}) %collective-permute-start.3) | collective-permute-done | bytes 262176 | tf_op jit(solution)/shard_map/ppermute | solution.py:32
  41.4 5.5 %collective-permute-start.5 = (bf16[64,2048]{1,0:T(8,128)(2,1)S(1)}, bf16[64,2048]{1,0:T(8,128)(2,1)S(1)}, u32[]{:S(2)}, u32[]{:S(2)}) collective-permute-start(bf16[64,2048]{1,0:T(8,128)(2,1)S(1)} %collective-permute-done.3.refs_2_), channel_id=1, source_target_pairs={{0,224},{32,0},{64,32},{96,64},{128,96},{160,128},{192,160},{224,1... | collective-permute-start | bytes 786440 | tf_op jit(solution)/shard_map/ppermute | solution.py:32
  48.8 4.8 %collective-permute-done.5.refs_4_ = bf16[64,2048]{1,0:T(8,128)(2,1)S(1)} collective-permute-done((bf16[64,2048]{1,0:T(8,128)(2,1)S(1)}, bf16[64,2048]{1,0:T(8,128)(2,1)S(1)}, u32[]{:S(2)}, u32[]{:S(2)}) %collective-permute-start.5) | collective-permute-done | bytes 262176 | tf_op jit(solution)/shard_map/ppermute | solution.py:32
  53.6 5.6 %collective-permute-start.7 = (bf16[64,2048]{1,0:T(8,128)(2,1)S(1)}, bf16[64,2048]{1,0:T(8,128)(2,1)S(1)}, u32[]{:S(2)}, u32[]{:S(2)}) collective-permute-start(bf16[64,2048]{1,0:T(8,128)(2,1)S(1)} %collective-permute-done.5.refs_4_), channel_id=1, source_target_pairs={{0,224},{32,0},{64,32},{96,64},{128,96},{160,128},{192,160},{224,1... | collective-permute-start | bytes 786440 | tf_op jit(solution)/shard_map/ppermute | solution.py:32
  59.2 3.6 %collective-permute-done.6.refs_5_ = bf16[64,2048]{1,0:T(8,128)(2,1)S(1)} collective-permute-done((bf16[64,2048]{1,0:T(8,128)(2,1)S(1)}, bf16[64,2048]{1,0:T(8,128)(2,1)S(1)}, u32[]{:S(2)}, u32[]{:S(2)}) %collective-permute-start.6) | collective-permute-done | bytes 262176 | tf_op jit(solution)/shard_map/ppermute | solution.py:32
  66.8 10.9 %collective-permute-done.8.refs_7_ = bf16[64,2048]{1,0:T(8,128)(2,1)} collective-permute-done((bf16[64,2048]{1,0:T(8,128)(2,1)S(1)}, bf16[64,2048]{1,0:T(8,128)(2,1)}, u32[]{:S(2)}, u32[]{:S(2)}) %collective-permute-start.8) | collective-permute-done | bytes 262176 | tf_op jit(solution)/shard_map/ppermute | solution.py:32
  85.7 12.5 %all-to-all-start.1 = ((f32[16,16,384]{2,1,0:T(8,128)}), f32[16,16,384]{2,1,0:T(8,128)S(1)}, u32[]{:S(2)}, u32[]{:S(2)}) async-start(f32[16,16,384]{2,1,0:T(8,128)} %bitcast.8), calls=%async_computation.1 | async-start | bytes 786432 | tf_op jit(solution)/shard_map/all_to_all | solution.py:24
  105.5 4.4 %all-to-all-done.1 = f32[16,16,384]{2,1,0:T(8,128)S(1)} async-done(((f32[16,16,384]{2,1,0:T(8,128)}), f32[16,16,384]{2,1,0:T(8,128)S(1)}, u32[]{:S(2)}, u32[]{:S(2)}) %all-to-all-start.1) | async-done | bytes 393248 | tf_op jit(solution)/shard_map/all_to_all | solution.py:24
  109.9 5.8 %all-to-all-start = ((f32[16,16,384]{2,1,0:T(8,128)}), f32[16,16,384]{2,1,0:T(8,128)S(1)}, u32[]{:S(2)}, u32[]{:S(2)}) async-start(f32[16,16,384]{2,1,0:T(8,128)} %bitcast.5), calls=%async_computation | async-start | bytes 786432 | tf_op jit(solution)/shard_map/all_to_all | solution.py:24
  115.8 10.6 %all-to-all-done = f32[16,16,384]{2,1,0:T(8,128)S(1)} async-done(((f32[16,16,384]{2,1,0:T(8,128)}), f32[16,16,384]{2,1,0:T(8,128)S(1)}, u32[]{:S(2)}, u32[]{:S(2)}) %all-to-all-start) | async-done | bytes 393248 | tf_op jit(solution)/shard_map/all_to_all | solution.py:24
  126.9 19.5 %all_to_all.25 = f32[16,2,32]{2,1,0:T(2,128)S(1)} all-to-all(f32[16,2,32]{2,1,0:T(2,128)S(1)} %broadcast_in_dim.9), channel_id=1, replica_groups=mesh['yh'=2,'z'=8,'x'=4,'yl'=4,'core'=2] {'yh','z'}, dimensions={0} | all-to-all | bytes 8192 | tf_op jit(solution)/shard_map/all_to_all | solution.py:24
  146.7 14.5 %all_to_all.26.mine_ref = bf16[16,2,16,384]{3,2,1,0:T(8,128)(2,1)S(1)} all-to-all(bf16[16,2,16,384]{3,2,1,0:T(8,128)(2,1)S(1)} %broadcast_in_dim.10), channel_id=1, replica_groups=mesh['yh'=2,'z'=8,'x'=4,'yl'=4,'core'=2] {'x','yl'}, dimensions={0} | all-to-all | bytes 786432 | tf_op jit(solution)/shard_map/all_to_all | solution.py:24
  166.4 5.0 %shard_map.66 = (bf16[768,1024]{1,0:T(8,128)(2,1)S(1)}, bf16[1024,1024]{1,0:T(8,128)(2,1)S(1)}) custom-call(s32[1]{0:T(128)} %bitcast.3.core_ref, bf16[16,2,16,384]{3,2,1,0:T(8,128)(2,1)S(1)} %all_to_all.26.mine_ref, bf16[16,2,16,384]{3,2,1,0:T(8,128)(2,1)S(1)} %collective-permute-done.10.twin_ref, bf16[512,2048]{1,0:T(8,128)(2,1)S(1)} %copy-done.2, ...), custom_call_target="tpu_custom_call" | custom-call | flops 3221225472 | bytes 7864320 | tf_op jit(solution)/shard_map/pallas_call | solution.py:173
  173.4 4.0 %collective-permute-done.11.got_ref = bf16[1024,1024]{1,0:T(8,128)(2,1)S(1)} collective-permute-done((bf16[1024,1024]{1,0:T(8,128)(2,1)S(1)}, bf16[1024,1024]{1,0:T(8,128)(2,1)S(1)}, u32[]{:S(2)}, u32[]{:S(2)}) %collective-permute-start.11) | collective-permute-done | bytes 2097184 | tf_op jit(solution)/shard_map/ppermute | solution.py:20
  178.0 3.1 %collective-permute-start.12 = (bf16[256,1024]{1,0:T(8,128)(2,1)S(1)}, bf16[256,1024]{1,0:T(8,128)(2,1)S(1)}, u32[]{:S(2)}, u32[]{:S(2)}) collective-permute-start(bf16[256,1024]{1,0:T(8,128)(2,1)S(1)} %shard_map.68), channel_id=1, source_target_pairs={{0,16},{8,24},{16,0},{24,8},{1,17},{9,25},{17,1},{25,9},{2,18},{10... | collective-permute-start | bytes 1572872 | tf_op jit(solution)/shard_map/ppermute | solution.py:32
  181.7 4.0 %collective-permute-start.13 = (bf16[256,1024]{1,0:T(8,128)(2,1)S(1)}, bf16[256,1024]{1,0:T(8,128)(2,1)S(1)}, u32[]{:S(2)}, u32[]{:S(2)}) collective-permute-start(bf16[256,1024]{1,0:T(8,128)(2,1)S(1)} %shard_map.69), channel_id=1, source_target_pairs={{0,8},{8,16},{16,24},{24,0},{1,9},{9,17},{17,25},{25,1},{2,10},{10... | collective-permute-start | bytes 1572872 | tf_op jit(solution)/shard_map/ppermute | solution.py:32
  188.8 7.4 %collective-permute-done.12 = bf16[256,1024]{1,0:T(8,128)(2,1)S(1)} collective-permute-done((bf16[256,1024]{1,0:T(8,128)(2,1)S(1)}, bf16[256,1024]{1,0:T(8,128)(2,1)S(1)}, u32[]{:S(2)}, u32[]{:S(2)}) %collective-permute-start.12) | collective-permute-done | bytes 524320 | tf_op jit(solution)/shard_map/ppermute | solution.py:32
  196.2 10.1 %collective-permute-done.13 = bf16[256,1024]{1,0:T(8,128)(2,1)S(1)} collective-permute-done((bf16[256,1024]{1,0:T(8,128)(2,1)S(1)}, bf16[256,1024]{1,0:T(8,128)(2,1)S(1)}, u32[]{:S(2)}, u32[]{:S(2)}) %collective-permute-start.13) | collective-permute-done | bytes 524320 | tf_op jit(solution)/shard_map/ppermute | solution.py:32
  207.2 23.0 %all_to_all.27 = bf16[64,4,1024]{2,1,0:T(4,128)(2,1)S(1)} all-to-all(bf16[64,4,1024]{2,1,0:T(4,128)(2,1)S(1)} %reshape.464), channel_id=1, replica_groups=mesh['yh'=2,'z'=8,'x'=4,'yl'=4,'core'=2] {'yl','yh','z'}, dimensions={0} | all-to-all | bytes 1048576 | tf_op jit(solution)/shard_map/all_to_all | solution.py:24
  (74 shorter events, 37.9 us)
Async XLA Ops:
  6.5 223.9 %copy-start = (bf16[1,4,128,128]{3,2,1,0:T(8,128)(2,1)S(1)}, bf16[1,4,128,128]{3,2,1,0:T(8,128)(2,1)}, u32[]{:S(2)}) copy-start(bf16[1,4,128,128]{3,2,1,0:T(8,128)(2,1)} %param.11) | copy-start | bytes 393220
  6.5 71.2 %copy-start.3 = (bf16[64,2048]{1,0:T(8,128)(2,1)S(1)}, bf16[64,2048]{1,0:T(8,128)(2,1)}, u32[]{:S(2)}) copy-start(bf16[64,2048]{1,0:T(8,128)(2,1)} %refs_0_.1) | copy-start | bytes 786436
  6.5 91.7 %all-gather.3.cloned.1.call-start = ((), (), s32[]{:S(2)}) async-start(), calls=%async_computation.5 | async-start | bytes 2359296 | tf_op jit(solution)/shard_map/all_gather | solution.py:250
  6.5 17.6 %collective-permute-start = (bf16[64,2048]{1,0:T(8,128)(2,1)}, bf16[64,2048]{1,0:T(8,128)(2,1)S(1)}, u32[]{:S(2)}, u32[]{:S(2)}) collective-permute-start(bf16[64,2048]{1,0:T(8,128)(2,1)} %refs_0_.1), channel_id=1, source_target_pairs={{0,32},{32,64},{64,96},{96,128},{128,160},{160,192},{192,224},{224... | collective-permute-start | bytes 786440 | tf_op jit(solution)/shard_map/ppermute | solution.py:32
  10.9 15.8 %collective-permute-start.1 = (bf16[64,2048]{1,0:T(8,128)(2,1)}, bf16[64,2048]{1,0:T(8,128)(2,1)S(1)}, u32[]{:S(2)}, u32[]{:S(2)}) collective-permute-start(bf16[64,2048]{1,0:T(8,128)(2,1)} %refs_0_.1), channel_id=1, source_target_pairs={{0,256},{256,0},{1,257},{257,1},{2,258},{258,2},{3,259},{259,3},{4... | collective-permute-start | bytes 786440 | tf_op jit(solution)/shard_map/ppermute | solution.py:20
  27.5 13.9 %collective-permute-start.3 = (bf16[64,2048]{1,0:T(8,128)(2,1)}, bf16[64,2048]{1,0:T(8,128)(2,1)S(1)}, u32[]{:S(2)}, u32[]{:S(2)}) collective-permute-start(bf16[64,2048]{1,0:T(8,128)(2,1)} %refs_0_.1), channel_id=1, source_target_pairs={{0,224},{32,0},{64,32},{96,64},{128,96},{160,128},{192,160},{224,1... | collective-permute-start | bytes 786440 | tf_op jit(solution)/shard_map/ppermute | solution.py:32
  36.3 10.5 %collective-permute-start.4 = (bf16[64,2048]{1,0:T(8,128)(2,1)S(1)}, bf16[64,2048]{1,0:T(8,128)(2,1)S(1)}, u32[]{:S(2)}, u32[]{:S(2)}) collective-permute-start(bf16[64,2048]{1,0:T(8,128)(2,1)S(1)} %collective-permute-done.refs_1_), channel_id=1, source_target_pairs={{0,32},{32,64},{64,96},{96,128},{128,160},{160,192},{192,224},{224... | collective-permute-start | bytes 786440 | tf_op jit(solution)/shard_map/ppermute | solution.py:32
  41.4 12.3 %collective-permute-start.5 = (bf16[64,2048]{1,0:T(8,128)(2,1)S(1)}, bf16[64,2048]{1,0:T(8,128)(2,1)S(1)}, u32[]{:S(2)}, u32[]{:S(2)}) collective-permute-start(bf16[64,2048]{1,0:T(8,128)(2,1)S(1)} %collective-permute-done.3.refs_2_), channel_id=1, source_target_pairs={{0,224},{32,0},{64,32},{96,64},{128,96},{160,128},{192,160},{224,1... | collective-permute-start | bytes 786440 | tf_op jit(solution)/shard_map/ppermute | solution.py:32
  46.9 15.9 %collective-permute-start.6 = (bf16[64,2048]{1,0:T(8,128)(2,1)S(1)}, bf16[64,2048]{1,0:T(8,128)(2,1)S(1)}, u32[]{:S(2)}, u32[]{:S(2)}) collective-permute-start(bf16[64,2048]{1,0:T(8,128)(2,1)S(1)} %collective-permute-done.4.refs_3_), channel_id=1, source_target_pairs={{0,32},{32,64},{64,96},{96,128},{128,160},{160,192},{192,224},{224... | collective-permute-start | bytes 786440 | tf_op jit(solution)/shard_map/ppermute | solution.py:32
  53.6 13.1 %collective-permute-start.7 = (bf16[64,2048]{1,0:T(8,128)(2,1)S(1)}, bf16[64,2048]{1,0:T(8,128)(2,1)S(1)}, u32[]{:S(2)}, u32[]{:S(2)}) collective-permute-start(bf16[64,2048]{1,0:T(8,128)(2,1)S(1)} %collective-permute-done.5.refs_4_), channel_id=1, source_target_pairs={{0,224},{32,0},{64,32},{96,64},{128,96},{160,128},{192,160},{224,1... | collective-permute-start | bytes 786440 | tf_op jit(solution)/shard_map/ppermute | solution.py:32
  62.8 14.9 %collective-permute-start.8 = (bf16[64,2048]{1,0:T(8,128)(2,1)S(1)}, bf16[64,2048]{1,0:T(8,128)(2,1)}, u32[]{:S(2)}, u32[]{:S(2)}) collective-permute-start(bf16[64,2048]{1,0:T(8,128)(2,1)S(1)} %collective-permute-done.6.refs_5_), channel_id=1, source_target_pairs={{0,32},{32,64},{64,96},{96,128},{128,160},{160,192},{192,224},{224... | collective-permute-start | bytes 786440 | tf_op jit(solution)/shard_map/ppermute | solution.py:32
  81.3 3.6 %collective-permute-start.9 = (f32[256,384]{1,0:T(8,128)S(1)}, f32[256,384]{1,0:T(8,128)S(1)}, u32[]{:S(2)}, u32[]{:S(2)}) collective-permute-start(f32[256,384]{1,0:T(8,128)S(1)} %get-tuple-element.19), channel_id=1, source_target_pairs={{0,1},{1,0},{2,3},{3,2},{4,5},{5,4},{6,7},{7,6},{8,9},{9,8},{10,11... | collective-permute-start | bytes 1179656 | tf_op jit(solution)/shard_map/ppermute | solution.py:20
  85.7 24.2 %all-to-all-start.1 = ((f32[16,16,384]{2,1,0:T(8,128)}), f32[16,16,384]{2,1,0:T(8,128)S(1)}, u32[]{:S(2)}, u32[]{:S(2)}) async-start(f32[16,16,384]{2,1,0:T(8,128)} %bitcast.8), calls=%async_computation.1 | async-start | bytes 786432 | tf_op jit(solution)/shard_map/all_to_all | solution.py:24
  98.2 1.6 copy-start.1
  99.8 15.9 %copy-start.8 = (f32[8,48]{1,0:T(8,128)S(1)}, f32[8,48]{1,0:T(8,128)}, u32[]{:S(2)}) copy-start(f32[8,48]{1,0:T(8,128)} %param.9) | copy-start | bytes 4612
  101.1 3.6 %collective-permute-start.2 = (f32[256,384]{1,0:T(8,128)S(1)}, f32[256,384]{1,0:T(8,128)S(1)}, u32[]{:S(2)}, u32[]{:S(2)}) collective-permute-start(f32[256,384]{1,0:T(8,128)S(1)} %get-tuple-element.16), channel_id=1, source_target_pairs={{0,1},{1,0},{2,3},{3,2},{4,5},{5,4},{6,7},{7,6},{8,9},{9,8},{10,11... | collective-permute-start | bytes 1179656 | tf_op jit(solution)/shard_map/ppermute | solution.py:20
  104.7 58.5 %copy-start.7 = (s32[1,48,16,2]{1,3,2,0:T(2,128)S(1)}, s32[1,48,16,2]{1,3,2,0:T(2,128)}, u32[]{:S(2)}) copy-start(s32[1,48,16,2]{1,3,2,0:T(2,128)} %param.10) | copy-start | bytes 18436
  104.7 60.1 %copy-start.2 = (bf16[512,2048]{1,0:T(8,128)(2,1)S(1)}, bf16[512,2048]{1,0:T(8,128)(2,1)}, u32[]{:S(2)}) copy-start(bf16[512,2048]{1,0:T(8,128)(2,1)} %all-gather.3.cloned.1.call-done.image_ref.other_ref) | copy-start | bytes 6291460
  109.9 16.6 %all-to-all-start = ((f32[16,16,384]{2,1,0:T(8,128)}), f32[16,16,384]{2,1,0:T(8,128)S(1)}, u32[]{:S(2)}, u32[]{:S(2)}) async-start(f32[16,16,384]{2,1,0:T(8,128)} %bitcast.5), calls=%async_computation | async-start | bytes 786432 | tf_op jit(solution)/shard_map/all_to_all | solution.py:24
  161.2 3.6 %collective-permute-start.10 = (bf16[16,2,16,384]{3,2,1,0:T(8,128)(2,1)S(1)}, bf16[16,2,16,384]{3,2,1,0:T(8,128)(2,1)S(1)}, u32[]{:S(2)}, u32[]{:S(2)}) collective-permute-start(bf16[16,2,16,384]{3,2,1,0:T(8,128)(2,1)S(1)} %all_to_all.26.mine_ref), channel_id=1, source_target_pairs={{0,1},{1,0},{2,3},{3,2},{4,5},{5,4},{6,7},{7,6},{8,9},{9,8},{10,11... | collective-permute-start | bytes 1179656 | tf_op jit(solution)/shard_map/ppermute | solution.py:20
  171.4 6.1 %collective-permute-start.11 = (bf16[1024,1024]{1,0:T(8,128)(2,1)S(1)}, bf16[1024,1024]{1,0:T(8,128)(2,1)S(1)}, u32[]{:S(2)}, u32[]{:S(2)}) collective-permute-start(bf16[1024,1024]{1,0:T(8,128)(2,1)S(1)} %get-tuple-element.22), channel_id=1, source_target_pairs={{0,1},{1,0},{2,3},{3,2},{4,5},{5,4},{6,7},{7,6},{8,9},{9,8},{10,11... | collective-permute-start | bytes 6291464 | tf_op jit(solution)/shard_map/ppermute | solution.py:20
  178.0 18.2 %collective-permute-start.12 = (bf16[256,1024]{1,0:T(8,128)(2,1)S(1)}, bf16[256,1024]{1,0:T(8,128)(2,1)S(1)}, u32[]{:S(2)}, u32[]{:S(2)}) collective-permute-start(bf16[256,1024]{1,0:T(8,128)(2,1)S(1)} %shard_map.68), channel_id=1, source_target_pairs={{0,16},{8,24},{16,0},{24,8},{1,17},{9,25},{17,1},{25,9},{2,18},{10... | collective-permute-start | bytes 1572872 | tf_op jit(solution)/shard_map/ppermute | solution.py:32
  181.7 24.7 %collective-permute-start.13 = (bf16[256,1024]{1,0:T(8,128)(2,1)S(1)}, bf16[256,1024]{1,0:T(8,128)(2,1)S(1)}, u32[]{:S(2)}, u32[]{:S(2)}) collective-permute-start(bf16[256,1024]{1,0:T(8,128)(2,1)S(1)} %shard_map.69), channel_id=1, source_target_pairs={{0,8},{8,16},{16,24},{24,0},{1,9},{9,17},{17,25},{25,1},{2,10},{10... | collective-permute-start | bytes 1572872 | tf_op jit(solution)/shard_map/ppermute | solution.py:32
  186.3 20.4 %collective-permute-start.14 = (bf16[256,1024]{1,0:T(8,128)(2,1)S(1)}, bf16[256,1024]{1,0:T(8,128)(2,1)S(1)}, u32[]{:S(2)}, u32[]{:S(2)}) collective-permute-start(bf16[256,1024]{1,0:T(8,128)(2,1)S(1)} %shard_map.70), channel_id=1, source_target_pairs={{0,24},{8,0},{16,8},{24,16},{1,25},{9,1},{17,9},{25,17},{2,26},{10... | collective-permute-start | bytes 1572872 | tf_op jit(solution)/shard_map/ppermute | solution.py:32
  (3 other events, 3.6 us)
Sparse Core Ops, SparseCore 0:
  27.6 55.0 all-gather.2

commit v7 on v6

--- a/solution.py
+++ b/solution.py
@@ -39,13 +39,13 @@
     got = [block]
     up = down = block
     for step in range(1, 5):
-        if step == 2:
-            up, held_back = lax.optimization_barrier((up, held_back))
         up = turned(up, 1)
         got.append(up)
         if step < 4:
             down = turned(down, -1)
             got.append(down)
+        if step == 2:
+            held_back = lax.optimization_barrier((up, down, held_back))[2]
     return got, held_back
 
 

time: 241 us -> 224 us (0.929)
  waiting for transfers between devices: 72.2 us -> 58.6 us
    ppermute x10, waiting for transfers between devices: 45.7 us -> 34 us  [turned(): lax.ppermute(block, axis, [(i, (i + step) % count) for i in range(count)])]
where the time goes in v7:
time: 224 us; the launch traced here: 221 us
  starting transfers between devices  71 us (32%)
  waiting for transfers between devices  58.6 us (26%)
  blocking collectives  55.5 us (25%)
  between operations  13.7 us (6%)
  Pallas kernels  10.9 us (5%)
  other arithmetic  5.7 us (3%)
  local copies, waits for them, and re-layouts  5.35 us (2%)
    all_to_all x3, blocking collectives, exchanged(): return lax.all_to_all(value, axis, 0, 0, tiled=True)  55.5 us
    ppermute x10, starting transfers between devices, turned(): lax.ppermute(block, axis, [(i, (i + step) % count) for i in range(count)])  38.4 us
    ppermute x10, waiting for transfers between devices, turned(): lax.ppermute(block, axis, [(i, (i + step) % count) for i in range(count)])  34 us
    all_to_all x2, starting transfers between devices, exchanged(): return lax.all_to_all(value, axis, 0, 0, tiled=True)  17 us
    ppermute x5, starting transfers between devices, swapped(): return lax.ppermute(value, axis, [(0, 1), (1, 0)])  15.5 us
    all_to_all x2, waiting for transfers between devices, exchanged(): return lax.all_to_all(value, axis, 0, 0, tiled=True)  14.2 us
    ppermute x5, waiting for transfers between devices, swapped(): return lax.ppermute(value, axis, [(0, 1), (1, 0)])  9.71 us
    pallas_call x1, Pallas kernels, sliced(): pl.pallas_call(slice_kernel, grid=(steps,), out_shape=(jax.ShapeDtypeStru...  4.96 us
  transfers between devices with their start and end apart: 18, of which 15 were waited for; matrix products, arithmetic and copies ran while one was open for 2% of the time, Pallas kernels for 2%

profile of v7, /device:TPU:6, one launch (start us, length us, event | category | flops | bytes accessed | tf_op | source)
XLA Modules:
  0.0 221.4 jit_solution(11531259441992353516)
XLA Ops:
  6.5 4.4 %collective-permute-start = (bf16[64,2048]{1,0:T(8,128)(2,1)}, bf16[64,2048]{1,0:T(8,128)(2,1)S(1)}, u32[]{:S(2)}, u32[]{:S(2)}) collective-permute-start(bf16[64,2048]{1,0:T(8,128)(2,1)} %refs_0_.1), channel_id=1, source_target_pairs={{0,32},{32,64},{64,96},{96,128},{128,160},{160,192},{192,224},{224... | collective-permute-start | bytes 786440 | tf_op jit(solution)/shard_map/ppermute | solution.py:32
  10.9 8.6 %collective-permute-start.2 = (bf16[64,2048]{1,0:T(8,128)(2,1)}, bf16[64,2048]{1,0:T(8,128)(2,1)S(1)}, u32[]{:S(2)}, u32[]{:S(2)}) collective-permute-start(bf16[64,2048]{1,0:T(8,128)(2,1)} %refs_0_.1), channel_id=1, source_target_pairs={{0,224},{32,0},{64,32},{96,64},{128,96},{160,128},{192,160},{224,1... | collective-permute-start | bytes 786440 | tf_op jit(solution)/shard_map/ppermute | solution.py:32
  19.5 7.7 %collective-permute-start.4 = (bf16[64,2048]{1,0:T(8,128)(2,1)}, bf16[64,2048]{1,0:T(8,128)(2,1)S(1)}, u32[]{:S(2)}, u32[]{:S(2)}) collective-permute-start(bf16[64,2048]{1,0:T(8,128)(2,1)} %refs_0_.1), channel_id=1, source_target_pairs={{0,256},{256,0},{1,257},{257,1},{2,258},{258,2},{3,259},{259,3},{4... | collective-permute-start | bytes 786440 | tf_op jit(solution)/shard_map/ppermute | solution.py:20
  29.2 5.1 %collective-permute-start.3 = (bf16[64,2048]{1,0:T(8,128)(2,1)S(1)}, bf16[64,2048]{1,0:T(8,128)(2,1)S(1)}, u32[]{:S(2)}, u32[]{:S(2)}) collective-permute-start(bf16[64,2048]{1,0:T(8,128)(2,1)S(1)} %collective-permute-done.2.refs_2_), channel_id=1, source_target_pairs={{0,224},{32,0},{64,32},{96,64},{128,96},{160,128},{192,160},{224,1... | collective-permute-start | bytes 786440 | tf_op jit(solution)/shard_map/ppermute | solution.py:32
  35.3 2.6 %collective-permute-done.1.refs_3_ = bf16[64,2048]{1,0:T(8,128)(2,1)S(1)} collective-permute-done((bf16[64,2048]{1,0:T(8,128)(2,1)S(1)}, bf16[64,2048]{1,0:T(8,128)(2,1)S(1)}, u32[]{:S(2)}, u32[]{:S(2)}) %collective-permute-start.1) | collective-permute-done | bytes 262176 | tf_op jit(solution)/shard_map/ppermute | solution.py:32
  41.0 5.6 %collective-permute-start.7 = (bf16[64,2048]{1,0:T(8,128)(2,1)S(1)}, bf16[64,2048]{1,0:T(8,128)(2,1)S(1)}, u32[]{:S(2)}, u32[]{:S(2)}) collective-permute-start(bf16[64,2048]{1,0:T(8,128)(2,1)S(1)} %collective-permute-done.3.refs_4_), channel_id=1, source_target_pairs={{0,224},{32,0},{64,32},{96,64},{128,96},{160,128},{192,160},{224,1... | collective-permute-start | bytes 786440 | tf_op jit(solution)/shard_map/ppermute | solution.py:32
  46.6 2.6 %collective-permute-done.6.refs_5_ = bf16[64,2048]{1,0:T(8,128)(2,1)S(1)} collective-permute-done((bf16[64,2048]{1,0:T(8,128)(2,1)S(1)}, bf16[64,2048]{1,0:T(8,128)(2,1)S(1)}, u32[]{:S(2)}, u32[]{:S(2)}) %collective-permute-start.6) | collective-permute-done | bytes 262176 | tf_op jit(solution)/shard_map/ppermute | solution.py:32
  51.2 1.9 fusion
  53.2 9.9 %collective-permute-done.8.refs_7_ = bf16[64,2048]{1,0:T(8,128)(2,1)} collective-permute-done((bf16[64,2048]{1,0:T(8,128)(2,1)S(1)}, bf16[64,2048]{1,0:T(8,128)(2,1)}, u32[]{:S(2)}, u32[]{:S(2)}) %collective-permute-start.8) | collective-permute-done | bytes 262176 | tf_op jit(solution)/shard_map/ppermute | solution.py:32
  63.1 2.3 %shard_map.65 = (f32[256,384]{1,0:T(8,128)S(1)}, f32[256,384]{1,0:T(8,128)S(1)}, bf16[512,2048]{1,0:T(8,128)(2,1)S(1)}) custom-call(s32[1]{0:T(128)} %bitcast.3.core_ref, s32[1]{0:T(128)} %bitcast.7.z_ref, bf16[64,2048]{1,0:T(8,128)(2,1)S(1)} %copy-done.3, bf16[64,2048]{1,0:T(8,128)(2,1)S(1)} %collective-permute-done.refs_1_, ...), custom_call_target="tpu_custom_call" | custom-call | flops 805306368 | bytes 6553600 | tf_op jit(solution)/shard_map/pallas_call | solution.py:72
  71.1 11.2 %all-to-all-start.1 = ((f32[16,16,384]{2,1,0:T(8,128)}), f32[16,16,384]{2,1,0:T(8,128)}, u32[]{:S(2)}, u32[]{:S(2)}) async-start(f32[16,16,384]{2,1,0:T(8,128)} %bitcast.8), calls=%async_computation.1 | async-start | bytes 786432 | tf_op jit(solution)/shard_map/all_to_all | solution.py:24
  90.3 3.9 %all-to-all-done.1 = f32[16,16,384]{2,1,0:T(8,128)} async-done(((f32[16,16,384]{2,1,0:T(8,128)}), f32[16,16,384]{2,1,0:T(8,128)}, u32[]{:S(2)}, u32[]{:S(2)}) %all-to-all-start.1) | async-done | bytes 393248 | tf_op jit(solution)/shard_map/all_to_all | solution.py:24
  94.1 5.8 %all-to-all-start = ((f32[16,16,384]{2,1,0:T(8,128)}), f32[16,16,384]{2,1,0:T(8,128)S(1)}, u32[]{:S(2)}, u32[]{:S(2)}) async-start(f32[16,16,384]{2,1,0:T(8,128)} %bitcast.5), calls=%async_computation | async-start | bytes 786432 | tf_op jit(solution)/shard_map/all_to_all | solution.py:24
  101.1 10.3 %all-to-all-done = f32[16,16,384]{2,1,0:T(8,128)S(1)} async-done(((f32[16,16,384]{2,1,0:T(8,128)}), f32[16,16,384]{2,1,0:T(8,128)S(1)}, u32[]{:S(2)}, u32[]{:S(2)}) %all-to-all-start) | async-done | bytes 393248 | tf_op jit(solution)/shard_map/all_to_all | solution.py:24
  111.8 17.6 %all_to_all.25 = f32[16,2,32]{2,1,0:T(2,128)S(1)} all-to-all(f32[16,2,32]{2,1,0:T(2,128)S(1)} %broadcast_in_dim.9), channel_id=1, replica_groups=mesh['yh'=2,'z'=8,'x'=4,'yl'=4,'core'=2] {'yh','z'}, dimensions={0} | all-to-all | bytes 8192 | tf_op jit(solution)/shard_map/all_to_all | solution.py:24
  129.7 14.9 %all_to_all.26.mine_ref = bf16[16,2,16,384]{3,2,1,0:T(8,128)(2,1)S(1)} all-to-all(bf16[16,2,16,384]{3,2,1,0:T(8,128)(2,1)S(1)} %broadcast_in_dim.10), channel_id=1, replica_groups=mesh['yh'=2,'z'=8,'x'=4,'yl'=4,'core'=2] {'x','yl'}, dimensions={0} | all-to-all | bytes 786432 | tf_op jit(solution)/shard_map/all_to_all | solution.py:24
  149.8 5.0 %shard_map.66 = (bf16[768,1024]{1,0:T(8,128)(2,1)S(1)}, bf16[1024,1024]{1,0:T(8,128)(2,1)S(1)}) custom-call(s32[1]{0:T(128)} %bitcast.3.core_ref, bf16[16,2,16,384]{3,2,1,0:T(8,128)(2,1)S(1)} %all_to_all.26.mine_ref, bf16[16,2,16,384]{3,2,1,0:T(8,128)(2,1)S(1)} %collective-permute-done.10.twin_ref, bf16[512,2048]{1,0:T(8,128)(2,1)S(1)} %copy-done.2, ...), custom_call_target="tpu_custom_call" | custom-call | flops 3221225472 | bytes 7864320 | tf_op jit(solution)/shard_map/pallas_call | solution.py:173
  154.8 2.0 collective-permute-start.11
  156.8 4.0 %collective-permute-done.11.got_ref = bf16[1024,1024]{1,0:T(8,128)(2,1)S(1)} collective-permute-done((bf16[1024,1024]{1,0:T(8,128)(2,1)S(1)}, bf16[1024,1024]{1,0:T(8,128)(2,1)S(1)}, u32[]{:S(2)}, u32[]{:S(2)}) %collective-permute-start.11) | collective-permute-done | bytes 2097184 | tf_op jit(solution)/shard_map/ppermute | solution.py:20
  161.4 3.1 %collective-permute-start.12 = (bf16[256,1024]{1,0:T(8,128)(2,1)S(1)}, bf16[256,1024]{1,0:T(8,128)(2,1)S(1)}, u32[]{:S(2)}, u32[]{:S(2)}) collective-permute-start(bf16[256,1024]{1,0:T(8,128)(2,1)S(1)} %shard_map.68), channel_id=1, source_target_pairs={{0,16},{8,24},{16,0},{24,8},{1,17},{9,25},{17,1},{25,9},{2,18},{10... | collective-permute-start | bytes 1572872 | tf_op jit(solution)/shard_map/ppermute | solution.py:32
  165.1 4.0 %collective-permute-start.13 = (bf16[256,1024]{1,0:T(8,128)(2,1)S(1)}, bf16[256,1024]{1,0:T(8,128)(2,1)S(1)}, u32[]{:S(2)}, u32[]{:S(2)}) collective-permute-start(bf16[256,1024]{1,0:T(8,128)(2,1)S(1)} %shard_map.69), channel_id=1, source_target_pairs={{0,8},{8,16},{16,24},{24,0},{1,9},{9,17},{17,25},{25,1},{2,10},{10... | collective-permute-start | bytes 1572872 | tf_op jit(solution)/shard_map/ppermute | solution.py:32
  172.2 7.4 %collective-permute-done.12 = bf16[256,1024]{1,0:T(8,128)(2,1)S(1)} collective-permute-done((bf16[256,1024]{1,0:T(8,128)(2,1)S(1)}, bf16[256,1024]{1,0:T(8,128)(2,1)S(1)}, u32[]{:S(2)}, u32[]{:S(2)}) %collective-permute-start.12) | collective-permute-done | bytes 524320 | tf_op jit(solution)/shard_map/ppermute | solution.py:32
  179.6 10.1 %collective-permute-done.13 = bf16[256,1024]{1,0:T(8,128)(2,1)S(1)} collective-permute-done((bf16[256,1024]{1,0:T(8,128)(2,1)S(1)}, bf16[256,1024]{1,0:T(8,128)(2,1)S(1)}, u32[]{:S(2)}, u32[]{:S(2)}) %collective-permute-start.13) | collective-permute-done | bytes 524320 | tf_op jit(solution)/shard_map/ppermute | solution.py:32
  190.6 23.0 %all_to_all.27 = bf16[64,4,1024]{2,1,0:T(4,128)(2,1)S(1)} all-to-all(bf16[64,4,1024]{2,1,0:T(4,128)(2,1)S(1)} %reshape.464), channel_id=1, replica_groups=mesh['yh'=2,'z'=8,'x'=4,'yl'=4,'core'=2] {'yl','yh','z'}, dimensions={0} | all-to-all | bytes 1048576 | tf_op jit(solution)/shard_map/all_to_all | solution.py:24
  (74 shorter events, 34.7 us)
Async XLA Ops:
  6.5 207.3 %copy-start = (bf16[1,4,128,128]{3,2,1,0:T(8,128)(2,1)S(1)}, bf16[1,4,128,128]{3,2,1,0:T(8,128)(2,1)}, u32[]{:S(2)}) copy-start(bf16[1,4,128,128]{3,2,1,0:T(8,128)(2,1)} %param.11) | copy-start | bytes 393220
  6.5 56.5 %copy-start.3 = (bf16[64,2048]{1,0:T(8,128)(2,1)S(1)}, bf16[64,2048]{1,0:T(8,128)(2,1)}, u32[]{:S(2)}) copy-start(bf16[64,2048]{1,0:T(8,128)(2,1)} %refs_0_.1) | copy-start | bytes 786436
  6.5 76.5 %all-gather.3.cloned.1.call-start = ((), (), s32[]{:S(2)}) async-start(), calls=%async_computation.5 | async-start | bytes 2359296 | tf_op jit(solution)/shard_map/all_gather | solution.py:250
  6.5 20.7 %collective-permute-start = (bf16[64,2048]{1,0:T(8,128)(2,1)}, bf16[64,2048]{1,0:T(8,128)(2,1)S(1)}, u32[]{:S(2)}, u32[]{:S(2)}) collective-permute-start(bf16[64,2048]{1,0:T(8,128)(2,1)} %refs_0_.1), channel_id=1, source_target_pairs={{0,32},{32,64},{64,96},{96,128},{128,160},{160,192},{192,224},{224... | collective-permute-start | bytes 786440 | tf_op jit(solution)/shard_map/ppermute | solution.py:32
  10.9 18.3 %collective-permute-start.2 = (bf16[64,2048]{1,0:T(8,128)(2,1)}, bf16[64,2048]{1,0:T(8,128)(2,1)S(1)}, u32[]{:S(2)}, u32[]{:S(2)}) collective-permute-start(bf16[64,2048]{1,0:T(8,128)(2,1)} %refs_0_.1), channel_id=1, source_target_pairs={{0,224},{32,0},{64,32},{96,64},{128,96},{160,128},{192,160},{224,1... | collective-permute-start | bytes 786440 | tf_op jit(solution)/shard_map/ppermute | solution.py:32
  19.5 15.8 %collective-permute-start.4 = (bf16[64,2048]{1,0:T(8,128)(2,1)}, bf16[64,2048]{1,0:T(8,128)(2,1)S(1)}, u32[]{:S(2)}, u32[]{:S(2)}) collective-permute-start(bf16[64,2048]{1,0:T(8,128)(2,1)} %refs_0_.1), channel_id=1, source_target_pairs={{0,256},{256,0},{1,257},{257,1},{2,258},{258,2},{3,259},{259,3},{4... | collective-permute-start | bytes 786440 | tf_op jit(solution)/shard_map/ppermute | solution.py:20
  27.3 10.6 %collective-permute-start.1 = (bf16[64,2048]{1,0:T(8,128)(2,1)S(1)}, bf16[64,2048]{1,0:T(8,128)(2,1)S(1)}, u32[]{:S(2)}, u32[]{:S(2)}) collective-permute-start(bf16[64,2048]{1,0:T(8,128)(2,1)S(1)} %collective-permute-done.refs_1_), channel_id=1, source_target_pairs={{0,32},{32,64},{64,96},{96,128},{128,160},{160,192},{192,224},{224... | collective-permute-start | bytes 786440 | tf_op jit(solution)/shard_map/ppermute | solution.py:32
  29.2 9.8 %collective-permute-start.3 = (bf16[64,2048]{1,0:T(8,128)(2,1)S(1)}, bf16[64,2048]{1,0:T(8,128)(2,1)S(1)}, u32[]{:S(2)}, u32[]{:S(2)}) collective-permute-start(bf16[64,2048]{1,0:T(8,128)(2,1)S(1)} %collective-permute-done.2.refs_2_), channel_id=1, source_target_pairs={{0,224},{32,0},{64,32},{96,64},{128,96},{160,128},{192,160},{224,1... | collective-permute-start | bytes 786440 | tf_op jit(solution)/shard_map/ppermute | solution.py:32
  35.3 3.8 %copy-start.6 = (bf16[64,2048]{1,0:T(8,128)(2,1)}, bf16[64,2048]{1,0:T(8,128)(2,1)S(1)}, u32[]{:S(2)}) copy-start(bf16[64,2048]{1,0:T(8,128)(2,1)S(1)} %collective-permute-done.4) | copy-start | bytes 786436
  39.1 10.1 %collective-permute-start.6 = (bf16[64,2048]{1,0:T(8,128)(2,1)S(1)}, bf16[64,2048]{1,0:T(8,128)(2,1)S(1)}, u32[]{:S(2)}, u32[]{:S(2)}) collective-permute-start(bf16[64,2048]{1,0:T(8,128)(2,1)S(1)} %collective-permute-done.1.refs_3_), channel_id=1, source_target_pairs={{0,32},{32,64},{64,96},{96,128},{128,160},{160,192},{192,224},{224... | collective-permute-start | bytes 786440 | tf_op jit(solution)/shard_map/ppermute | solution.py:32
  41.0 12.2 %collective-permute-start.7 = (bf16[64,2048]{1,0:T(8,128)(2,1)S(1)}, bf16[64,2048]{1,0:T(8,128)(2,1)S(1)}, u32[]{:S(2)}, u32[]{:S(2)}) collective-permute-start(bf16[64,2048]{1,0:T(8,128)(2,1)S(1)} %collective-permute-done.3.refs_4_), channel_id=1, source_target_pairs={{0,224},{32,0},{64,32},{96,64},{128,96},{160,128},{192,160},{224,1... | collective-permute-start | bytes 786440 | tf_op jit(solution)/shard_map/ppermute | solution.py:32
  49.2 13.8 %collective-permute-start.8 = (bf16[64,2048]{1,0:T(8,128)(2,1)S(1)}, bf16[64,2048]{1,0:T(8,128)(2,1)}, u32[]{:S(2)}, u32[]{:S(2)}) collective-permute-start(bf16[64,2048]{1,0:T(8,128)(2,1)S(1)} %collective-permute-done.6.refs_5_), channel_id=1, source_target_pairs={{0,32},{32,64},{64,96},{96,128},{128,160},{160,192},{192,224},{224... | collective-permute-start | bytes 786440 | tf_op jit(solution)/shard_map/ppermute | solution.py:32
  66.7 3.6 %collective-permute-start.9 = (f32[256,384]{1,0:T(8,128)S(1)}, f32[256,384]{1,0:T(8,128)S(1)}, u32[]{:S(2)}, u32[]{:S(2)}) collective-permute-start(f32[256,384]{1,0:T(8,128)S(1)} %get-tuple-element.17), channel_id=1, source_target_pairs={{0,1},{1,0},{2,3},{3,2},{4,5},{5,4},{6,7},{7,6},{8,9},{9,8},{10,11... | collective-permute-start | bytes 1179656 | tf_op jit(solution)/shard_map/ppermute | solution.py:20
  71.1 23.1 %all-to-all-start.1 = ((f32[16,16,384]{2,1,0:T(8,128)}), f32[16,16,384]{2,1,0:T(8,128)}, u32[]{:S(2)}, u32[]{:S(2)}) async-start(f32[16,16,384]{2,1,0:T(8,128)} %bitcast.8), calls=%async_computation.1 | async-start | bytes 786432 | tf_op jit(solution)/shard_map/all_to_all | solution.py:24
  84.6 15.4 %copy-start.8 = (f32[8,48]{1,0:T(8,128)S(1)}, f32[8,48]{1,0:T(8,128)}, u32[]{:S(2)}) copy-start(f32[8,48]{1,0:T(8,128)} %param.9) | copy-start | bytes 4612
  85.9 3.6 %collective-permute-start.5 = (f32[256,384]{1,0:T(8,128)S(1)}, f32[256,384]{1,0:T(8,128)S(1)}, u32[]{:S(2)}, u32[]{:S(2)}) collective-permute-start(f32[256,384]{1,0:T(8,128)S(1)} %get-tuple-element.15), channel_id=1, source_target_pairs={{0,1},{1,0},{2,3},{3,2},{4,5},{5,4},{6,7},{7,6},{8,9},{9,8},{10,11... | collective-permute-start | bytes 1179656 | tf_op jit(solution)/shard_map/ppermute | solution.py:20
  89.5 57.1 %copy-start.7 = (s32[1,48,16,2]{1,3,2,0:T(2,128)S(1)}, s32[1,48,16,2]{1,3,2,0:T(2,128)}, u32[]{:S(2)}) copy-start(s32[1,48,16,2]{1,3,2,0:T(2,128)} %param.10) | copy-start | bytes 18436
  89.5 58.8 %copy-start.2 = (bf16[512,2048]{1,0:T(8,128)(2,1)S(1)}, bf16[512,2048]{1,0:T(8,128)(2,1)}, u32[]{:S(2)}) copy-start(bf16[512,2048]{1,0:T(8,128)(2,1)} %all-gather.3.cloned.1.call-done.image_ref.other_ref) | copy-start | bytes 6291460
  94.1 17.2 %all-to-all-start = ((f32[16,16,384]{2,1,0:T(8,128)}), f32[16,16,384]{2,1,0:T(8,128)S(1)}, u32[]{:S(2)}, u32[]{:S(2)}) async-start(f32[16,16,384]{2,1,0:T(8,128)} %bitcast.5), calls=%async_computation | async-start | bytes 786432 | tf_op jit(solution)/shard_map/all_to_all | solution.py:24
  144.6 3.6 %collective-permute-start.10 = (bf16[16,2,16,384]{3,2,1,0:T(8,128)(2,1)S(1)}, bf16[16,2,16,384]{3,2,1,0:T(8,128)(2,1)S(1)}, u32[]{:S(2)}, u32[]{:S(2)}) collective-permute-start(bf16[16,2,16,384]{3,2,1,0:T(8,128)(2,1)S(1)} %all_to_all.26.mine_ref), channel_id=1, source_target_pairs={{0,1},{1,0},{2,3},{3,2},{4,5},{5,4},{6,7},{7,6},{8,9},{9,8},{10,11... | collective-permute-start | bytes 1179656 | tf_op jit(solution)/shard_map/ppermute | solution.py:20
  154.8 6.1 %collective-permute-start.11 = (bf16[1024,1024]{1,0:T(8,128)(2,1)S(1)}, bf16[1024,1024]{1,0:T(8,128)(2,1)S(1)}, u32[]{:S(2)}, u32[]{:S(2)}) collective-permute-start(bf16[1024,1024]{1,0:T(8,128)(2,1)S(1)} %get-tuple-element.20), channel_id=1, source_target_pairs={{0,1},{1,0},{2,3},{3,2},{4,5},{5,4},{6,7},{7,6},{8,9},{9,8},{10,11... | collective-permute-start | bytes 6291464 | tf_op jit(solution)/shard_map/ppermute | solution.py:20
  161.4 18.2 %collective-permute-start.12 = (bf16[256,1024]{1,0:T(8,128)(2,1)S(1)}, bf16[256,1024]{1,0:T(8,128)(2,1)S(1)}, u32[]{:S(2)}, u32[]{:S(2)}) collective-permute-start(bf16[256,1024]{1,0:T(8,128)(2,1)S(1)} %shard_map.68), channel_id=1, source_target_pairs={{0,16},{8,24},{16,0},{24,8},{1,17},{9,25},{17,1},{25,9},{2,18},{10... | collective-permute-start | bytes 1572872 | tf_op jit(solution)/shard_map/ppermute | solution.py:32
  165.1 24.7 %collective-permute-start.13 = (bf16[256,1024]{1,0:T(8,128)(2,1)S(1)}, bf16[256,1024]{1,0:T(8,128)(2,1)S(1)}, u32[]{:S(2)}, u32[]{:S(2)}) collective-permute-start(bf16[256,1024]{1,0:T(8,128)(2,1)S(1)} %shard_map.69), channel_id=1, source_target_pairs={{0,8},{8,16},{16,24},{24,0},{1,9},{9,17},{17,25},{25,1},{2,10},{10... | collective-permute-start | bytes 1572872 | tf_op jit(solution)/shard_map/ppermute | solution.py:32
  169.7 20.3 %collective-permute-start.14 = (bf16[256,1024]{1,0:T(8,128)(2,1)S(1)}, bf16[256,1024]{1,0:T(8,128)(2,1)S(1)}, u32[]{:S(2)}, u32[]{:S(2)}) collective-permute-start(bf16[256,1024]{1,0:T(8,128)(2,1)S(1)} %shard_map.70), channel_id=1, source_target_pairs={{0,24},{8,0},{16,8},{24,16},{1,25},{9,1},{17,9},{25,17},{2,26},{10... | collective-permute-start | bytes 1572872 | tf_op jit(solution)/shard_map/ppermute | solution.py:32
  (3 other events, 4.5 us)
Sparse Core Ops, SparseCore 0:
  39.2 43.7 all-gather.2

commit v8 on v7

--- a/solution.py
+++ b/solution.py
@@ -153,11 +153,10 @@
 
     @pl.when(step == pl.num_programs(0) - 1)
     def _():
-        slots = away_ref.shape[0]
-        for r in range(0, slots, 256):
-            away_ref[r : r + 256, :] = jnp.dot(
-                spots(slot_ref, slots + r, 256), pieces_ref[...], preferred_element_type=f32
-            ).astype(bf16)
+        count = away_ref.shape[0]
+        away_ref[...] = jnp.dot(
+            spots(slot_ref, 6 * count, count), pieces_ref[...], preferred_element_type=f32
+        ).astype(bf16)
 
 
 def sliced(core, mine, twin, other_plane, own_plane, slot, slots):
@@ -199,30 +198,59 @@
     )(core, mine, twin, other_plane, own_plane, slot)
 
 
-def near_kernel(start, slot_ref, pieces_ref, got_ref, sum_ref):
+def away_kernel(slot_ref, pieces_ref, away_ref):
+    count = away_ref.shape[0] // 3
+    for row, part in enumerate((1, 3, 0)):
+        away_ref[row * count : (row + 1) * count, :] = jnp.dot(
+            spots(slot_ref, (4 + part) * count, count),
+            pieces_ref[...],
+            preferred_element_type=f32,
+        ).astype(bf16)
+
+
+def near_kernel(part, row, slot_ref, pieces_ref, got_ref, sum_ref):
     count = sum_ref.shape[0]
     near = jnp.dot(
-        spots(slot_ref, start, count), pieces_ref[...], preferred_element_type=f32
+        spots(slot_ref, part * count, count), pieces_ref[...], preferred_element_type=f32
     )
-    sum_ref[...] = (near + got_ref[start : start + count, :].astype(f32)).astype(sum_ref.dtype)
-
-
-def near_summed(slot, pieces, got, part, dtype):
-    slots, width = got.shape
-    count = slots // 4
+    got = got_ref[row * count : (row + 1) * count, :].astype(f32)
+    sum_ref[...] = (near + got).astype(sum_ref.dtype)
+
+
+def whole_call(kernel, out, flops, *args):
     whole = pl.BlockSpec(memory_space=pltpu.VMEM)
+    moved = sum(x.size * x.dtype.itemsize for x in args)
     return pl.pallas_call(
-        functools.partial(near_kernel, part * count),
-        out_shape=jax.ShapeDtypeStruct((count, width), dtype),
-        in_specs=[whole] * 3,
+        kernel,
+        out_shape=out,
+        in_specs=[whole] * len(args),
         out_specs=whole,
         compiler_params=kernel_params(),
-        cost_estimate=pl.CostEstimate(
-            flops=2 * count * pieces.shape[0] * width,
-            bytes_accessed=2 * width * (pieces.shape[0] + 2 * count),
-            transcendentals=0,
-        ),
-    )(slot, pieces, got)
+        cost_estimate=pl.CostEstimate(flops=flops, bytes_accessed=moved, transcendentals=0),
+    )(*args)
+
+
+def slots_summed(slot, cut, away, count):
+    pieces, width = cut.shape
+    flops = 2 * count * pieces * width
+    far = swapped(away, "core")
+    rest = jax.ShapeDtypeStruct((3 * count, width), bf16)
+    rest = whole_call(away_kernel, rest, 3 * flops, slot, cut)
+
+    def near(part, row, got, dtype=bf16):
+        out = jax.ShapeDtypeStruct((count, width), dtype)
+        return whole_call(functools.partial(near_kernel, part, row), out, flops, slot, cut, got)
+
+    two = near(2, 0, far)
+    rest = lax.optimization_barrier((two, rest))[1]
+    two = turned(two, 2, "x", 4)
+    rest = swapped(rest, "core")
+    one = turned(near(1, 0, rest), 1, "x", 4)
+    three = turned(near(3, 1, rest), 3, "x", 4)
+    summed = near(0, 2, rest, f32)
+    for got in (two, one, three):
+        summed = summed + got.astype(f32)
+    return summed.astype(bf16)
 
 
 def local(images, projections, noise_weight, prior_score, routing, insert_kernel):
@@ -277,14 +305,9 @@
     mine = shared(own_weights, ("x", "yl"), half)
     twin = swapped(mine, "core")
 
-    cut, away = sliced(core_one, mine, twin, other_plane, own_plane, slot, half * voxels)
-    got = swapped(away, "core")
+    cut, away = sliced(core_one, mine, twin, other_plane, own_plane, slot, 4 * voxels)
     width = classes * PIECE
-    summed = near_summed(slot, cut, got, 0, f32)
-    for part in (2, 1, 3):
-        sent = near_summed(slot, cut, got, part, bf16)
-        summed = summed + turned(sent, part, "x", 4).astype(f32)
-    summed = summed.astype(bf16)
+    summed = slots_summed(slot, cut, away, 4 * voxels)
     summed = exchanged(summed.reshape(4 * orients, voxels // orients, width), ("yl", "yh", "z"))
     own_blocks = jnp.sum(summed.astype(f32), axis=0)
     rounded = own_blocks.astype(bf16).reshape(own_blocks.shape[0], classes, PIECE)

time: 224 us -> 224 us (level)
  waiting for transfers between devices: 58.6 us -> 55 us
  starting transfers between devices: 71 us -> 73.5 us
    ppermute x5 -> x6, waiting for transfers between devices: 9.71 us -> 6.18 us  [swapped(): return lax.ppermute(value, axis, [(0, 1), (1, 0)])]
    ppermute x5 -> x6, starting transfers between devices: 15.5 us -> 17.6 us  [swapped(): return lax.ppermute(value, axis, [(0, 1), (1, 0)])]
    unnamed x18 -> x20, local copies, waits for them, and re-layouts: 4.5 us -> 5.28 us
  transfers between devices with their start and end apart: 18 -> 19, of which waited for: 15 -> 16; matrix products, arithmetic and copies ran while one was open for 2% -> 2% of each run, Pallas kernels for 2% -> 3%
where the time goes in v8:
time: 224 us; the launch traced here: 221 us
  starting transfers between devices  73.5 us (33%)
  blocking collectives  55.4 us (25%)
  waiting for transfers between devices  55 us (25%)
  between operations  13.7 us (6%)
  Pallas kernels  11 us (5%)
  local copies, waits for them, and re-layouts  6.13 us (3%)
  other arithmetic  5.72 us (3%)
    all_to_all x3, blocking collectives, exchanged(): return lax.all_to_all(value, axis, 0, 0, tiled=True)  55.4 us
    ppermute x10, starting transfers between devices, turned(): lax.ppermute(block, axis, [(i, (i + step) % count) for i in range(count)])  38.9 us
    ppermute x10, waiting for transfers between devices, turned(): lax.ppermute(block, axis, [(i, (i + step) % count) for i in range(count)])  34.1 us
    ppermute x6, starting transfers between devices, swapped(): return lax.ppermute(value, axis, [(0, 1), (1, 0)])  17.6 us
    all_to_all x2, starting transfers between devices, exchanged(): return lax.all_to_all(value, axis, 0, 0, tiled=True)  17 us
    all_to_all x2, waiting for transfers between devices, exchanged(): return lax.all_to_all(value, axis, 0, 0, tiled=True)  13.8 us
    ppermute x6, waiting for transfers between devices, swapped(): return lax.ppermute(value, axis, [(0, 1), (1, 0)])  6.18 us
    unnamed x20, local copies, waits for them, and re-layouts  5.28 us
  transfers between devices with their start and end apart: 19, of which 16 were waited for; matrix products, arithmetic and copies ran while one was open for 2% of the time, Pallas kernels for 3%

profile of v8, /device:TPU:6, one launch (start us, length us, event | category | flops | bytes accessed | tf_op | source)
XLA Modules:
  0.0 221.2 jit_solution(4935517818642234723)
XLA Ops:
  6.5 4.4 %collective-permute-start = (bf16[64,2048]{1,0:T(8,128)(2,1)}, bf16[64,2048]{1,0:T(8,128)(2,1)S(1)}, u32[]{:S(2)}, u32[]{:S(2)}) collective-permute-start(bf16[64,2048]{1,0:T(8,128)(2,1)} %refs_0_.1), channel_id=1, source_target_pairs={{0,32},{32,64},{64,96},{96,128},{128,160},{160,192},{192,224},{224... | collective-permute-start | bytes 786440 | tf_op jit(solution)/shard_map/ppermute | solution.py:32
  10.9 8.6 %collective-permute-start.2 = (bf16[64,2048]{1,0:T(8,128)(2,1)}, bf16[64,2048]{1,0:T(8,128)(2,1)S(1)}, u32[]{:S(2)}, u32[]{:S(2)}) collective-permute-start(bf16[64,2048]{1,0:T(8,128)(2,1)} %refs_0_.1), channel_id=1, source_target_pairs={{0,224},{32,0},{64,32},{96,64},{128,96},{160,128},{192,160},{224,1... | collective-permute-start | bytes 786440 | tf_op jit(solution)/shard_map/ppermute | solution.py:32
  19.5 7.7 %collective-permute-start.4 = (bf16[64,2048]{1,0:T(8,128)(2,1)}, bf16[64,2048]{1,0:T(8,128)(2,1)S(1)}, u32[]{:S(2)}, u32[]{:S(2)}) collective-permute-start(bf16[64,2048]{1,0:T(8,128)(2,1)} %refs_0_.1), channel_id=1, source_target_pairs={{0,256},{256,0},{1,257},{257,1},{2,258},{258,2},{3,259},{259,3},{4... | collective-permute-start | bytes 786440 | tf_op jit(solution)/shard_map/ppermute | solution.py:20
  29.2 5.1 %collective-permute-start.3 = (bf16[64,2048]{1,0:T(8,128)(2,1)S(1)}, bf16[64,2048]{1,0:T(8,128)(2,1)S(1)}, u32[]{:S(2)}, u32[]{:S(2)}) collective-permute-start(bf16[64,2048]{1,0:T(8,128)(2,1)S(1)} %collective-permute-done.2.refs_2_), channel_id=1, source_target_pairs={{0,224},{32,0},{64,32},{96,64},{128,96},{160,128},{192,160},{224,1... | collective-permute-start | bytes 786440 | tf_op jit(solution)/shard_map/ppermute | solution.py:32
  35.3 2.6 %collective-permute-done.1.refs_3_ = bf16[64,2048]{1,0:T(8,128)(2,1)S(1)} collective-permute-done((bf16[64,2048]{1,0:T(8,128)(2,1)S(1)}, bf16[64,2048]{1,0:T(8,128)(2,1)S(1)}, u32[]{:S(2)}, u32[]{:S(2)}) %collective-permute-start.1) | collective-permute-done | bytes 262176 | tf_op jit(solution)/shard_map/ppermute | solution.py:32
  39.1 2.1 collective-permute-start.6
  41.2 5.6 %collective-permute-start.7 = (bf16[64,2048]{1,0:T(8,128)(2,1)S(1)}, bf16[64,2048]{1,0:T(8,128)(2,1)S(1)}, u32[]{:S(2)}, u32[]{:S(2)}) collective-permute-start(bf16[64,2048]{1,0:T(8,128)(2,1)S(1)} %collective-permute-done.3.refs_4_), channel_id=1, source_target_pairs={{0,224},{32,0},{64,32},{96,64},{128,96},{160,128},{192,160},{224,1... | collective-permute-start | bytes 786440 | tf_op jit(solution)/shard_map/ppermute | solution.py:32
  46.8 2.6 %collective-permute-done.6.refs_5_ = bf16[64,2048]{1,0:T(8,128)(2,1)S(1)} collective-permute-done((bf16[64,2048]{1,0:T(8,128)(2,1)S(1)}, bf16[64,2048]{1,0:T(8,128)(2,1)S(1)}, u32[]{:S(2)}, u32[]{:S(2)}) %collective-permute-start.6) | collective-permute-done | bytes 262176 | tf_op jit(solution)/shard_map/ppermute | solution.py:32
  53.4 10.1 %collective-permute-done.8.refs_7_ = bf16[64,2048]{1,0:T(8,128)(2,1)} collective-permute-done((bf16[64,2048]{1,0:T(8,128)(2,1)S(1)}, bf16[64,2048]{1,0:T(8,128)(2,1)}, u32[]{:S(2)}, u32[]{:S(2)}) %collective-permute-start.8) | collective-permute-done | bytes 262176 | tf_op jit(solution)/shard_map/ppermute | solution.py:32
  63.5 2.3 %shard_map.65 = (f32[256,384]{1,0:T(8,128)S(1)}, f32[256,384]{1,0:T(8,128)S(1)}, bf16[512,2048]{1,0:T(8,128)(2,1)S(1)}) custom-call(s32[1]{0:T(128)} %bitcast.3.core_ref, s32[1]{0:T(128)} %bitcast.7.z_ref, bf16[64,2048]{1,0:T(8,128)(2,1)S(1)} %copy-done.3, bf16[64,2048]{1,0:T(8,128)(2,1)S(1)} %collective-permute-done.refs_1_, ...), custom_call_target="tpu_custom_call" | custom-call | flops 805306368 | bytes 6553600 | tf_op jit(solution)/shard_map/pallas_call | solution.py:72
  71.6 11.1 %all-to-all-start.1 = ((f32[16,16,384]{2,1,0:T(8,128)}), f32[16,16,384]{2,1,0:T(8,128)S(1)}, u32[]{:S(2)}, u32[]{:S(2)}) async-start(f32[16,16,384]{2,1,0:T(8,128)} %bitcast.8), calls=%async_computation.1 | async-start | bytes 786432 | tf_op jit(solution)/shard_map/all_to_all | solution.py:24
  90.8 3.6 %all-to-all-done.1 = f32[16,16,384]{2,1,0:T(8,128)S(1)} async-done(((f32[16,16,384]{2,1,0:T(8,128)}), f32[16,16,384]{2,1,0:T(8,128)S(1)}, u32[]{:S(2)}, u32[]{:S(2)}) %all-to-all-start.1) | async-done | bytes 393248 | tf_op jit(solution)/shard_map/all_to_all | solution.py:24
  95.1 5.9 %all-to-all-start = ((f32[16,16,384]{2,1,0:T(8,128)}), f32[16,16,384]{2,1,0:T(8,128)S(1)}, u32[]{:S(2)}, u32[]{:S(2)}) async-start(f32[16,16,384]{2,1,0:T(8,128)} %bitcast.5), calls=%async_computation | async-start | bytes 786432 | tf_op jit(solution)/shard_map/all_to_all | solution.py:24
  102.2 10.2 %all-to-all-done = f32[16,16,384]{2,1,0:T(8,128)S(1)} async-done(((f32[16,16,384]{2,1,0:T(8,128)}), f32[16,16,384]{2,1,0:T(8,128)S(1)}, u32[]{:S(2)}, u32[]{:S(2)}) %all-to-all-start) | async-done | bytes 393248 | tf_op jit(solution)/shard_map/all_to_all | solution.py:24
  112.8 17.5 %all_to_all.25 = f32[16,2,32]{2,1,0:T(2,128)S(1)} all-to-all(f32[16,2,32]{2,1,0:T(2,128)S(1)} %broadcast_in_dim.9), channel_id=1, replica_groups=mesh['yh'=2,'z'=8,'x'=4,'yl'=4,'core'=2] {'yh','z'}, dimensions={0} | all-to-all | bytes 8192 | tf_op jit(solution)/shard_map/all_to_all | solution.py:24
  130.7 14.9 %all_to_all.26.mine_ref = bf16[16,2,16,384]{3,2,1,0:T(8,128)(2,1)S(1)} all-to-all(bf16[16,2,16,384]{3,2,1,0:T(8,128)(2,1)S(1)} %broadcast_in_dim.10), channel_id=1, replica_groups=mesh['yh'=2,'z'=8,'x'=4,'yl'=4,'core'=2] {'x','yl'}, dimensions={0} | all-to-all | bytes 786432 | tf_op jit(solution)/shard_map/all_to_all | solution.py:24
  150.8 3.7 %shard_map.66 = (bf16[768,1024]{1,0:T(8,128)(2,1)S(1)}, bf16[256,1024]{1,0:T(8,128)(2,1)S(1)}) custom-call(s32[1]{0:T(128)} %bitcast.3.core_ref, bf16[16,2,16,384]{3,2,1,0:T(8,128)(2,1)S(1)} %all_to_all.26.mine_ref, bf16[16,2,16,384]{3,2,1,0:T(8,128)(2,1)S(1)} %collective-permute-done.10.twin_ref, bf16[512,2048]{1,0:T(8,128)(2,1)S(1)} %copy-done.2, ...), custom_call_target="tpu_custom_call" | custom-call | flops 2013265920 | bytes 6291456 | tf_op jit(solution)/shard_map/pallas_call | solution.py:172
  154.5 2.1 collective-permute-start.11
  158.9 2.1 collective-permute-start.12
  161.0 3.1 %collective-permute-start.13 = (bf16[256,1024]{1,0:T(8,128)(2,1)S(1)}, bf16[256,1024]{1,0:T(8,128)(2,1)S(1)}, u32[]{:S(2)}, u32[]{:S(2)}) collective-permute-start(bf16[256,1024]{1,0:T(8,128)(2,1)S(1)} %shard_map.67), channel_id=1, source_target_pairs={{0,16},{8,24},{16,0},{24,8},{1,17},{9,25},{17,1},{25,9},{2,18},{10... | collective-permute-start | bytes 1572872 | tf_op jit(solution)/shard_map/ppermute | solution.py:32
  164.8 4.3 %collective-permute-start.14 = (bf16[256,1024]{1,0:T(8,128)(2,1)S(1)}, bf16[256,1024]{1,0:T(8,128)(2,1)S(1)}, u32[]{:S(2)}, u32[]{:S(2)}) collective-permute-start(bf16[256,1024]{1,0:T(8,128)(2,1)S(1)} %shard_map.70), channel_id=1, source_target_pairs={{0,8},{8,16},{16,24},{24,0},{1,9},{9,17},{17,25},{25,1},{2,10},{10... | collective-permute-start | bytes 1572872 | tf_op jit(solution)/shard_map/ppermute | solution.py:32
  172.2 7.0 %collective-permute-done.13 = bf16[256,1024]{1,0:T(8,128)(2,1)S(1)} collective-permute-done((bf16[256,1024]{1,0:T(8,128)(2,1)S(1)}, bf16[256,1024]{1,0:T(8,128)(2,1)S(1)}, u32[]{:S(2)}, u32[]{:S(2)}) %collective-permute-start.13) | collective-permute-done | bytes 524320 | tf_op jit(solution)/shard_map/ppermute | solution.py:32
  179.2 10.4 %collective-permute-done.14 = bf16[256,1024]{1,0:T(8,128)(2,1)S(1)} collective-permute-done((bf16[256,1024]{1,0:T(8,128)(2,1)S(1)}, bf16[256,1024]{1,0:T(8,128)(2,1)S(1)}, u32[]{:S(2)}, u32[]{:S(2)}) %collective-permute-start.14) | collective-permute-done | bytes 524320 | tf_op jit(solution)/shard_map/ppermute | solution.py:32
  190.4 23.0 %all_to_all.27 = bf16[64,4,1024]{2,1,0:T(4,128)(2,1)S(1)} all-to-all(bf16[64,4,1024]{2,1,0:T(4,128)(2,1)S(1)} %reshape.464), channel_id=1, replica_groups=mesh['yh'=2,'z'=8,'x'=4,'yl'=4,'core'=2] {'yl','yh','z'}, dimensions={0} | all-to-all | bytes 1048576 | tf_op jit(solution)/shard_map/all_to_all | solution.py:24
  (79 shorter events, 37.6 us)
Async XLA Ops:
  6.5 207.1 %copy-start = (bf16[1,4,128,128]{3,2,1,0:T(8,128)(2,1)S(1)}, bf16[1,4,128,128]{3,2,1,0:T(8,128)(2,1)}, u32[]{:S(2)}) copy-start(bf16[1,4,128,128]{3,2,1,0:T(8,128)(2,1)} %param.11) | copy-start | bytes 393220
  6.5 76.9 %all-gather.3.cloned.1.call-start = ((), (), s32[]{:S(2)}) async-start(), calls=%async_computation.5 | async-start | bytes 2359296 | tf_op jit(solution)/shard_map/all_gather | solution.py:278
  6.5 20.7 %collective-permute-start = (bf16[64,2048]{1,0:T(8,128)(2,1)}, bf16[64,2048]{1,0:T(8,128)(2,1)S(1)}, u32[]{:S(2)}, u32[]{:S(2)}) collective-permute-start(bf16[64,2048]{1,0:T(8,128)(2,1)} %refs_0_.1), channel_id=1, source_target_pairs={{0,32},{32,64},{64,96},{96,128},{128,160},{160,192},{192,224},{224... | collective-permute-start | bytes 786440 | tf_op jit(solution)/shard_map/ppermute | solution.py:32
  10.9 18.3 %collective-permute-start.2 = (bf16[64,2048]{1,0:T(8,128)(2,1)}, bf16[64,2048]{1,0:T(8,128)(2,1)S(1)}, u32[]{:S(2)}, u32[]{:S(2)}) collective-permute-start(bf16[64,2048]{1,0:T(8,128)(2,1)} %refs_0_.1), channel_id=1, source_target_pairs={{0,224},{32,0},{64,32},{96,64},{128,96},{160,128},{192,160},{224,1... | collective-permute-start | bytes 786440 | tf_op jit(solution)/shard_map/ppermute | solution.py:32
  19.5 15.8 %collective-permute-start.4 = (bf16[64,2048]{1,0:T(8,128)(2,1)}, bf16[64,2048]{1,0:T(8,128)(2,1)S(1)}, u32[]{:S(2)}, u32[]{:S(2)}) collective-permute-start(bf16[64,2048]{1,0:T(8,128)(2,1)} %refs_0_.1), channel_id=1, source_target_pairs={{0,256},{256,0},{1,257},{257,1},{2,258},{258,2},{3,259},{259,3},{4... | collective-permute-start | bytes 786440 | tf_op jit(solution)/shard_map/ppermute | solution.py:20
  27.3 10.6 %collective-permute-start.1 = (bf16[64,2048]{1,0:T(8,128)(2,1)S(1)}, bf16[64,2048]{1,0:T(8,128)(2,1)S(1)}, u32[]{:S(2)}, u32[]{:S(2)}) collective-permute-start(bf16[64,2048]{1,0:T(8,128)(2,1)S(1)} %collective-permute-done.refs_1_), channel_id=1, source_target_pairs={{0,32},{32,64},{64,96},{96,128},{128,160},{160,192},{192,224},{224... | collective-permute-start | bytes 786440 | tf_op jit(solution)/shard_map/ppermute | solution.py:32
  29.2 9.8 %collective-permute-start.3 = (bf16[64,2048]{1,0:T(8,128)(2,1)S(1)}, bf16[64,2048]{1,0:T(8,128)(2,1)S(1)}, u32[]{:S(2)}, u32[]{:S(2)}) collective-permute-start(bf16[64,2048]{1,0:T(8,128)(2,1)S(1)} %collective-permute-done.2.refs_2_), channel_id=1, source_target_pairs={{0,224},{32,0},{64,32},{96,64},{128,96},{160,128},{192,160},{224,1... | collective-permute-start | bytes 786440 | tf_op jit(solution)/shard_map/ppermute | solution.py:32
  39.1 24.4 %copy-start.3 = (bf16[64,2048]{1,0:T(8,128)(2,1)S(1)}, bf16[64,2048]{1,0:T(8,128)(2,1)}, u32[]{:S(2)}) copy-start(bf16[64,2048]{1,0:T(8,128)(2,1)} %refs_0_.1) | copy-start | bytes 786436
  39.1 10.3 %collective-permute-start.6 = (bf16[64,2048]{1,0:T(8,128)(2,1)S(1)}, bf16[64,2048]{1,0:T(8,128)(2,1)S(1)}, u32[]{:S(2)}, u32[]{:S(2)}) collective-permute-start(bf16[64,2048]{1,0:T(8,128)(2,1)S(1)} %collective-permute-done.1.refs_3_), channel_id=1, source_target_pairs={{0,32},{32,64},{64,96},{96,128},{128,160},{160,192},{192,224},{224... | collective-permute-start | bytes 786440 | tf_op jit(solution)/shard_map/ppermute | solution.py:32
  41.2 12.2 %collective-permute-start.7 = (bf16[64,2048]{1,0:T(8,128)(2,1)S(1)}, bf16[64,2048]{1,0:T(8,128)(2,1)S(1)}, u32[]{:S(2)}, u32[]{:S(2)}) collective-permute-start(bf16[64,2048]{1,0:T(8,128)(2,1)S(1)} %collective-permute-done.3.refs_4_), channel_id=1, source_target_pairs={{0,224},{32,0},{64,32},{96,64},{128,96},{160,128},{192,160},{224,1... | collective-permute-start | bytes 786440 | tf_op jit(solution)/shard_map/ppermute | solution.py:32
  49.4 14.1 %collective-permute-start.8 = (bf16[64,2048]{1,0:T(8,128)(2,1)S(1)}, bf16[64,2048]{1,0:T(8,128)(2,1)}, u32[]{:S(2)}, u32[]{:S(2)}) collective-permute-start(bf16[64,2048]{1,0:T(8,128)(2,1)S(1)} %collective-permute-done.6.refs_5_), channel_id=1, source_target_pairs={{0,32},{32,64},{64,96},{96,128},{128,160},{160,192},{192,224},{224... | collective-permute-start | bytes 786440 | tf_op jit(solution)/shard_map/ppermute | solution.py:32
  67.2 3.6 %collective-permute-start.9 = (f32[256,384]{1,0:T(8,128)S(1)}, f32[256,384]{1,0:T(8,128)S(1)}, u32[]{:S(2)}, u32[]{:S(2)}) collective-permute-start(f32[256,384]{1,0:T(8,128)S(1)} %get-tuple-element.18), channel_id=1, source_target_pairs={{0,1},{1,0},{2,3},{3,2},{4,5},{5,4},{6,7},{7,6},{8,9},{9,8},{10,11... | collective-permute-start | bytes 1179656 | tf_op jit(solution)/shard_map/ppermute | solution.py:20
  71.6 22.8 %all-to-all-start.1 = ((f32[16,16,384]{2,1,0:T(8,128)}), f32[16,16,384]{2,1,0:T(8,128)S(1)}, u32[]{:S(2)}, u32[]{:S(2)}) async-start(f32[16,16,384]{2,1,0:T(8,128)} %bitcast.8), calls=%async_computation.1 | async-start | bytes 786432 | tf_op jit(solution)/shard_map/all_to_all | solution.py:24
  86.3 14.7 %copy-start.9 = (f32[8,48]{1,0:T(8,128)S(1)}, f32[8,48]{1,0:T(8,128)}, u32[]{:S(2)}) copy-start(f32[8,48]{1,0:T(8,128)} %param.9) | copy-start | bytes 4612
  86.3 3.6 %collective-permute-start.5 = (f32[256,384]{1,0:T(8,128)S(1)}, f32[256,384]{1,0:T(8,128)S(1)}, u32[]{:S(2)}, u32[]{:S(2)}) collective-permute-start(f32[256,384]{1,0:T(8,128)S(1)} %get-tuple-element.16), channel_id=1, source_target_pairs={{0,1},{1,0},{2,3},{3,2},{4,5},{5,4},{6,7},{7,6},{8,9},{9,8},{10,11... | collective-permute-start | bytes 1179656 | tf_op jit(solution)/shard_map/ppermute | solution.py:20
  95.1 52.4 %copy-start.8 = (s32[1,48,16,2]{1,3,2,0:T(2,128)S(1)}, s32[1,48,16,2]{1,3,2,0:T(2,128)}, u32[]{:S(2)}) copy-start(s32[1,48,16,2]{1,3,2,0:T(2,128)} %param.10) | copy-start | bytes 18436
  95.1 54.1 %copy-start.2 = (bf16[512,2048]{1,0:T(8,128)(2,1)S(1)}, bf16[512,2048]{1,0:T(8,128)(2,1)}, u32[]{:S(2)}) copy-start(bf16[512,2048]{1,0:T(8,128)(2,1)} %all-gather.3.cloned.1.call-done.image_ref.other_ref) | copy-start | bytes 6291460
  95.1 17.3 %all-to-all-start = ((f32[16,16,384]{2,1,0:T(8,128)}), f32[16,16,384]{2,1,0:T(8,128)S(1)}, u32[]{:S(2)}, u32[]{:S(2)}) async-start(f32[16,16,384]{2,1,0:T(8,128)} %bitcast.5), calls=%async_computation | async-start | bytes 786432 | tf_op jit(solution)/shard_map/all_to_all | solution.py:24
  145.6 3.6 %collective-permute-start.10 = (bf16[16,2,16,384]{3,2,1,0:T(8,128)(2,1)S(1)}, bf16[16,2,16,384]{3,2,1,0:T(8,128)(2,1)S(1)}, u32[]{:S(2)}, u32[]{:S(2)}) collective-permute-start(bf16[16,2,16,384]{3,2,1,0:T(8,128)(2,1)S(1)} %all_to_all.26.mine_ref), channel_id=1, source_target_pairs={{0,1},{1,0},{2,3},{3,2},{4,5},{5,4},{6,7},{7,6},{8,9},{9,8},{10,11... | collective-permute-start | bytes 1179656 | tf_op jit(solution)/shard_map/ppermute | solution.py:20
  154.5 3.8 %collective-permute-start.11 = (bf16[256,1024]{1,0:T(8,128)(2,1)S(1)}, bf16[256,1024]{1,0:T(8,128)(2,1)S(1)}, u32[]{:S(2)}, u32[]{:S(2)}) collective-permute-start(bf16[256,1024]{1,0:T(8,128)(2,1)S(1)} %get-tuple-element.21), channel_id=1, source_target_pairs={{0,1},{1,0},{2,3},{3,2},{4,5},{5,4},{6,7},{7,6},{8,9},{9,8},{10,11... | collective-permute-start | bytes 1572872 | tf_op jit(solution)/shard_map/ppermute | solution.py:20
  158.9 5.3 %collective-permute-start.12 = (bf16[768,1024]{1,0:T(8,128)(2,1)S(1)}, bf16[768,1024]{1,0:T(8,128)(2,1)S(1)}, u32[]{:S(2)}, u32[]{:S(2)}) collective-permute-start(bf16[768,1024]{1,0:T(8,128)(2,1)S(1)} %shard_map.68), channel_id=1, source_target_pairs={{0,1},{1,0},{2,3},{3,2},{4,5},{5,4},{6,7},{7,6},{8,9},{9,8},{10,11... | collective-permute-start | bytes 4718600 | tf_op jit(solution)/shard_map/ppermute | solution.py:20
  161.0 18.2 %collective-permute-start.13 = (bf16[256,1024]{1,0:T(8,128)(2,1)S(1)}, bf16[256,1024]{1,0:T(8,128)(2,1)S(1)}, u32[]{:S(2)}, u32[]{:S(2)}) collective-permute-start(bf16[256,1024]{1,0:T(8,128)(2,1)S(1)} %shard_map.67), channel_id=1, source_target_pairs={{0,16},{8,24},{16,0},{24,8},{1,17},{9,25},{17,1},{25,9},{2,18},{10... | collective-permute-start | bytes 1572872 | tf_op jit(solution)/shard_map/ppermute | solution.py:32
  164.8 24.7 %collective-permute-start.14 = (bf16[256,1024]{1,0:T(8,128)(2,1)S(1)}, bf16[256,1024]{1,0:T(8,128)(2,1)S(1)}, u32[]{:S(2)}, u32[]{:S(2)}) collective-permute-start(bf16[256,1024]{1,0:T(8,128)(2,1)S(1)} %shard_map.70), channel_id=1, source_target_pairs={{0,8},{8,16},{16,24},{24,0},{1,9},{9,17},{17,25},{25,1},{2,10},{10... | collective-permute-start | bytes 1572872 | tf_op jit(solution)/shard_map/ppermute | solution.py:32
  169.7 20.1 %collective-permute-start.15 = (bf16[256,1024]{1,0:T(8,128)(2,1)S(1)}, bf16[256,1024]{1,0:T(8,128)(2,1)S(1)}, u32[]{:S(2)}, u32[]{:S(2)}) collective-permute-start(bf16[256,1024]{1,0:T(8,128)(2,1)S(1)} %shard_map.71), channel_id=1, source_target_pairs={{0,24},{8,0},{16,8},{24,16},{1,25},{9,1},{17,9},{25,17},{2,26},{10... | collective-permute-start | bytes 1572872 | tf_op jit(solution)/shard_map/ppermute | solution.py:32
  (5 other events, 9.0 us)
Sparse Core Ops, SparseCore 0:
  39.2 44.2 all-gather.2

commit v9 on v8

--- a/solution.py
+++ b/solution.py
@@ -8,6 +8,8 @@
 from jax.sharding import Mesh, PartitionSpec as P
 
 PIECE = 128
+SLICE = 50
+SCORE = 50
 NAMES = ("yh", "z", "x", "yl", "core")
 SIZES = (2, 8, 4, 4, 2)
 ORIENT = ("yh", "z")
@@ -49,8 +51,8 @@
     return got, held_back
 
 
-def kernel_params():
-    return pltpu.CompilerParams(vmem_limit_bytes=24 * 2**20)
+def kernel_params(mebibytes=24):
+    return pltpu.CompilerParams(vmem_limit_bytes=mebibytes * 2**20)
 
 
 def ring_score_kernel(core_ref, z_ref, *refs):
@@ -106,7 +108,7 @@
         out_shape=(side, side),
         in_specs=[pl.BlockSpec(memory_space=pltpu.SMEM), whole, whole, whole],
         out_specs=(whole, whole),
-        compiler_params=kernel_params(),
+        compiler_params=kernel_params(SCORE),
         cost_estimate=pl.CostEstimate(
             flops=2 * rows * pixels * columns,
             bytes_accessed=2 * pixels * (rows + columns) + 4 * rows * columns,
@@ -189,7 +191,7 @@
             pl.BlockSpec((slots, width), fixed(2)),
         ),
         scratch_shapes=[pltpu.VMEM((columns, 2 * rows), bf16)],
-        compiler_params=kernel_params(),
+        compiler_params=kernel_params(SLICE),
         cost_estimate=pl.CostEstimate(
             flops=4 * rows * pixels * columns + 2 * slots * pieces * width,
             bytes_accessed=4 * rows * pixels + 2 * width * (pieces + slots),

time: 224 us -> 224 us (level)
  local copies, waits for them, and re-layouts: 6.13 us -> 2.18 us
  Pallas kernels: 11 us -> 14.2 us
    unnamed x20 -> x12, local copies, waits for them, and re-layouts: 5.28 us -> 1.33 us
  transfers between devices with their start and end apart: 19 -> 19, of which waited for: 16 -> 16; matrix products, arithmetic and copies ran while one was open for 2% -> 2% of each run, Pallas kernels for 3% -> 4%
where the time goes in v9:
time: 224 us; the launch traced here: 220 us
  starting transfers between devices  73.5 us (33%)
  waiting for transfers between devices  55.9 us (25%)
  blocking collectives  55.5 us (25%)
  Pallas kernels  14.2 us (6%)
  between operations  13.7 us (6%)
  other arithmetic  4.74 us (2%)
    all_to_all x3, blocking collectives, exchanged(): return lax.all_to_all(value, axis, 0, 0, tiled=True)  55.5 us
    ppermute x10, starting transfers between devices, turned(): lax.ppermute(block, axis, [(i, (i + step) % count) for i in range(count)])  38.9 us
    ppermute x10, waiting for transfers between devices, turned(): lax.ppermute(block, axis, [(i, (i + step) % count) for i in range(count)])  34 us
    ppermute x6, starting transfers between devices, swapped(): return lax.ppermute(value, axis, [(0, 1), (1, 0)])  17.6 us
    all_to_all x2, starting transfers between devices, exchanged(): return lax.all_to_all(value, axis, 0, 0, tiled=True)  17.1 us
    all_to_all x2, waiting for transfers between devices, exchanged(): return lax.all_to_all(value, axis, 0, 0, tiled=True)  14.8 us
    ppermute x6, waiting for transfers between devices, swapped(): return lax.ppermute(value, axis, [(0, 1), (1, 0)])  6.2 us
    pallas_call x1, Pallas kernels, sliced(): pl.pallas_call(slice_kernel, grid=(steps,), out_shape=(jax.ShapeDtypeStru...  5.27 us
  transfers between devices with their start and end apart: 19, of which 16 were waited for; matrix products, arithmetic and copies ran while one was open for 2% of the time, Pallas kernels for 4%

profile of v9, /device:TPU:6, one launch (start us, length us, event | category | flops | bytes accessed | tf_op | source)
XLA Modules:
  0.0 220.5 jit_solution(17795881306431442054)
XLA Ops:
  6.5 4.4 %collective-permute-start = (bf16[64,2048]{1,0:T(8,128)(2,1)}, bf16[64,2048]{1,0:T(8,128)(2,1)S(1)}, u32[]{:S(2)}, u32[]{:S(2)}) collective-permute-start(bf16[64,2048]{1,0:T(8,128)(2,1)} %refs_0_.1), channel_id=1, source_target_pairs={{0,32},{32,64},{64,96},{96,128},{128,160},{160,192},{192,224},{224... | collective-permute-start | bytes 786440 | tf_op jit(solution)/shard_map/ppermute | solution.py:34
  10.9 8.6 %collective-permute-start.2 = (bf16[64,2048]{1,0:T(8,128)(2,1)}, bf16[64,2048]{1,0:T(8,128)(2,1)S(1)}, u32[]{:S(2)}, u32[]{:S(2)}) collective-permute-start(bf16[64,2048]{1,0:T(8,128)(2,1)} %refs_0_.1), channel_id=1, source_target_pairs={{0,224},{32,0},{64,32},{96,64},{128,96},{160,128},{192,160},{224,1... | collective-permute-start | bytes 786440 | tf_op jit(solution)/shard_map/ppermute | solution.py:34
  19.5 7.7 %collective-permute-start.4 = (bf16[64,2048]{1,0:T(8,128)(2,1)}, bf16[64,2048]{1,0:T(8,128)(2,1)S(1)}, u32[]{:S(2)}, u32[]{:S(2)}) collective-permute-start(bf16[64,2048]{1,0:T(8,128)(2,1)} %refs_0_.1), channel_id=1, source_target_pairs={{0,256},{256,0},{1,257},{257,1},{2,258},{258,2},{3,259},{259,3},{4... | collective-permute-start | bytes 786440 | tf_op jit(solution)/shard_map/ppermute | solution.py:22
  29.2 5.1 %collective-permute-start.3 = (bf16[64,2048]{1,0:T(8,128)(2,1)S(1)}, bf16[64,2048]{1,0:T(8,128)(2,1)S(1)}, u32[]{:S(2)}, u32[]{:S(2)}) collective-permute-start(bf16[64,2048]{1,0:T(8,128)(2,1)S(1)} %collective-permute-done.2.refs_2_), channel_id=1, source_target_pairs={{0,224},{32,0},{64,32},{96,64},{128,96},{160,128},{192,160},{224,1... | collective-permute-start | bytes 786440 | tf_op jit(solution)/shard_map/ppermute | solution.py:34
  35.3 2.6 %collective-permute-done.1.refs_3_ = bf16[64,2048]{1,0:T(8,128)(2,1)S(1)} collective-permute-done((bf16[64,2048]{1,0:T(8,128)(2,1)S(1)}, bf16[64,2048]{1,0:T(8,128)(2,1)S(1)}, u32[]{:S(2)}, u32[]{:S(2)}) %collective-permute-start.1) | collective-permute-done | bytes 262176 | tf_op jit(solution)/shard_map/ppermute | solution.py:34
  39.1 2.1 collective-permute-start.6
  41.2 5.6 %collective-permute-start.7 = (bf16[64,2048]{1,0:T(8,128)(2,1)S(1)}, bf16[64,2048]{1,0:T(8,128)(2,1)S(1)}, u32[]{:S(2)}, u32[]{:S(2)}) collective-permute-start(bf16[64,2048]{1,0:T(8,128)(2,1)S(1)} %collective-permute-done.3.refs_4_), channel_id=1, source_target_pairs={{0,224},{32,0},{64,32},{96,64},{128,96},{160,128},{192,160},{224,1... | collective-permute-start | bytes 786440 | tf_op jit(solution)/shard_map/ppermute | solution.py:34
  46.8 2.6 %collective-permute-done.6.refs_5_ = bf16[64,2048]{1,0:T(8,128)(2,1)S(1)} collective-permute-done((bf16[64,2048]{1,0:T(8,128)(2,1)S(1)}, bf16[64,2048]{1,0:T(8,128)(2,1)S(1)}, u32[]{:S(2)}, u32[]{:S(2)}) %collective-permute-start.6) | collective-permute-done | bytes 262176 | tf_op jit(solution)/shard_map/ppermute | solution.py:34
  53.4 10.1 %collective-permute-done.8.refs_7_ = bf16[64,2048]{1,0:T(8,128)(2,1)} collective-permute-done((bf16[64,2048]{1,0:T(8,128)(2,1)S(1)}, bf16[64,2048]{1,0:T(8,128)(2,1)}, u32[]{:S(2)}, u32[]{:S(2)}) %collective-permute-start.8) | collective-permute-done | bytes 262176 | tf_op jit(solution)/shard_map/ppermute | solution.py:34
  63.5 2.3 %shard_map.65 = (f32[256,384]{1,0:T(8,128)S(1)}, f32[256,384]{1,0:T(8,128)S(1)}, bf16[512,2048]{1,0:T(8,128)(2,1)S(1)}) custom-call(s32[1]{0:T(128)} %bitcast.3.core_ref, s32[1]{0:T(128)} %bitcast.7.z_ref, bf16[64,2048]{1,0:T(8,128)(2,1)S(1)} %copy-done.1, bf16[64,2048]{1,0:T(8,128)(2,1)S(1)} %collective-permute-done.refs_1_, ...), custom_call_target="tpu_custom_call" | custom-call | flops 805306368 | bytes 6553600 | tf_op jit(solution)/shard_map/pallas_call | solution.py:74
  71.5 11.1 %all-to-all-start.1 = ((f32[16,16,384]{2,1,0:T(8,128)}), f32[16,16,384]{2,1,0:T(8,128)S(1)}, u32[]{:S(2)}, u32[]{:S(2)}) async-start(f32[16,16,384]{2,1,0:T(8,128)} %bitcast.8), calls=%async_computation.1 | async-start | bytes 786432 | tf_op jit(solution)/shard_map/all_to_all | solution.py:26
  83.5 2.8 %shard_map.64 = (f32[256,384]{1,0:T(8,128)S(1)}, f32[256,384]{1,0:T(8,128)S(1)}) custom-call(s32[1]{0:T(128)} %bitcast.3.core_ref, bf16[512,2048]{1,0:T(8,128)(2,1)} %all-gather.3.cloned.1.call-done.image_ref.other_ref, bf16[384,2048]{1,0:T(8,128)(2,1)S(1)} %bitcast.28, f32[1,384]{1,0:T(1,128)S(1)} %mul.75.penalty_ref.refs_9_), custom_call_target="tpu_custom_call" | custom-call | flops 805306368 | bytes 4456448 | tf_op jit(solution)/shard_map/pallas_call | solution.py:106
  90.8 3.6 %all-to-all-done.1 = f32[16,16,384]{2,1,0:T(8,128)S(1)} async-done(((f32[16,16,384]{2,1,0:T(8,128)}), f32[16,16,384]{2,1,0:T(8,128)S(1)}, u32[]{:S(2)}, u32[]{:S(2)}) %all-to-all-start.1) | async-done | bytes 393248 | tf_op jit(solution)/shard_map/all_to_all | solution.py:26
  94.4 5.9 %all-to-all-start = ((f32[16,16,384]{2,1,0:T(8,128)}), f32[16,16,384]{2,1,0:T(8,128)S(1)}, u32[]{:S(2)}, u32[]{:S(2)}) async-start(f32[16,16,384]{2,1,0:T(8,128)} %bitcast.5), calls=%async_computation | async-start | bytes 786432 | tf_op jit(solution)/shard_map/all_to_all | solution.py:26
  100.4 11.3 %all-to-all-done = f32[16,16,384]{2,1,0:T(8,128)S(1)} async-done(((f32[16,16,384]{2,1,0:T(8,128)}), f32[16,16,384]{2,1,0:T(8,128)S(1)}, u32[]{:S(2)}, u32[]{:S(2)}) %all-to-all-start) | async-done | bytes 393248 | tf_op jit(solution)/shard_map/all_to_all | solution.py:26
  112.1 17.5 %all_to_all.25 = f32[16,2,32]{2,1,0:T(2,128)S(1)} all-to-all(f32[16,2,32]{2,1,0:T(2,128)S(1)} %broadcast_in_dim.9), channel_id=1, replica_groups=mesh['yh'=2,'z'=8,'x'=4,'yl'=4,'core'=2] {'yh','z'}, dimensions={0} | all-to-all | bytes 8192 | tf_op jit(solution)/shard_map/all_to_all | solution.py:26
  130.0 14.9 %all_to_all.26.mine_ref = bf16[16,2,16,384]{3,2,1,0:T(8,128)(2,1)S(1)} all-to-all(bf16[16,2,16,384]{3,2,1,0:T(8,128)(2,1)S(1)} %broadcast_in_dim.10), channel_id=1, replica_groups=mesh['yh'=2,'z'=8,'x'=4,'yl'=4,'core'=2] {'x','yl'}, dimensions={0} | all-to-all | bytes 786432 | tf_op jit(solution)/shard_map/all_to_all | solution.py:26
  148.5 5.3 %shard_map.66 = (bf16[768,1024]{1,0:T(8,128)(2,1)S(1)}, bf16[256,1024]{1,0:T(8,128)(2,1)S(1)}) custom-call(s32[1]{0:T(128)} %bitcast.3.core_ref, bf16[16,2,16,384]{3,2,1,0:T(8,128)(2,1)S(1)} %all_to_all.26.mine_ref, bf16[16,2,16,384]{3,2,1,0:T(8,128)(2,1)S(1)} %collective-permute-done.10.twin_ref, ...), custom_call_target="tpu_custom_call" | custom-call | flops 2013265920 | bytes 6291456 | tf_op jit(solution)/shard_map/pallas_call | solution.py:174
  158.2 2.1 collective-permute-start.12
  160.2 3.1 %collective-permute-start.13 = (bf16[256,1024]{1,0:T(8,128)(2,1)S(1)}, bf16[256,1024]{1,0:T(8,128)(2,1)S(1)}, u32[]{:S(2)}, u32[]{:S(2)}) collective-permute-start(bf16[256,1024]{1,0:T(8,128)(2,1)S(1)} %shard_map.67), channel_id=1, source_target_pairs={{0,16},{8,24},{16,0},{24,8},{1,17},{9,25},{17,1},{25,9},{2,18},{10... | collective-permute-start | bytes 1572872 | tf_op jit(solution)/shard_map/ppermute | solution.py:34
  164.1 4.3 %collective-permute-start.14 = (bf16[256,1024]{1,0:T(8,128)(2,1)S(1)}, bf16[256,1024]{1,0:T(8,128)(2,1)S(1)}, u32[]{:S(2)}, u32[]{:S(2)}) collective-permute-start(bf16[256,1024]{1,0:T(8,128)(2,1)S(1)} %shard_map.70), channel_id=1, source_target_pairs={{0,8},{8,16},{16,24},{24,0},{1,9},{9,17},{17,25},{25,1},{2,10},{10... | collective-permute-start | bytes 1572872 | tf_op jit(solution)/shard_map/ppermute | solution.py:34
  171.5 7.0 %collective-permute-done.13 = bf16[256,1024]{1,0:T(8,128)(2,1)S(1)} collective-permute-done((bf16[256,1024]{1,0:T(8,128)(2,1)S(1)}, bf16[256,1024]{1,0:T(8,128)(2,1)S(1)}, u32[]{:S(2)}, u32[]{:S(2)}) %collective-permute-start.13) | collective-permute-done | bytes 524320 | tf_op jit(solution)/shard_map/ppermute | solution.py:34
  178.4 10.4 %collective-permute-done.14 = bf16[256,1024]{1,0:T(8,128)(2,1)S(1)} collective-permute-done((bf16[256,1024]{1,0:T(8,128)(2,1)S(1)}, bf16[256,1024]{1,0:T(8,128)(2,1)S(1)}, u32[]{:S(2)}, u32[]{:S(2)}) %collective-permute-start.14) | collective-permute-done | bytes 524320 | tf_op jit(solution)/shard_map/ppermute | solution.py:34
  189.6 23.0 %all_to_all.27 = bf16[64,4,1024]{2,1,0:T(4,128)(2,1)S(1)} all-to-all(bf16[64,4,1024]{2,1,0:T(4,128)(2,1)S(1)} %reshape.464), channel_id=1, replica_groups=mesh['yh'=2,'z'=8,'x'=4,'yl'=4,'core'=2] {'yl','yh','z'}, dimensions={0} | all-to-all | bytes 1048576 | tf_op jit(solution)/shard_map/all_to_all | solution.py:26
  (71 shorter events, 33.4 us)
Async XLA Ops:
  6.5 206.3 %copy-start = (bf16[1,4,128,128]{3,2,1,0:T(8,128)(2,1)S(1)}, bf16[1,4,128,128]{3,2,1,0:T(8,128)(2,1)}, u32[]{:S(2)}) copy-start(bf16[1,4,128,128]{3,2,1,0:T(8,128)(2,1)} %param.11) | copy-start | bytes 393220
  6.5 76.9 %all-gather.3.cloned.1.call-start = ((), (), s32[]{:S(2)}) async-start(), calls=%async_computation.5 | async-start | bytes 2359296 | tf_op jit(solution)/shard_map/all_gather | solution.py:280
  6.5 20.7 %collective-permute-start = (bf16[64,2048]{1,0:T(8,128)(2,1)}, bf16[64,2048]{1,0:T(8,128)(2,1)S(1)}, u32[]{:S(2)}, u32[]{:S(2)}) collective-permute-start(bf16[64,2048]{1,0:T(8,128)(2,1)} %refs_0_.1), channel_id=1, source_target_pairs={{0,32},{32,64},{64,96},{96,128},{128,160},{160,192},{192,224},{224... | collective-permute-start | bytes 786440 | tf_op jit(solution)/shard_map/ppermute | solution.py:34
  10.9 18.3 %collective-permute-start.2 = (bf16[64,2048]{1,0:T(8,128)(2,1)}, bf16[64,2048]{1,0:T(8,128)(2,1)S(1)}, u32[]{:S(2)}, u32[]{:S(2)}) collective-permute-start(bf16[64,2048]{1,0:T(8,128)(2,1)} %refs_0_.1), channel_id=1, source_target_pairs={{0,224},{32,0},{64,32},{96,64},{128,96},{160,128},{192,160},{224,1... | collective-permute-start | bytes 786440 | tf_op jit(solution)/shard_map/ppermute | solution.py:34
  19.5 15.8 %collective-permute-start.4 = (bf16[64,2048]{1,0:T(8,128)(2,1)}, bf16[64,2048]{1,0:T(8,128)(2,1)S(1)}, u32[]{:S(2)}, u32[]{:S(2)}) collective-permute-start(bf16[64,2048]{1,0:T(8,128)(2,1)} %refs_0_.1), channel_id=1, source_target_pairs={{0,256},{256,0},{1,257},{257,1},{2,258},{258,2},{3,259},{259,3},{4... | collective-permute-start | bytes 786440 | tf_op jit(solution)/shard_map/ppermute | solution.py:22
  27.3 10.6 %collective-permute-start.1 = (bf16[64,2048]{1,0:T(8,128)(2,1)S(1)}, bf16[64,2048]{1,0:T(8,128)(2,1)S(1)}, u32[]{:S(2)}, u32[]{:S(2)}) collective-permute-start(bf16[64,2048]{1,0:T(8,128)(2,1)S(1)} %collective-permute-done.refs_1_), channel_id=1, source_target_pairs={{0,32},{32,64},{64,96},{96,128},{128,160},{160,192},{192,224},{224... | collective-permute-start | bytes 786440 | tf_op jit(solution)/shard_map/ppermute | solution.py:34
  29.2 9.8 %collective-permute-start.3 = (bf16[64,2048]{1,0:T(8,128)(2,1)S(1)}, bf16[64,2048]{1,0:T(8,128)(2,1)S(1)}, u32[]{:S(2)}, u32[]{:S(2)}) collective-permute-start(bf16[64,2048]{1,0:T(8,128)(2,1)S(1)} %collective-permute-done.2.refs_2_), channel_id=1, source_target_pairs={{0,224},{32,0},{64,32},{96,64},{128,96},{160,128},{192,160},{224,1... | collective-permute-start | bytes 786440 | tf_op jit(solution)/shard_map/ppermute | solution.py:34
  35.3 3.8 %copy-start.3 = (bf16[64,2048]{1,0:T(8,128)(2,1)}, bf16[64,2048]{1,0:T(8,128)(2,1)S(1)}, u32[]{:S(2)}) copy-start(bf16[64,2048]{1,0:T(8,128)(2,1)S(1)} %collective-permute-done.4) | copy-start | bytes 786436
  39.1 24.4 %copy-start.1 = (bf16[64,2048]{1,0:T(8,128)(2,1)S(1)}, bf16[64,2048]{1,0:T(8,128)(2,1)}, u32[]{:S(2)}) copy-start(bf16[64,2048]{1,0:T(8,128)(2,1)} %refs_0_.1) | copy-start | bytes 786436
  39.1 10.3 %collective-permute-start.6 = (bf16[64,2048]{1,0:T(8,128)(2,1)S(1)}, bf16[64,2048]{1,0:T(8,128)(2,1)S(1)}, u32[]{:S(2)}, u32[]{:S(2)}) collective-permute-start(bf16[64,2048]{1,0:T(8,128)(2,1)S(1)} %collective-permute-done.1.refs_3_), channel_id=1, source_target_pairs={{0,32},{32,64},{64,96},{96,128},{128,160},{160,192},{192,224},{224... | collective-permute-start | bytes 786440 | tf_op jit(solution)/shard_map/ppermute | solution.py:34
  41.2 12.2 %collective-permute-start.7 = (bf16[64,2048]{1,0:T(8,128)(2,1)S(1)}, bf16[64,2048]{1,0:T(8,128)(2,1)S(1)}, u32[]{:S(2)}, u32[]{:S(2)}) collective-permute-start(bf16[64,2048]{1,0:T(8,128)(2,1)S(1)} %collective-permute-done.3.refs_4_), channel_id=1, source_target_pairs={{0,224},{32,0},{64,32},{96,64},{128,96},{160,128},{192,160},{224,1... | collective-permute-start | bytes 786440 | tf_op jit(solution)/shard_map/ppermute | solution.py:34
  49.4 14.1 %collective-permute-start.8 = (bf16[64,2048]{1,0:T(8,128)(2,1)S(1)}, bf16[64,2048]{1,0:T(8,128)(2,1)}, u32[]{:S(2)}, u32[]{:S(2)}) collective-permute-start(bf16[64,2048]{1,0:T(8,128)(2,1)S(1)} %collective-permute-done.6.refs_5_), channel_id=1, source_target_pairs={{0,32},{32,64},{64,96},{96,128},{128,160},{160,192},{192,224},{224... | collective-permute-start | bytes 786440 | tf_op jit(solution)/shard_map/ppermute | solution.py:34
  67.1 3.6 %collective-permute-start.9 = (f32[256,384]{1,0:T(8,128)S(1)}, f32[256,384]{1,0:T(8,128)S(1)}, u32[]{:S(2)}, u32[]{:S(2)}) collective-permute-start(f32[256,384]{1,0:T(8,128)S(1)} %get-tuple-element.18), channel_id=1, source_target_pairs={{0,1},{1,0},{2,3},{3,2},{4,5},{5,4},{6,7},{7,6},{8,9},{9,8},{10,11... | collective-permute-start | bytes 1179656 | tf_op jit(solution)/shard_map/ppermute | solution.py:22
  71.5 22.9 %all-to-all-start.1 = ((f32[16,16,384]{2,1,0:T(8,128)}), f32[16,16,384]{2,1,0:T(8,128)S(1)}, u32[]{:S(2)}, u32[]{:S(2)}) async-start(f32[16,16,384]{2,1,0:T(8,128)} %bitcast.8), calls=%async_computation.1 | async-start | bytes 786432 | tf_op jit(solution)/shard_map/all_to_all | solution.py:26
  86.3 14.0 %copy-start.5 = (f32[8,48]{1,0:T(8,128)S(1)}, f32[8,48]{1,0:T(8,128)}, u32[]{:S(2)}) copy-start(f32[8,48]{1,0:T(8,128)} %param.9) | copy-start | bytes 4612
  86.3 3.6 %collective-permute-start.5 = (f32[256,384]{1,0:T(8,128)S(1)}, f32[256,384]{1,0:T(8,128)S(1)}, u32[]{:S(2)}, u32[]{:S(2)}) collective-permute-start(f32[256,384]{1,0:T(8,128)S(1)} %get-tuple-element.16), channel_id=1, source_target_pairs={{0,1},{1,0},{2,3},{3,2},{4,5},{5,4},{6,7},{7,6},{8,9},{9,8},{10,11... | collective-permute-start | bytes 1179656 | tf_op jit(solution)/shard_map/ppermute | solution.py:22
  94.4 52.5 %copy-start.4 = (s32[1,48,16,2]{1,3,2,0:T(2,128)S(1)}, s32[1,48,16,2]{1,3,2,0:T(2,128)}, u32[]{:S(2)}) copy-start(s32[1,48,16,2]{1,3,2,0:T(2,128)} %param.10) | copy-start | bytes 18436
  94.4 17.3 %all-to-all-start = ((f32[16,16,384]{2,1,0:T(8,128)}), f32[16,16,384]{2,1,0:T(8,128)S(1)}, u32[]{:S(2)}, u32[]{:S(2)}) async-start(f32[16,16,384]{2,1,0:T(8,128)} %bitcast.5), calls=%async_computation | async-start | bytes 786432 | tf_op jit(solution)/shard_map/all_to_all | solution.py:26
  144.9 3.6 %collective-permute-start.10 = (bf16[16,2,16,384]{3,2,1,0:T(8,128)(2,1)S(1)}, bf16[16,2,16,384]{3,2,1,0:T(8,128)(2,1)S(1)}, u32[]{:S(2)}, u32[]{:S(2)}) collective-permute-start(bf16[16,2,16,384]{3,2,1,0:T(8,128)(2,1)S(1)} %all_to_all.26.mine_ref), channel_id=1, source_target_pairs={{0,1},{1,0},{2,3},{3,2},{4,5},{5,4},{6,7},{7,6},{8,9},{9,8},{10,11... | collective-permute-start | bytes 1179656 | tf_op jit(solution)/shard_map/ppermute | solution.py:22
  153.8 3.8 %collective-permute-start.11 = (bf16[256,1024]{1,0:T(8,128)(2,1)S(1)}, bf16[256,1024]{1,0:T(8,128)(2,1)S(1)}, u32[]{:S(2)}, u32[]{:S(2)}) collective-permute-start(bf16[256,1024]{1,0:T(8,128)(2,1)S(1)} %get-tuple-element.21), channel_id=1, source_target_pairs={{0,1},{1,0},{2,3},{3,2},{4,5},{5,4},{6,7},{7,6},{8,9},{9,8},{10,11... | collective-permute-start | bytes 1572872 | tf_op jit(solution)/shard_map/ppermute | solution.py:22
  158.2 5.3 %collective-permute-start.12 = (bf16[768,1024]{1,0:T(8,128)(2,1)S(1)}, bf16[768,1024]{1,0:T(8,128)(2,1)S(1)}, u32[]{:S(2)}, u32[]{:S(2)}) collective-permute-start(bf16[768,1024]{1,0:T(8,128)(2,1)S(1)} %shard_map.68), channel_id=1, source_target_pairs={{0,1},{1,0},{2,3},{3,2},{4,5},{5,4},{6,7},{7,6},{8,9},{9,8},{10,11... | collective-permute-start | bytes 4718600 | tf_op jit(solution)/shard_map/ppermute | solution.py:22
  160.2 18.2 %collective-permute-start.13 = (bf16[256,1024]{1,0:T(8,128)(2,1)S(1)}, bf16[256,1024]{1,0:T(8,128)(2,1)S(1)}, u32[]{:S(2)}, u32[]{:S(2)}) collective-permute-start(bf16[256,1024]{1,0:T(8,128)(2,1)S(1)} %shard_map.67), channel_id=1, source_target_pairs={{0,16},{8,24},{16,0},{24,8},{1,17},{9,25},{17,1},{25,9},{2,18},{10... | collective-permute-start | bytes 1572872 | tf_op jit(solution)/shard_map/ppermute | solution.py:34
  164.1 24.7 %collective-permute-start.14 = (bf16[256,1024]{1,0:T(8,128)(2,1)S(1)}, bf16[256,1024]{1,0:T(8,128)(2,1)S(1)}, u32[]{:S(2)}, u32[]{:S(2)}) collective-permute-start(bf16[256,1024]{1,0:T(8,128)(2,1)S(1)} %shard_map.70), channel_id=1, source_target_pairs={{0,8},{8,16},{16,24},{24,0},{1,9},{9,17},{17,25},{25,1},{2,10},{10... | collective-permute-start | bytes 1572872 | tf_op jit(solution)/shard_map/ppermute | solution.py:34
  169.0 20.1 %collective-permute-start.15 = (bf16[256,1024]{1,0:T(8,128)(2,1)S(1)}, bf16[256,1024]{1,0:T(8,128)(2,1)S(1)}, u32[]{:S(2)}, u32[]{:S(2)}) collective-permute-start(bf16[256,1024]{1,0:T(8,128)(2,1)S(1)} %shard_map.71), channel_id=1, source_target_pairs={{0,24},{8,0},{16,8},{24,16},{1,25},{9,1},{17,9},{25,17},{2,26},{10... | collective-permute-start | bytes 1572872 | tf_op jit(solution)/shard_map/ppermute | solution.py:34
  (1 other events, 1.3 us)
Sparse Core Ops, SparseCore 0:
  39.2 44.2 all-gather.2
